TPU v7x, 128 devices: a whole 4x4x4 slice. The times are simulated.
128 devices in a mesh: section: 2 (over core), seq: 4 (over z), shard: 16 (over x, y).
Axes of the slice: x: 4, y: 4, z: 4, core: 2. Of those that a mesh axis runs over, the one named last changes fastest.
Arguments:
- inputs: bfloat16 [3, 16, 1024, 512], P(None, 'shard', 'seq'), may hold values from -6 to 6
- positions: int32 [3, 16, 1024], P(None, 'shard', 'seq'), may hold values from 0 to 1023, as said below
- cotangent: bfloat16 [3, 16, 1024, 512], P(None, 'shard', 'seq'), may hold values from -6 to 6
- qkv_weight: bfloat16 [2, 512, 1536], P('section', 'shard'), may hold values from -0.25 to 0.25
- proj_weight: bfloat16 [2, 512, 512], P('section', 'shard'), may hold values from -2 to 2
- up_weight: bfloat16 [2, 512, 2048], P('section', 'shard'), may hold values from -0.25 to 0.25
- down_weight: bfloat16 [2, 2048, 512], P('section', 'shard'), may hold values from -0.125 to 0.125
- norm_gain: bfloat16 [2, 2, 512], P('section', None, 'shard'), may hold values from 0.099609375 to 1.8984375
- norm_bias: bfloat16 [2, 2, 512], P('section', None, 'shard'), may hold values from -2 to 2
Outputs:
- activations: bfloat16 [2, 3, 16, 1024, 512], P('section', None, 'shard', 'seq')
- input_grads: bfloat16 [2, 3, 16, 1024, 512], P('section', None, 'shard', 'seq')
- qkv_grad: float32 [2, 512, 1536], P('section', 'shard')
- proj_grad: float32 [2, 512, 512], P('section', 'shard')
- up_grad: float32 [2, 512, 2048], P('section', 'shard')
- down_grad: float32 [2, 2048, 512], P('section', 'shard')
- gain_grad: float32 [2, 2, 512], P('section', None, 'shard')
- bias_grad: float32 [2, 2, 512], P('section', None, 'shard')
Inputs may be any that keep to these rules, and one draw needn't show every extreme that they name: Each sequence is a pack of documents: positions count from 0 at a document's first token and rise by one; every sequence starts at 0; for every sequence index one of the 3 micro-batches holds that sequence as a single document of 1024 tokens.
All inputs are finite; a program needn't handle non-finite values.
Results may differ from a plain program's by a relative error of at most 0.018.
Values may be sent and summed in bfloat16 or wider, within the bound.
No kernel may reach another device: no remote copies, remote signals or barrier semaphores. Data moves between devices by JAX's collectives and lax.ppermute only.
A program may use at most 192 MiB of HBM per device.

v0:
```python
import functools

import jax
import jax.numpy as jnp
from jax import lax
from jax.experimental import pallas as pl
from jax.experimental.pallas import tpu as pltpu
from jax.sharding import PartitionSpec as P

D = 512
HEADS = 8
HEAD = 64
ROT = 16
MICRO = 3
BLOCK = 256
TOKENS = MICRO * BLOCK
NORM_EPS = 1e-05
MASKED = -1e30
BF = jnp.bfloat16
F32 = jnp.float32
SHIFTS = (0, 1, 2, 3)
VMEM_LIMIT = 24 * 1024 * 1024


def dims(left, right, left_dim, right_dim):
    return lax.dot_general(
        left, right, (((left_dim,), (right_dim,)), ((), ())), preferred_element_type=F32
    )


def struct(shape, dtype):
    return jax.ShapeDtypeStruct(shape, dtype)


def call(body, place, grid, ins, outs, scratch=(), flops=10**9, moved=4 * 10**6):
    specs = [pl.BlockSpec(block, index) for _, block, index in ins]
    out_specs = [pl.BlockSpec(out[2], out[3]) for out in outs]
    return pl.pallas_call(
        body,
        out_shape=[
            (pltpu.HBM if out[4:] else struct)(out[0], out[1]) for out in outs
        ],
        grid_spec=pltpu.PrefetchScalarGridSpec(
            num_scalar_prefetch=1,
            grid=grid,
            in_specs=specs,
            out_specs=out_specs,
            scratch_shapes=list(scratch),
        ),
        compiler_params=pltpu.CompilerParams(
            vmem_limit_bytes=VMEM_LIMIT, dimension_semantics=("arbitrary",) * len(grid)
        ),
        cost_estimate=pl.CostEstimate(flops=flops, bytes_accessed=moved, transcendentals=0),
    )(place, *[array for array, _, _ in ins])


def whole(array):
    rank = array.ndim
    return (array, array.shape, lambda *_: (0,) * rank)


def whole_out(shape, dtype):
    rank = len(shape)
    return (shape, dtype, shape, lambda *_: (0,) * rank)


def kept_in_hbm(out):
    return out + (True,)


def rows(array):
    return (array, (BLOCK, array.shape[1]), lambda m, _: (m, 0))


def rows_out(width, dtype):
    return ((TOKENS, width), dtype, (BLOCK, width), lambda m, _: (m, 0))


def lanes(array):
    lead = array.shape[:-1]
    rank = len(lead)
    return (array, lead + (BLOCK,), lambda m, _: (0,) * rank + (m,))


def lanes_out(lead, dtype):
    rank = len(lead)
    return (lead + (TOKENS,), dtype, lead + (BLOCK,), lambda m, _: (0,) * rank + (m,))


def by_micro(array):
    rank = array.ndim - 1
    return (array, (1,) + array.shape[1:], lambda m, _: (m,) + (0,) * rank)


def by_micro_out(shape, dtype):
    rank = len(shape) - 1
    return (shape, dtype, (1,) + shape[1:], lambda m, _: (m,) + (0,) * rank)


def pack_body(place, qkv, proj, up, down, mine, other, held):
    low = lax.broadcasted_iota(jnp.int32, (32, 128), 1) < 64
    for half in range(2):
        for pair in range(8):
            first = up[:, 256 * pair : 256 * pair + 128].astype(F32)
            second = up[:, 256 * pair + 128 : 256 * pair + 256].astype(F32)
            if half == 0:
                cut = jnp.where(low, first, pltpu.roll(second, 64, 1))
            else:
                cut = jnp.where(low, pltpu.roll(first, 64, 1), second)
            at = 128 * (pair % 2)
            held[half, 32 * (pair // 2) : 32 * (pair // 2) + 32, at : at + 128] = cut.astype(BF)
        for side in range(2):
            held[half, 128 + 64 * side : 192 + 64 * side, :] = down[
                64 * half : 64 * half + 64, 256 * side : 256 * side + 256
            ]
            held[half, 256 + 32 * side : 288 + 32 * side, :] = proj[
                :, 256 * side : 256 * side + 256
            ]
        for part in range(3):
            at = 512 * part + 256 * half
            held[half, 320 + 32 * part : 352 + 32 * part, :] = qkv[:, at : at + 256]
    core = place[1]
    mine[...] = held[core]
    other[...] = held[1 - core]


def pack_weights(place, qkv, proj, up, down):
    return call(
        pack_body,
        place,
        (1,),
        [whole(qkv), whole(proj), whole(up), whole(down)],
        [whole_out((416, 256), BF), whole_out((416, 256), BF)],
        [pltpu.VMEM((2, 416, 256), BF)],
    )


def sort_body(place, mine, received, norms, early, middle, late):
    first = place[1] == 0
    kept = mine[...]
    came = received[...]
    layer0 = jnp.where(first, kept, came)
    layer1 = jnp.where(first, came, kept)
    early[0:96, :] = layer0[320:416]
    early[96:112, :] = norms[...]
    middle[0:320, :] = layer0[0:320]
    middle[320:480, :] = layer1[256:416]
    late[...] = layer1[0:256]


def sort_weights(place, mine, received, norms):
    return call(
        sort_body,
        place,
        (1,),
        [whole(mine), whole(received), whole(norms)],
        [whole_out((depth, 256), BF) for depth in (112, 480, 256)],
    )


def shift_z(value, step):
    return lax.ppermute(value, "seq", [(z, (z + step) % 4) for z in range(4)])


def swap_core(value):
    return lax.ppermute(value, "section", [(0, 1), (1, 0)])


def gather_now(value):
    copies = jnp.broadcast_to(value, (16,) + value.shape)
    return lax.all_to_all(copies, "shard", 0, 0, tiled=True)


def after(value, *others):
    return lax.optimization_barrier((value, others))[0]


def regroup(values):
    got = {0: values[0]}
    for step in (1, 3, 2):
        got[step] = shift_z(values[step], step)
    return [got[step] for step in SHIFTS]


def unit_of(states):
    centre = states - jnp.mean(states, axis=-1, keepdims=True)
    scaled = lax.rsqrt(jnp.mean(centre * centre, axis=-1, keepdims=True) + NORM_EPS)
    return centre * scaled, scaled


def qkv_rows(weights):
    array, first = weights
    return [
        (array, (16, 32, 256), functools.partial(lambda at, m, _: (0, at, 0), first + part))
        for part in range(3)
    ]


def proj_rows(weights):
    array, first = weights
    return (array, (8, 64, 256), lambda m, place: (place[1], first, 0))


def put_heads_grad(grad, proj, held, first):
    weight = proj[...]
    total = dims(weight[:, 0:32].reshape(256, 256), grad[:, 0:256], 1, 1) + dims(
        weight[:, 32:64].reshape(256, 256), grad[:, 256:512], 1, 1
    )
    for head in range(4):
        held[head, first : first + 64, :] = total[64 * head : 64 * head + 64].astype(BF)


def before_body(second, place, *refs):
    refs = list(refs)
    states = refs.pop(0)[...].astype(F32)
    if second:
        part_a, part_b, grad, proj = [refs.pop(0) for _ in range(4)]
        states = (states + (part_a[...] + part_b[...])).astype(BF)
    wq, wk, wv, norms, turns = refs[:5]
    outs = refs[5:9]
    attn_ref, mlp_ref = refs[9:11]
    held = refs[-1]
    if second:
        refs[11][...] = states
        states = states.astype(F32)
    unit, _ = unit_of(states)
    attn_in = (unit * norms[0:1, :] + norms[2:3, :]).astype(BF)
    attn_ref[...] = attn_in
    mlp_ref[...] = (unit * norms[1:2, :] + norms[3:4, :]).astype(BF)
    cosine, sine = turns[0], turns[1]
    for part, weight in enumerate((wq, wk, wv)):
        mixed = dims(weight[...].reshape(D, 256), attn_in, 0, 1)
        for head in range(4):
            block = mixed[64 * head : 64 * head + 64]
            if part < 2:
                a, b = block[0:8], block[8:16]
                block = jnp.concatenate(
                    [a * cosine - b * sine, b * cosine + a * sine, block[16:]], axis=0
                )
            if part == 0:
                block = block * 0.125
            held[head, 64 * part : 64 * part + 64, :] = block.astype(BF)
    if second:
        put_heads_grad(grad, proj, held, 192)
    for step in SHIFTS:
        outs[step][...] = held[lax.rem(place[0] + step, 4)]


def before_layer(place, states, extra, weights, norms, turns):
    array, first = weights
    ins = [rows(states)]
    depth = 192
    if extra:
        parts, grad, proj = extra
        ins += [rows(parts[0]), rows(parts[1]), rows(grad), proj_rows(proj)]
        depth = 256
    ins += qkv_rows(weights)
    ins += [whole(norms), lanes(turns)]
    outs = [lanes_out((depth,), BF) for _ in SHIFTS]
    outs += [kept_in_hbm(rows_out(D, BF)), kept_in_hbm(rows_out(D, BF))]
    if extra:
        outs.append(kept_in_hbm(rows_out(D, BF)))
    return call(
        functools.partial(before_body, bool(extra)),
        place,
        (MICRO,),
        ins,
        outs,
        [pltpu.VMEM((4, depth, BLOCK), BF)],
        flops=1_200_000_000,
        moved=6_000_000,
    )


def mlp_body(place, mlp_in, up, down, out, active_ref, slope_ref):
    step = pl.program_id(0)
    hidden = jnp.dot(mlp_in[...], up[...].reshape(D, 256), preferred_element_type=F32)
    cdf = 0.5 * (1.0 + lax.erf(hidden * 0.7071067811865476))
    pdf = jnp.exp(-0.5 * hidden * hidden) * 0.3989422804014327
    active = (hidden * cdf).astype(BF)
    active_ref[...] = active
    slope_ref[...] = cdf + hidden * pdf
    lower = down[...]
    both = jnp.concatenate(
        [lower[:, 0:64].reshape(256, 256), lower[:, 64:128].reshape(256, 256)], axis=1
    )
    product = jnp.dot(active, both, preferred_element_type=F32)

    @pl.when(step == 0)
    def _():
        out[...] = product

    @pl.when(step > 0)
    def _():
        out[...] += product


def mlp_layer(place, mlp_in, weights):
    return call(
        mlp_body,
        place,
        (4,),
        [
            whole(mlp_in),
            (weights, (16, 32, 256), lambda b, _: (0, b, 0)),
            (weights, (4, 128, 256), lambda b, _: (b, 1, 0)),
        ],
        [
            whole_out((TOKENS, D), F32),
            kept_in_hbm(((TOKENS, 1024), BF, (TOKENS, 256), lambda b, _: (0, b))),
            kept_in_hbm(((TOKENS, 1024), F32, (TOKENS, 256), lambda b, _: (0, b))),
        ],
        flops=6_000_000_000,
        moved=12_000_000,
    )


def put_starts(place, places, starts):
    along = lax.broadcasted_iota(jnp.int32, (1, BLOCK), 1)
    for step in SHIFTS:
        source = lax.rem(place[0] - step + 4, 4)
        starts[source] = along + BLOCK * source - places[step][...]


def allowed_keys(starts, query_block, key_block):
    keys = lax.broadcasted_iota(jnp.int32, (BLOCK, BLOCK), 0) + BLOCK * key_block
    allowed = keys >= starts[query_block]
    if query_block == key_block:
        queries = lax.broadcasted_iota(jnp.int32, (BLOCK, BLOCK), 1) + BLOCK * query_block
        allowed = allowed & (keys <= queries)
    return allowed


def attend_body(place, *refs):
    came, places = refs[0:4], refs[4:8]
    outs = refs[8:12]
    kept, heads_out, log_total = refs[12:15]
    starts, keys = refs[15:17]
    for step in SHIFTS:
        source = lax.rem(place[0] - step + 4, 4)
        kept[0, source] = came[step][...]
    put_starts(place, places, starts)
    for j in range(4):
        keys[j] = kept[0, j, 64:128].T
    for i in range(4):
        query = kept[0, i, 0:64]
        scores = []
        for j in range(i + 1):
            raw = jnp.dot(keys[j], query, preferred_element_type=F32)
            scores.append(jnp.where(allowed_keys(starts, i, j), raw, MASKED))
        peak = functools.reduce(
            jnp.maximum, [jnp.max(s, axis=0, keepdims=True) for s in scores]
        )
        total = jnp.zeros((1, BLOCK), F32)
        acc = jnp.zeros((HEAD, BLOCK), F32)
        for j in range(i + 1):
            probs = jnp.exp(scores[j] - peak)
            total = total + jnp.sum(probs, axis=0, keepdims=True)
            acc = acc + jnp.dot(
                kept[0, j, 128:192], probs.astype(BF), preferred_element_type=F32
            )
        heads_out[0, i] = (acc / total).astype(BF)
        log_total[0, i] = peak + jnp.log(total)
    for step in SHIFTS:
        outs[step][...] = heads_out[0, lax.rem(place[0] + step, 4)]


def attend(place, came, places):
    return call(
        attend_body,
        place,
        (MICRO,),
        [lanes(piece) for piece in came] + [lanes(piece) for piece in places],
        [lanes_out((HEAD,), BF) for _ in SHIFTS]
        + [
            kept_in_hbm(by_micro_out((MICRO, 4, 192, BLOCK), BF)),
            kept_in_hbm(by_micro_out((MICRO, 4, HEAD, BLOCK), BF)),
            kept_in_hbm(by_micro_out((MICRO, 4, 1, BLOCK), F32)),
        ],
        [pltpu.VMEM((4, 1, BLOCK), jnp.int32), pltpu.VMEM((4, BLOCK, HEAD), BF)],
        flops=8_000_000_000,
        moved=4_000_000,
    )


def after_body(place, *refs):
    came = refs[0:4]
    proj, mlp_out, out, heads = refs[4:8]
    for step in SHIFTS:
        source = lax.rem(place[0] - step + 4, 4)
        at = pl.multiple_of(source * HEAD, HEAD)
        heads[pl.ds(at, HEAD), :] = came[step][...]
    held = heads[...]
    weight = proj[...]
    for side in range(2):
        span = slice(256 * side, 256 * side + 256)
        product = dims(held, weight[:, 32 * side : 32 * side + 32].reshape(256, 256), 0, 0)
        out[:, span] = mlp_out[:, span] + product


def after_layer(place, came, first, proj, mlp_out):
    return call(
        after_body,
        place,
        (MICRO,),
        [(piece, (HEAD, BLOCK), lambda m, _: (first, m)) for piece in came]
        + [proj_rows(proj), rows(mlp_out)],
        [rows_out(D, F32), lanes_out((256,), BF)],
        flops=800_000_000,
        moved=4_000_000,
    )


def heads_grad_body(place, grad, proj, *refs):
    outs, held = refs[0:4], refs[4]
    put_heads_grad(grad, proj, held, 0)
    for step in SHIFTS:
        outs[step][...] = held[lax.rem(place[0] + step, 4)]


def heads_grad(place, grad, proj):
    return call(
        heads_grad_body,
        place,
        (MICRO,),
        [rows(grad), proj_rows(proj)],
        [lanes_out((HEAD,), BF) for _ in SHIFTS],
        [pltpu.VMEM((4, HEAD, BLOCK), BF)],
        flops=800_000_000,
        moved=2_000_000,
    )


def put_proj(core, heads, grad, pack, first):
    product = jnp.dot(heads[...], grad[...], preferred_element_type=F32).astype(BF)
    for side in range(2):
        span = pl.ds(first + 32 * side, 32)
        part = product[:, 256 * side : 256 * side + 256].reshape(8, 32, 256)
        pack[pl.ds(8 * core, 8), span, :] = part
        pack[pl.ds(8 - 8 * core, 8), span, :] = jnp.zeros_like(part)


def mlp_back_body(with_proj, place, grad, active, slope, mlp_in, up, down, *refs):
    out, pack = refs[-2:]
    step = pl.program_id(0)
    lower = down[...]
    both = jnp.concatenate(
        [lower[:, 0:64].reshape(256, 256), lower[:, 64:128].reshape(256, 256)], axis=1
    )
    active_grad = dims(grad[...], both, 1, 1)
    hidden_grad = (active_grad * slope[...]).astype(BF)
    product = dims(hidden_grad, up[...].reshape(D, 256), 1, 1)

    @pl.when(step == 0)
    def _():
        out[...] = product
        if with_proj:
            put_proj(place[1], refs[0], grad, pack, 256)

    @pl.when(step > 0)
    def _():
        out[...] += product

    up_part = dims(mlp_in[...], hidden_grad, 0, 0).astype(BF).reshape(16, 32, 256)
    pack[:, pl.ds(pl.multiple_of(32 * step, 32), 32), :] = up_part
    down_part = dims(active[...], grad[...], 0, 0).astype(BF)
    for side in range(2):
        pack[pl.ds(4 * step, 4), 128 + 64 * side : 192 + 64 * side, :] = down_part[
            :, 256 * side : 256 * side + 256
        ].reshape(4, 64, 256)


def mlp_back(place, grad, active, slope, mlp_in, weights, heads=None):
    ins = [
        whole(grad),
        (active, (TOKENS, 256), lambda b, _: (0, b)),
        (slope, (TOKENS, 256), lambda b, _: (0, b)),
        whole(mlp_in),
        (weights, (16, 32, 256), lambda b, _: (0, b, 0)),
        (weights, (4, 128, 256), lambda b, _: (b, 1, 0)),
    ]
    depth = 256
    if heads is not None:
        ins.append(whole(heads))
        depth = 320
    return call(
        functools.partial(mlp_back_body, heads is not None),
        place,
        (4,),
        ins,
        [whole_out((TOKENS, D), F32), whole_out((16, depth, 256), BF)],
        flops=8_000_000_000,
        moved=14_000_000,
    )


def attend_back_body(place, *refs):
    came, places = refs[0:4], refs[4:8]
    kept_ref, heads_out, log_total = refs[8:11]
    outs = refs[11:15]
    starts, keys, values, grads, acc = refs[15:20]
    for step in SHIFTS:
        source = lax.rem(place[0] - step + 4, 4)
        grads[source] = came[step][...]
    put_starts(place, places, starts)
    acc[...] = jnp.zeros_like(acc)
    for j in range(4):
        keys[j] = kept_ref[0, j, 64:128].T
        values[j] = kept_ref[0, j, 128:192].T
    for i in range(4):
        query = kept_ref[0, i, 0:64]
        grad = grads[i]
        log_row = log_total[0, i]
        centre = jnp.sum(
            grad.astype(F32) * heads_out[0, i].astype(F32), axis=0, keepdims=True
        )
        query_grad = jnp.zeros((HEAD, BLOCK), F32)
        for j in range(i + 1):
            raw = jnp.dot(keys[j], query, preferred_element_type=F32)
            probs = jnp.where(allowed_keys(starts, i, j), jnp.exp(raw - log_row), 0.0)
            probs_grad = jnp.dot(values[j], grad, preferred_element_type=F32)
            scores_grad = (probs * (probs_grad - centre)).astype(BF)
            acc[j, 128:192, :] += dims(grad, probs.astype(BF), 1, 1)
            acc[j, 64:128, :] += dims(query, scores_grad, 1, 1)
            query_grad = query_grad + jnp.dot(
                kept_ref[0, j, 64:128], scores_grad, preferred_element_type=F32
            )
        acc[i, 0:64, :] = query_grad * 0.125
    for step in SHIFTS:
        outs[step][...] = acc[lax.rem(place[0] + step, 4)].astype(BF)


def attend_back(place, came, places, kept, heads_out, log_total):
    return call(
        attend_back_body,
        place,
        (MICRO,),
        [lanes(piece) for piece in came]
        + [lanes(piece) for piece in places]
        + [by_micro(kept), by_micro(heads_out), by_micro(log_total)],
        [lanes_out((192,), BF) for _ in SHIFTS],
        [
            pltpu.VMEM((4, 1, BLOCK), jnp.int32),
            pltpu.VMEM((4, BLOCK, HEAD), BF),
            pltpu.VMEM((4, BLOCK, HEAD), BF),
            pltpu.VMEM((4, HEAD, BLOCK), BF),
            pltpu.VMEM((4, 192, BLOCK), F32),
        ],
        flops=16_000_000_000,
        moved=5_000_000,
    )


def attend_both_body(place, *refs):
    came, places, outs = refs[0:4], refs[4:8], refs[8:12]
    starts, kept, keys, values, acc, out = refs[12:18]
    for step in SHIFTS:
        source = lax.rem(place[0] - step + 4, 4)
        kept[source] = came[step][...]
    put_starts(place, places, starts)
    acc[...] = jnp.zeros_like(acc)
    for j in range(4):
        keys[j] = kept[j, 64:128].T
        values[j] = kept[j, 128:192].T
    for i in range(4):
        query = kept[i, 0:64]
        grad = kept[i, 192:256]
        scores = []
        for j in range(i + 1):
            raw = jnp.dot(keys[j], query, preferred_element_type=F32)
            scores.append(jnp.where(allowed_keys(starts, i, j), raw, MASKED))
        peak = functools.reduce(
            jnp.maximum, [jnp.max(s, axis=0, keepdims=True) for s in scores]
        )
        exps = [jnp.exp(s - peak) for s in scores]
        total = functools.reduce(jnp.add, [jnp.sum(e, axis=0, keepdims=True) for e in exps])
        inverse = 1.0 / total
        result = jnp.zeros((HEAD, BLOCK), F32)
        probs = []
        for j in range(i + 1):
            prob = exps[j] * inverse
            low = prob.astype(BF)
            probs.append(prob)
            result = result + jnp.dot(kept[j, 128:192], low, preferred_element_type=F32)
            acc[j, 128:192, :] += dims(grad, low, 1, 1)
        out[i] = result.astype(BF)
        centre = jnp.sum(grad.astype(F32) * result, axis=0, keepdims=True)
        query_grad = jnp.zeros((HEAD, BLOCK), F32)
        for j in range(i + 1):
            probs_grad = jnp.dot(values[j], grad, preferred_element_type=F32)
            scores_grad = (probs[j] * (probs_grad - centre)).astype(BF)
            acc[j, 64:128, :] += dims(query, scores_grad, 1, 1)
            query_grad = query_grad + jnp.dot(
                kept[j, 64:128], scores_grad, preferred_element_type=F32
            )
        acc[i, 0:64, :] = query_grad * 0.125
    for step in SHIFTS:
        other = lax.rem(place[0] + step, 4)
        outs[step][0:192, :] = acc[other].astype(BF)
        outs[step][192:256, :] = out[other]


def attend_both(place, came, places):
    return call(
        attend_both_body,
        place,
        (MICRO,),
        [lanes(piece) for piece in came] + [lanes(piece) for piece in places],
        [lanes_out((256,), BF) for _ in SHIFTS],
        [
            pltpu.VMEM((4, 1, BLOCK), jnp.int32),
            pltpu.VMEM((4, 256, BLOCK), BF),
            pltpu.VMEM((4, BLOCK, HEAD), BF),
            pltpu.VMEM((4, BLOCK, HEAD), BF),
            pltpu.VMEM((4, 192, BLOCK), F32),
            pltpu.VMEM((4, HEAD, BLOCK), BF),
        ],
        flops=18_000_000_000,
        moved=5_000_000,
    )


def mixed_back_body(place, *refs):
    came = refs[0:4]
    wq, wk, wv, norms, turns, states, mlp_grad = refs[4:11]
    out, mixed_ref, sums = refs[11:14]
    cosine, sine = turns[0], turns[1]
    for step in SHIFTS:
        head = lax.rem(place[0] - step + 4, 4)
        at = pl.multiple_of(head * HEAD, HEAD)
        for part in range(3):
            block = came[step][64 * part : 64 * part + 64]
            if part < 2:
                a, b = block[0:8].astype(F32), block[8:16].astype(F32)
                turned = jnp.concatenate(
                    [a * cosine + b * sine, b * cosine - a * sine], axis=0
                ).astype(BF)
                block = jnp.concatenate([turned, block[16:]], axis=0)
            mixed_ref[part, pl.ds(at, HEAD), :] = block
    attn_grad = jnp.zeros((BLOCK, D), F32)
    for part, weight in enumerate((wq, wk, wv)):
        attn_grad = attn_grad + dims(mixed_ref[part], weight[...].reshape(D, 256), 0, 1)
    unit, _ = unit_of(states[...].astype(F32))
    other_grad = mlp_grad[...]
    out[...] = attn_grad * norms[0:1, :] + other_grad * norms[1:2, :]

    @pl.when(pl.program_id(0) == 0)
    def _():
        sums[...] = jnp.zeros_like(sums)

    sums[0:1, :] += jnp.sum(attn_grad * unit, axis=0, keepdims=True)
    sums[1:2, :] += jnp.sum(other_grad * unit, axis=0, keepdims=True)
    sums[2:3, :] += jnp.sum(attn_grad, axis=0, keepdims=True)
    sums[3:4, :] += jnp.sum(other_grad, axis=0, keepdims=True)


def mixed_back(place, came, weights, norms, turns, states, mlp_grad):
    ins = [(piece, (192, BLOCK), lambda m, _: (0, m)) for piece in came]
    ins += qkv_rows(weights)
    ins += [whole(norms), lanes(turns), rows(states), rows(mlp_grad)]
    return call(
        mixed_back_body,
        place,
        (MICRO,),
        ins,
        [
            rows_out(D, F32),
            lanes_out((3, 256), BF),
            whole_out((8, D), F32),
        ],
        flops=1_500_000_000,
        moved=6_000_000,
    )


def weight_back_body(with_rest, place, attn_in, mixed, sums, *refs):
    pack = refs[-1]
    first = 0
    if with_rest:
        rest, heads, grad = refs[:3]
        pack[:, 0:256, :] = rest[...]
        put_proj(place[1], heads, grad, pack, 256)
        first = 320
    for part in range(3):
        product = dims(attn_in[...], mixed[part], 0, 1)
        at = first + 32 * part
        pack[:, at : at + 32, :] = product.astype(BF).reshape(16, 32, 256)
    at = first + 96
    pack[:, at : at + 16, :] = jnp.zeros((16, 16, 256), BF)
    for owner in range(16):
        tile, shift = owner // 4, owner % 4 * 32
        lines = sums[:, 128 * tile : 128 * tile + 128]
        if shift:
            lines = pltpu.roll(lines, 128 - shift, 1)
        lines = jnp.concatenate([lines, jnp.zeros_like(lines)], axis=0).astype(BF)
        pack[owner, at : at + 16, 0:128] = lines


def weight_back(place, attn_in, mixed, sums, rest=()):
    return call(
        functools.partial(weight_back_body, bool(rest)),
        place,
        (1,),
        [whole(attn_in), whole(mixed), whole(sums)] + [whole(array) for array in rest],
        [whole_out((16, 432 if rest else 112, 256), BF)],
        flops=2_000_000_000,
        moved=6_000_000,
    )[0]


def end_body(place, states, grad, own, came, out):
    unit, scaled = unit_of(states[...].astype(F32))
    through = own[...] + came[...]
    back = scaled * (
        through
        - jnp.mean(through, axis=-1, keepdims=True)
        - unit * jnp.mean(through * unit, axis=-1, keepdims=True)
    )
    out[...] = (grad[...].astype(F32) + back).astype(BF)


def end_back(place, states, grad, own, came):
    return call(
        end_body,
        place,
        (MICRO,),
        [rows(states), rows(grad), rows(own), rows(came)],
        [rows_out(D, BF)],
        flops=100_000_000,
        moved=5_000_000,
    )[0]


def scatter_sum(pack):
    got = lax.all_to_all(pack, "shard", 0, 0, tiled=True)
    return jnp.sum(got.astype(F32), axis=0).astype(BF)


def choose_body(place, *refs):
    keep, send = refs[12:14]
    total = []
    for group in range(3):
        held = refs[4 * group][...].astype(F32)
        for step in range(1, 4):
            held = held + refs[4 * group + step][...].astype(F32)
        total.append(held)
    layer1 = total[0]
    layer0 = jnp.concatenate([total[1], total[2]], axis=0)
    first = place[1] == 0
    keep[...] = jnp.where(first, layer0, layer1)
    send[...] = jnp.where(first, layer1, layer0).astype(BF)


def choose(place, pieces):
    return call(
        choose_body,
        place,
        (1,),
        [whole(piece) for piece in pieces],
        [whole_out((432, 256), F32), whole_out((432, 256), BF)],
    )


def unpack_body(place, keep, got, qkv, proj, up, down, sums, total):
    core = place[1]
    total[core] = keep[...]
    total[1 - core] = got[...].astype(F32)
    low = lax.broadcasted_iota(jnp.int32, (32, 128), 1) < 64
    sums[...] = total[0, 416:424, 0:128] + total[1, 416:424, 0:128]
    for half in range(2):
        for part in range(3):
            at = 512 * part + 256 * half
            qkv[:, at : at + 256] = total[half, 320 + 32 * part : 352 + 32 * part]
        at = 256 + 32 * half
        proj[:, 256 * half : 256 * half + 256] = total[0, at : at + 32] + total[1, at : at + 32]
        for side in range(2):
            down[64 * half : 64 * half + 64, 256 * side : 256 * side + 256] = total[
                half, 128 + 64 * side : 192 + 64 * side
            ]
    for tile in range(16):
        row = 32 * (tile // 4)
        at = 128 * (tile % 4 // 2)
        left = total[0, row : row + 32, at : at + 128]
        right = total[1, row : row + 32, at : at + 128]
        if tile % 2 == 0:
            joined = jnp.where(low, left, pltpu.roll(right, 64, 1))
        else:
            joined = jnp.where(low, pltpu.roll(left, 64, 1), right)
        up[:, 128 * tile : 128 * tile + 128] = joined


def unpack(place, keep, got):
    return call(
        unpack_body,
        place,
        (1,),
        [whole(keep), whole(got)],
        [
            whole_out((32, 1536), F32),
            whole_out((32, 512), F32),
            whole_out((32, 2048), F32),
            whole_out((128, 512), F32),
            whole_out((8, 128), F32),
        ],
        [pltpu.VMEM((2, 432, 256), F32)],
    )


def on_device(
    inputs,
    positions,
    cotangent,
    qkv_weight,
    proj_weight,
    up_weight,
    down_weight,
    norm_gain,
    norm_bias,
):
    core = lax.axis_index("section")
    chip_z = lax.axis_index("seq")
    shard = lax.axis_index("shard")
    first = core == 0
    place = jnp.stack([chip_z, core, shard // 4, shard % 4]).astype(jnp.int32)

    mine, other = pack_weights(
        place, qkv_weight[0], proj_weight[0], up_weight[0], down_weight[0]
    )
    own_norms = jnp.concatenate([norm_gain[0], norm_bias[0]], axis=0).reshape(1, 128)
    other_norms = swap_core(jnp.broadcast_to(own_norms, (16, 128)))[0:1]
    both_norms = jnp.where(
        first,
        jnp.concatenate([own_norms, other_norms], axis=1),
        jnp.concatenate([other_norms, own_norms], axis=1),
    )
    early, middle, late = sort_weights(
        place, mine, swap_core(other), jnp.broadcast_to(both_norms, (16, 256))
    )
    places_row = positions.reshape(1, TOKENS)
    gathered, places = lax.optimization_barrier(
        (gather_now(early), regroup([places_row] * 4))
    )
    middle_all = lax.all_gather(middle, "shard")
    late_all = lax.all_gather(late, "shard")
    norms = (
        gathered[:, 96, :]
        .reshape(16, 2, 4, 32)
        .transpose(1, 2, 0, 3)
        .reshape(2, 4, D)
        .astype(F32)
    )
    qkv_of = ((gathered, 0), (middle_all, 12))
    proj_of = ((middle_all, 4), (middle_all, 5))
    mlp_of = (middle_all, late_all)
    rates = 10000.0 ** (-jnp.arange(ROT // 2, dtype=F32) * 2.0 / ROT)
    angles = rates[:, None] * places_row.astype(F32)
    turns = jnp.stack([jnp.cos(angles), jnp.sin(angles)])

    states = inputs.reshape(TOKENS, D)
    grad = cotangent.reshape(TOKENS, D)
    extra = ()
    saved = []
    for layer in range(2):
        done = before_layer(place, states, extra, qkv_of[layer], norms[layer], turns)
        sent, attn_in, mlp_in = done[0:4], done[4], done[5]
        if layer == 1:
            states = done[6]
        came = regroup(sent)
        if layer == 1:
            sent = attend_both(place, came, places)
            mlp_in = after(mlp_in, sent)
            came = regroup(sent)
        mlp_out, active, slope = mlp_layer(place, mlp_in, mlp_of[layer])
        if layer == 0:
            done = attend(place, came, places)
            kept, heads_out, log_total = done[4:7]
            came = regroup(done[0:4])
        part, heads = after_layer(place, came, 3 * layer, proj_of[layer], mlp_out)
        parts = (part, swap_core(part))
        extra = (parts, grad, proj_of[1])
        saved.append((states, attn_in, mlp_in, active, slope, heads))
    result = (states.astype(F32) + (parts[0] + parts[1])).astype(BF)
    layer_out = jnp.where(first, saved[1][0], result)

    grads = [None, None]
    for layer in (1, 0):
        states, attn_in, mlp_in, active, slope, heads = saved[layer]
        if layer == 1:
            mlp_grad, pack = mlp_back(place, grad, active, slope, mlp_in, mlp_of[1])
        else:
            sent = heads_grad(place, grad, proj_of[0])
            came = regroup(sent)
            mlp_grad, pack = mlp_back(
                place, after(grad, sent), active, slope, mlp_in, mlp_of[0], heads
            )
            came = after(came, pack)
            sent = attend_back(place, came, places, kept, heads_out, log_total)
            sum_a = scatter_sum(pack)
            came = regroup(sent)
        through, mixed, norm_sums = mixed_back(
            place, came, qkv_of[layer], norms[layer], turns, states, mlp_grad
        )
        if layer == 1:
            pack = weight_back(place, attn_in, mixed, norm_sums, (pack, heads, grad))
            total = lax.psum_scatter(pack, "shard", scatter_dimension=0, tiled=False)
            through = after(through, pack)
        else:
            pack, sum_a = lax.optimization_barrier(
                (weight_back(place, attn_in, mixed, norm_sums), sum_a)
            )
            pieces_a = regroup([sum_a] * 4)
            pieces_b = regroup([scatter_sum(pack)] * 4)
        grad = end_back(place, states, grad, through, swap_core(through))
        grads[layer] = grad
    grads_out = jnp.where(first, grads[0], grads[1])

    keep, send = choose(place, regroup([total] * 4) + pieces_a + pieces_b)
    qkv_grad, proj_grad, up_grad, down_grad, norm_sums = unpack(place, keep, swap_core(send))
    return (
        layer_out.reshape(1, MICRO, 1, BLOCK, D),
        grads_out.reshape(1, MICRO, 1, BLOCK, D),
        qkv_grad[None],
        proj_grad[None],
        up_grad[None],
        down_grad[None],
        norm_sums[None, 0:2, 0:32],
        norm_sums[None, 2:4, 0:32],
    )


def solution(mesh):
    placed = (
        P(None, "shard", "seq", None),
        P(None, "shard", "seq"),
        P(None, "shard", "seq", None),
        P("section", "shard", None),
        P("section", "shard", None),
        P("section", "shard", None),
        P("section", "shard", None),
        P("section", None, "shard"),
        P("section", None, "shard"),
    )
    return jax.shard_map(
        on_device,
        mesh=mesh,
        in_specs=placed,
        out_specs=(
            P("section", None, "shard", "seq", None),
            P("section", None, "shard", "seq", None),
            P("section", "shard", None),
            P("section", "shard", None),
            P("section", "shard", None),
            P("section", "shard", None),
            P("section", None, "shard"),
            P("section", None, "shard"),
        ),
        check_vma=False,
    )
```

profile of v0, /device:TPU:1, one launch (start us, length us, event | category | flops | bytes accessed | tf_op | source)
XLA Modules:
  0.0 301.8 jit_solution(12510741925180004697)
XLA Ops:
  8.0 1.4 collective-permute-start.1
  13.8 1.4 collective-permute-done.received
  17.5 6.8 %all-to-all-start = ((bf16[16,112,256]{2,1,0:T(8,128)(2,1)}), bf16[16,112,256]{2,1,0:T(8,128)(2,1)S(1)}, u32[]{:S(2)}, u32[]{:S(2)}) async-start(bf16[16,112,256]{2,1,0:T(8,128)(2,1)} %broadcast_in_dim.34), calls=%async_computation | async-start | bytes 1835008 | tf_op jit(solution)/shard_map/all_to_all | solution.py:171
  24.4 1.7 collective-permute-start.2
  26.1 3.3 %collective-permute-start.3 = (s32[1,768]{1,0:T(1,128)S(1)}, s32[1,768]{1,0:T(1,128)S(1)}, u32[]{:S(2)}, u32[]{:S(2)}) collective-permute-start(s32[1,768]{1,0:T(1,128)S(1)} %bitcast.63), channel_id=1, source_target_pairs={{0,32},{16,48},{32,0},{48,16},{1,33},{17,49},{33,1},{49,17},{2,34}... | collective-permute-start | bytes 9224 | tf_op jit(solution)/shard_map/ppermute | solution.py:162
  30.5 1.8 collective-permute-done.4.refs_7_
  32.3 8.4 %all-to-all-done.refs_1_.refs_2_.refs_3_.refs_4_.refs_5_.refs_6_ = bf16[16,112,256]{2,1,0:T(8,128)(2,1)S(1)} async-done(((bf16[16,112,256]{2,1,0:T(8,128)(2,1)}), bf16[16,112,256]{2,1,0:T(8,128)(2,1)S(1)}, u32[]{:S(2)}, u32[]{:S(2)}) %all-to-all-start) | async-done | bytes 917536 | tf_op jit(solution)/shard_map/all_to_all | solution.py:171
  40.9 3.8 %shard_map.154 = (bf16[192,768]{1,0:T(8,128)(2,1)S(1)}, bf16[192,768]{1,0:T(8,128)(2,1)}, bf16[192,768]{1,0:T(8,128)(2,1)}, bf16[192,768]{1,0:T(8,128)(2,1)S(1)}...) custom-call(s32[4]{0:T(128)S(1)} %pad_add_fusion.place, bf16[768,512]{1,0:T(8,128)(2,1)S(1)} %bitcast.58, ...), custom_call_target="tpu_custom_call" | custom-call | flops 1200000000 | bytes 6000000 | tf_op jit(solution)/shard_map/pallas_call | solution.py:38
  45.5 1.8 collective-permute-start.5
  47.3 3.7 %collective-permute-start.6 = (bf16[192,768]{1,0:T(8,128)(2,1)}, bf16[192,768]{1,0:T(8,128)(2,1)S(1)}, u32[]{:S(2)}, u32[]{:S(2)}) collective-permute-start(bf16[192,768]{1,0:T(8,128)(2,1)} %get-tuple-element.92), channel_id=1, source_target_pairs={{0,32},{16,48},{32,0},{48,16},{1,33},{17,49},{33,1},{49,17},{2,34}... | collective-permute-start | bytes 884744 | tf_op jit(solution)/shard_map/ppermute | solution.py:162
  51.7 2.5 collective-permute-done.5.refs_1_
  54.2 7.1 %collective-permute-done.6.refs_2_ = bf16[192,768]{1,0:T(8,128)(2,1)S(1)} collective-permute-done((bf16[192,768]{1,0:T(8,128)(2,1)}, bf16[192,768]{1,0:T(8,128)(2,1)S(1)}, u32[]{:S(2)}, u32[]{:S(2)}) %collective-permute-start.6) | collective-permute-done | bytes 294944 | tf_op jit(solution)/shard_map/ppermute | solution.py:162
  63.1 7.1 %shard_map.155 = (bf16[64,768]{1,0:T(8,128)(2,1)S(1)}, bf16[64,768]{1,0:T(8,128)(2,1)S(1)}, bf16[64,768]{1,0:T(8,128)(2,1)S(1)}, bf16[64,768]{1,0:T(8,128)(2,1)S...) custom-call(s32[4]{0:T(128)S(1)} %pad_add_fusion.place, ...), custom_call_target="tpu_custom_call" | custom-call | flops 8000000000 | bytes 4000000 | tf_op jit(solution)/shard_map/pallas_call | solution.py:38
  70.2 3.0 %collective-permute-start.8 = (bf16[64,768]{1,0:T(8,128)(2,1)S(1)}, bf16[64,768]{1,0:T(8,128)(2,1)S(1)}, u32[]{:S(2)}, u32[]{:S(2)}) collective-permute-start(bf16[64,768]{1,0:T(8,128)(2,1)S(1)} %get-tuple-element.99), channel_id=1, source_target_pairs={{0,16},{16,32},{32,48},{48,0},{1,17},{17,33},{33,49},{49,1},{2,18}... | collective-permute-start | bytes 294920 | tf_op jit(solution)/shard_map/ppermute | solution.py:162
  73.2 1.7 collective-permute-start.9
  75.6 2.1 copy-done
  78.9 6.5 %shard_map.156 = (f32[768,512]{1,0:T(8,128)S(1)}, bf16[768,1024]{1,0:T(8,128)(2,1)}, f32[768,1024]{1,0:T(8,128)}) custom-call(s32[4]{0:T(128)S(1)} %pad_add_fusion.place, bf16[768,512]{1,0:T(8,128)(2,1)S(1)} %copy-done.38, bf16[16,480,256]{2,1,0:T(8,128)(2,1)S(1)} %bitcast.40, bf16[16,480,256]{2,1,0:T(8,128)(2,1)S(1)} %bitcast.41), custom_call_target="tpu_custom_call" | custom-call | flops 6000000000 | bytes 12000000 | tf_op jit(solution)/shard_map/pallas_call | solution.py:38
  85.4 2.8 shard_map.157
  89.0 2.7 collective-permute-start.11
  91.7 3.3 %collective-permute-done.11.refs_2_ = f32[768,512]{1,0:T(8,128)} collective-permute-done((f32[768,512]{1,0:T(8,128)}, f32[768,512]{1,0:T(8,128)}, u32[]{:S(2)}, u32[]{:S(2)}) %collective-permute-start.11) | collective-permute-done | bytes 1572896 | tf_op jit(solution)/shard_map/ppermute | solution.py:166
  95.0 2.1 copy-done.2
  97.1 5.8 %shard_map.158 = (bf16[256,768]{1,0:T(8,128)(2,1)S(1)}, bf16[256,768]{1,0:T(8,128)(2,1)S(1)}, bf16[256,768]{1,0:T(8,128)(2,1)S(1)}, bf16[256,768]{1,0:T(8,128)(2...) custom-call(s32[4]{0:T(128)S(1)} %pad_add_fusion.place, ...), custom_call_target="tpu_custom_call" | custom-call | flops 1200000000 | bytes 6000000 | tf_op jit(solution)/shard_map/pallas_call | solution.py:38
  104.2 2.0 collective-permute-start.14
  106.2 16.6 %collective-permute-done.12.refs_1_ = bf16[256,768]{1,0:T(8,128)(2,1)S(1)} collective-permute-done((bf16[256,768]{1,0:T(8,128)(2,1)S(1)}, bf16[256,768]{1,0:T(8,128)(2,1)S(1)}, u32[]{:S(2)}, u32[]{:S(2)}) %collective-permute-start.12) | collective-permute-done | bytes 393248 | tf_op jit(solution)/shard_map/ppermute | solution.py:162
  123.1 13.9 %shard_map.159 = (bf16[256,768]{1,0:T(8,128)(2,1)S(1)}, bf16[256,768]{1,0:T(8,128)(2,1)}, bf16[256,768]{1,0:T(8,128)(2,1)}, bf16[256,768]{1,0:T(8,128)(2,1)}) custom-call(s32[4]{0:T(128)S(1)} %pad_add_fusion.place, bf16[256,768]{1,0:T(8,128)(2,1)S(1)} %get-tuple-element.107.refs_0_, bf16[256,768]{1,0:T(8,128)(2,1)S(1)} %collective-permute-done.12.refs_1_, ...), custom_call_target="tpu_custom_call" | custom-call | flops 17999998976 | bytes 5000000 | tf_op jit(solution)/shard_map/pallas_call | solution.py:38
  137.8 1.6 collective-permute-start.15
  139.4 3.0 collective-permute-start.16
  142.4 1.6 copy-done.20
  145.2 6.5 %shard_map.160 = (f32[768,512]{1,0:T(8,128)S(1)}, bf16[768,1024]{1,0:T(8,128)(2,1)}, f32[768,1024]{1,0:T(8,128)}) custom-call(s32[4]{0:T(128)S(1)} %pad_add_fusion.place, bf16[768,512]{1,0:T(8,128)(2,1)S(1)} %copy-done.22, bf16[16,256,256]{2,1,0:T(8,128)(2,1)S(1)} %bitcast.68, bf16[16,256,256]{2,1,0:T(8,128)(2,1)S(1)} %bitcast.69), custom_call_target="tpu_custom_call" | custom-call | flops 6000000000 | bytes 12000000 | tf_op jit(solution)/shard_map/pallas_call | solution.py:38
  151.7 1.9 copy-done.43
  155.0 7.9 %shard_map.162 = (f32[768,512]{1,0:T(8,128)S(1)}, bf16[16,256,256]{2,1,0:T(8,128)(2,1)S(1)}) custom-call(s32[4]{0:T(128)S(1)} %pad_add_fusion.place, bf16[768,512]{1,0:T(8,128)(2,1)S(1)} %bitcast.55, bf16[768,1024]{1,0:T(8,128)(2,1)S(1)} %copy-done.45, f32[768,1024]{1,0:T(8,128)S(1)} %copy-done.43, bf16[768,512]{1,0:T(8,128)(2,1)S(1)} %copy-done.23, ...), custom_call_target="tpu_custom_call" | custom-call | flops 8000000000 | bytes 14000000 | tf_op jit(solution)/shard_map/pallas_call | solution.py:38
  162.9 3.6 %shard_map.161 = (f32[768,512]{1,0:T(8,128)}, bf16[256,768]{1,0:T(8,128)(2,1)S(1)}) custom-call(s32[4]{0:T(128)S(1)} %pad_add_fusion.place, bf16[256,768]{1,0:T(8,128)(2,1)S(1)} %copy-done.13, bf16[256,768]{1,0:T(8,128)(2,1)} %collective-permute-done.15.refs_1_, bf16[256,768]{1,0:T(8,128)(2,1)} %collective-permute-done.16.refs_2_, ...), custom_call_target="tpu_custom_call" | custom-call | flops 800000000 | bytes 4000000 | tf_op jit(solution)/shard_map/pallas_call | solution.py:38
  166.5 4.0 %shard_map.163 = (f32[768,512]{1,0:T(8,128)S(1)}, bf16[3,256,768]{2,1,0:T(8,128)(2,1)S(1)}, f32[8,512]{1,0:T(8,128)S(1)}) custom-call(s32[4]{0:T(128)S(1)} %pad_add_fusion.place, bf16[256,768]{1,0:T(8,128)(2,1)S(1)} %copy-done.13, bf16[256,768]{1,0:T(8,128)(2,1)} %collective-permute-done.15.refs_1_, bf16[256,768]{1,0:T(8,128)(2,1)} %collective-permute-done.16.refs_2_, ...), custom_call_target="tpu_custom_call" | custom-call | flops 1500000000 | bytes 6000000 | tf_op jit(solution)/shard_map/pallas_call | solution.py:38
  171.7 1.6 shard_map.164
  173.3 1.8 copy-done.5
  176.3 3.2 %collective-permute-done.19.came = f32[768,512]{1,0:T(8,128)S(1)} collective-permute-done((f32[768,512]{1,0:T(8,128)}, f32[768,512]{1,0:T(8,128)S(1)}, u32[]{:S(2)}, u32[]{:S(2)}) %collective-permute-start.19) | collective-permute-done | bytes 1572896 | tf_op jit(solution)/shard_map/ppermute | solution.py:166
  182.1 1.7 shard_map.165.grad
  183.9 2.4 shard_map.166
  186.4 1.7 collective-permute-start.20
  188.1 2.4 collective-permute-start.22
  190.5 8.3 %shard_map.167 = (f32[768,512]{1,0:T(8,128)S(1)}, bf16[16,320,256]{2,1,0:T(8,128)(2,1)S(1)}) custom-call(s32[4]{0:T(128)S(1)} %pad_add_fusion.place, bf16[768,512]{1,0:T(8,128)(2,1)S(1)} %shard_map.165.grad, bf16[768,1024]{1,0:T(8,128)(2,1)S(1)} %copy-done.44, f32[768,1024]{1,0:T(8,128)S(1)} %copy-done.42, bf16[768,512]{1,0:T(8,128)(2,1)S(1)} %copy-done.39, ...), custom_call_target="tpu_custom_call" | custom-call | flops 8000000000 | bytes 14000000 | tf_op jit(solution)/shard_map/pallas_call | solution.py:38
  198.8 1.5 copy-done.11
  201.4 4.5 %all-to-all-start.1 = ((bf16[16,320,256]{2,1,0:T(8,128)(2,1)}), bf16[16,320,256]{2,1,0:T(8,128)(2,1)}, u32[]{:S(2)}, u32[]{:S(2)}) async-start(bf16[16,320,256]{2,1,0:T(8,128)(2,1)} %copy-done.11), calls=%async_computation.1 | async-start | bytes 5242880 | tf_op jit(solution)/shard_map/all_to_all | solution.py:735
  208.9 9.2 %shard_map.168 = (bf16[192,768]{1,0:T(8,128)(2,1)S(1)}, bf16[192,768]{1,0:T(8,128)(2,1)S(1)}, bf16[192,768]{1,0:T(8,128)(2,1)S(1)}, bf16[192,768]{1,0:T(8,128)(2,1)S(1)}) custom-call(s32[4]{0:T(128)S(1)} %pad_add_fusion.place, bf16[64,768]{1,0:T(8,128)(2,1)S(1)} %get-tuple-element.139.refs_0_, bf16[64,768]{1,0:T(8,128)(2,1)S(1)} %collective-permute-done.20.refs_1_, ...), custom_call_target="tpu_custom_call" | custom-call | flops 16000000000 | bytes 5000000 | tf_op jit(solution)/shard_map/pallas_call | solution.py:38
  218.2 2.0 collective-permute-start.24
  221.2 2.2 collective-permute-start.18
  223.4 4.3 %collective-permute-done.23.refs_1_ = bf16[192,768]{1,0:T(8,128)(2,1)S(1)} collective-permute-done((bf16[192,768]{1,0:T(8,128)(2,1)S(1)}, bf16[192,768]{1,0:T(8,128)(2,1)S(1)}, u32[]{:S(2)}, u32[]{:S(2)}) %collective-permute-start.23) | collective-permute-done | bytes 294944 | tf_op jit(solution)/shard_map/ppermute | solution.py:162
  227.7 4.7 %collective-permute-done.24.refs_2_ = bf16[192,768]{1,0:T(8,128)(2,1)S(1)} collective-permute-done((bf16[192,768]{1,0:T(8,128)(2,1)S(1)}, bf16[192,768]{1,0:T(8,128)(2,1)S(1)}, u32[]{:S(2)}, u32[]{:S(2)}) %collective-permute-start.24) | collective-permute-done | bytes 294944 | tf_op jit(solution)/shard_map/ppermute | solution.py:162
  232.4 1.9 collective-permute-done.25.refs_3_
  234.2 3.6 %shard_map.169 = (f32[768,512]{1,0:T(8,128)}, bf16[3,256,768]{2,1,0:T(8,128)(2,1)S(1)}, f32[8,512]{1,0:T(8,128)S(1)}) custom-call(s32[4]{0:T(128)S(1)} %pad_add_fusion.place, bf16[192,768]{1,0:T(8,128)(2,1)S(1)} %get-tuple-element.146.refs_0_, bf16[192,768]{1,0:T(8,128)(2,1)S(1)} %collective-permute-done.23.refs_1_, ...), custom_call_target="tpu_custom_call" | custom-call | flops 1500000000 | bytes 6000000 | tf_op jit(solution)/shard_map/pallas_call | solution.py:38
  237.9 1.6 collective-permute-start.26
  239.4 2.3 shard_map.171
  241.7 3.0 all-to-all-done.1
  244.7 2.1 reduce_sum.24.refs_4_
  246.8 5.6 %all-to-all-start.2 = ((bf16[16,112,256]{2,1,0:T(8,128)(2,1)}), bf16[16,112,256]{2,1,0:T(8,128)(2,1)}, u32[]{:S(2)}, u32[]{:S(2)}) async-start(bf16[16,112,256]{2,1,0:T(8,128)(2,1)} %shard_map.171), calls=%async_computation.2 | async-start | bytes 1835008 | tf_op jit(solution)/shard_map/all_to_all | solution.py:735
  252.6 1.6 collective-permute-start.31
  255.2 10.5 %all-to-all-done.2 = bf16[16,112,256]{2,1,0:T(8,128)(2,1)} async-done(((bf16[16,112,256]{2,1,0:T(8,128)(2,1)}), bf16[16,112,256]{2,1,0:T(8,128)(2,1)}, u32[]{:S(2)}, u32[]{:S(2)}) %all-to-all-start.2) | async-done | bytes 917536 | tf_op jit(solution)/shard_map/all_to_all | solution.py:735
  271.4 4.5 %reduce-scatter.4.cloned.1.call-done = bf16[1,432,256]{2,1,0:T(8,128)(2,1)} async-done(((bf16[16,432,256]{2,1,0:T(8,128)(2,1)}), bf16[1,432,256]{2,1,0:T(8,128)(2,1)}) %reduce-scatter.4.cloned.1.call-update) | async-done | bytes 221200
  276.9 1.5 collective-permute-start.28
  279.3 3.2 %fusion = bf16[768,512]{1,0:T(8,128)(2,1)} fusion(bf16[768,512]{1,0:T(8,128)(2,1)S(1)} %copy-done.10, f32[768,512]{1,0:T(8,128)} %get-tuple-element.119, f32[768,512]{1,0:T(8,128)} %collective-permute-done.18, pred[]{:T(512)S(6)} %eq.5), kind=kLoop, calls=%fused_computation.1 | loop fusion | flops 1966080 | bytes 4718593 | tf_op jit(solution)/shard_map/jit(_where)/select_n | solution.py:883
  282.5 3.7 %shard_map.170 = bf16[768,512]{1,0:T(8,128)(2,1)S(1)} custom-call(s32[4]{0:T(128)S(1)} %pad_add_fusion.place, bf16[768,512]{1,0:T(8,128)(2,1)S(1)} %bitcast.61, bf16[768,512]{1,0:T(8,128)(2,1)S(1)} %shard_map.165.grad, f32[768,512]{1,0:T(8,128)} %get-tuple-element.151.own, f32[768,512]{1,0:T(8,128)} %collective-permute-done.26.came), custom_call_target="tpu_custom_call" | custom-call | flops 100000000 | bytes 5000000 | tf_op jit(solution)/shard_map/pallas_call | solution.py:38
  286.3 2.4 collective-permute-done.29.refs_3_
  289.5 2.6 collective-permute-start.36
  293.2 1.5 shard_map.173
  (169 shorter events, 40.9 us)
Async XLA Ops:
  7.2 68.4 %all-gather.5.cloned.1.call-start = ((), (), s32[]{:S(2)}) async-start(), calls=%async_computation.4 | async-start | bytes 4177920 | tf_op jit(solution)/shard_map/all_gather | solution.py:843
  8.0 5.8 %collective-permute-start.1 = (bf16[16,128]{1,0:T(8,128)(2,1)S(1)}, bf16[16,128]{1,0:T(8,128)(2,1)S(1)}, u32[]{:S(2)}, u32[]{:S(2)}) collective-permute-start(bf16[16,128]{1,0:T(8,128)(2,1)S(1)} %broadcast_in_dim.32), channel_id=1, source_target_pairs={{0,64},{64,0},{1,65},{65,1},{2,66},{66,2},{3,67},{67,3},{4,68},{68... | collective-permute-start | bytes 12296 | tf_op jit(solution)/shard_map/ppermute | solution.py:166
  13.6 1.5 collective-permute-start
  16.5 7.9 %copy-start.19 = (s32[3,1,256]{2,1,0:T(1,128)S(1)}, s32[3,1,256]{2,1,0:T(1,128)}, u32[]{:S(2)}) copy-start(s32[3,1,256]{2,1,0:T(1,128)} %param.10) | copy-start | bytes 9220
  16.5 24.4 %copy-start.7 = (bf16[3,1,256,512]{3,2,1,0:T(8,128)(2,1)S(1)}, bf16[3,1,256,512]{3,2,1,0:T(8,128)(2,1)}, u32[]{:S(2)}) copy-start(bf16[3,1,256,512]{3,2,1,0:T(8,128)(2,1)} %param.9) | copy-start | bytes 2359300
  17.5 23.1 %all-to-all-start = ((bf16[16,112,256]{2,1,0:T(8,128)(2,1)}), bf16[16,112,256]{2,1,0:T(8,128)(2,1)S(1)}, u32[]{:S(2)}, u32[]{:S(2)}) async-start(bf16[16,112,256]{2,1,0:T(8,128)(2,1)} %broadcast_in_dim.34), calls=%async_computation | async-start | bytes 1835008 | tf_op jit(solution)/shard_map/all_to_all | solution.py:171
  24.4 118.1 %all-gather.7.cloned.1.call-start = ((), (), s32[]{:S(2)}) async-start(), calls=%async_computation.5 | async-start | bytes 2228224 | tf_op jit(solution)/shard_map/all_gather | solution.py:844
  24.4 6.0 %collective-permute-start.2 = (s32[1,768]{1,0:T(1,128)S(1)}, s32[1,768]{1,0:T(1,128)S(1)}, u32[]{:S(2)}, u32[]{:S(2)}) collective-permute-start(s32[1,768]{1,0:T(1,128)S(1)} %bitcast.62), channel_id=1, source_target_pairs={{0,16},{16,32},{32,48},{48,0},{1,17},{17,33},{33,49},{49,1},{2,18}... | collective-permute-start | bytes 9224 | tf_op jit(solution)/shard_map/ppermute | solution.py:162
  26.1 4.4 %collective-permute-start.3 = (s32[1,768]{1,0:T(1,128)S(1)}, s32[1,768]{1,0:T(1,128)S(1)}, u32[]{:S(2)}, u32[]{:S(2)}) collective-permute-start(s32[1,768]{1,0:T(1,128)S(1)} %bitcast.63), channel_id=1, source_target_pairs={{0,32},{16,48},{32,0},{48,16},{1,33},{17,49},{33,1},{49,17},{2,34}... | collective-permute-start | bytes 9224 | tf_op jit(solution)/shard_map/ppermute | solution.py:162
  29.4 2.8 collective-permute-start.4
  45.5 8.6 %collective-permute-start.5 = (bf16[192,768]{1,0:T(8,128)(2,1)}, bf16[192,768]{1,0:T(8,128)(2,1)S(1)}, u32[]{:S(2)}, u32[]{:S(2)}) collective-permute-start(bf16[192,768]{1,0:T(8,128)(2,1)} %get-tuple-element.91), channel_id=1, source_target_pairs={{0,16},{16,32},{32,48},{48,0},{1,17},{17,33},{33,49},{49,1},{2,18}... | collective-permute-start | bytes 884744 | tf_op jit(solution)/shard_map/ppermute | solution.py:162
  47.3 13.9 %collective-permute-start.6 = (bf16[192,768]{1,0:T(8,128)(2,1)}, bf16[192,768]{1,0:T(8,128)(2,1)S(1)}, u32[]{:S(2)}, u32[]{:S(2)}) collective-permute-start(bf16[192,768]{1,0:T(8,128)(2,1)} %get-tuple-element.92), channel_id=1, source_target_pairs={{0,32},{16,48},{32,0},{48,16},{1,33},{17,49},{33,1},{49,17},{2,34}... | collective-permute-start | bytes 884744 | tf_op jit(solution)/shard_map/ppermute | solution.py:162
  51.0 11.1 %collective-permute-start.7 = (bf16[192,768]{1,0:T(8,128)(2,1)S(1)}, bf16[192,768]{1,0:T(8,128)(2,1)S(1)}, u32[]{:S(2)}, u32[]{:S(2)}) collective-permute-start(bf16[192,768]{1,0:T(8,128)(2,1)S(1)} %get-tuple-element.93), channel_id=1, source_target_pairs={{0,48},{16,0},{32,16},{48,32},{1,49},{17,1},{33,17},{49,33},{2,50}... | collective-permute-start | bytes 884744 | tf_op jit(solution)/shard_map/ppermute | solution.py:162
  51.6 224.3 %reduce-scatter.4.cloned.1.call-start = ((), (), s32[]{:S(2)}) async-start(), calls=%async_computation.6 | async-start | bytes 3760128
  70.2 15.2 %collective-permute-start.8 = (bf16[64,768]{1,0:T(8,128)(2,1)S(1)}, bf16[64,768]{1,0:T(8,128)(2,1)S(1)}, u32[]{:S(2)}, u32[]{:S(2)}) collective-permute-start(bf16[64,768]{1,0:T(8,128)(2,1)S(1)} %get-tuple-element.99), channel_id=1, source_target_pairs={{0,16},{16,32},{32,48},{48,0},{1,17},{17,33},{33,49},{49,1},{2,18}... | collective-permute-start | bytes 294920 | tf_op jit(solution)/shard_map/ppermute | solution.py:162
  73.2 12.2 %collective-permute-start.9 = (bf16[64,768]{1,0:T(8,128)(2,1)S(1)}, bf16[64,768]{1,0:T(8,128)(2,1)S(1)}, u32[]{:S(2)}, u32[]{:S(2)}) collective-permute-start(bf16[64,768]{1,0:T(8,128)(2,1)S(1)} %get-tuple-element.100), channel_id=1, source_target_pairs={{0,32},{16,48},{32,0},{48,16},{1,33},{17,49},{33,1},{49,17},{2,34}... | collective-permute-start | bytes 294920 | tf_op jit(solution)/shard_map/ppermute | solution.py:162
  74.9 10.5 %collective-permute-start.10 = (bf16[64,768]{1,0:T(8,128)(2,1)S(1)}, bf16[64,768]{1,0:T(8,128)(2,1)S(1)}, u32[]{:S(2)}, u32[]{:S(2)}) collective-permute-start(bf16[64,768]{1,0:T(8,128)(2,1)S(1)} %get-tuple-element.101), channel_id=1, source_target_pairs={{0,48},{16,0},{32,16},{48,32},{1,49},{17,1},{33,17},{49,33},{2,50}... | collective-permute-start | bytes 294920 | tf_op jit(solution)/shard_map/ppermute | solution.py:162
  78.9 6.5 %copy-start.1 = (bf16[7680,256]{1,0:T(8,128)(2,1)S(1)}, bf16[7680,256]{1,0:T(8,128)(2,1)}, u32[]{:S(2)}) copy-start(bf16[7680,256]{1,0:T(8,128)(2,1)} %all-gather.5.cloned.1.call-done) | copy-start | bytes 11796484
  85.4 9.7 %copy-start.6 = (bf16[3,1,256,512]{3,2,1,0:T(8,128)(2,1)S(1)}, bf16[3,1,256,512]{3,2,1,0:T(8,128)(2,1)}, u32[]{:S(2)}) copy-start(bf16[3,1,256,512]{3,2,1,0:T(8,128)(2,1)} %param.11) | copy-start | bytes 2359300
  89.0 6.1 %collective-permute-start.11 = (f32[768,512]{1,0:T(8,128)}, f32[768,512]{1,0:T(8,128)}, u32[]{:S(2)}, u32[]{:S(2)}) collective-permute-start(f32[768,512]{1,0:T(8,128)} %get-tuple-element.105.refs_1_), channel_id=1, source_target_pairs={{0,64},{64,0},{1,65},{65,1},{2,66},{66,2},{3,67},{67,3},{4,68},{68... | collective-permute-start | bytes 4718600 | tf_op jit(solution)/shard_map/ppermute | solution.py:166
  102.9 19.9 %collective-permute-start.12 = (bf16[256,768]{1,0:T(8,128)(2,1)S(1)}, bf16[256,768]{1,0:T(8,128)(2,1)S(1)}, u32[]{:S(2)}, u32[]{:S(2)}) collective-permute-start(bf16[256,768]{1,0:T(8,128)(2,1)S(1)} %get-tuple-element.108), channel_id=1, source_target_pairs={{0,16},{16,32},{32,48},{48,0},{1,17},{17,33},{33,49},{49,1},{2,18}... | collective-permute-start | bytes 1179656 | tf_op jit(solution)/shard_map/ppermute | solution.py:162
  103.5 19.3 %collective-permute-start.13 = (bf16[256,768]{1,0:T(8,128)(2,1)S(1)}, bf16[256,768]{1,0:T(8,128)(2,1)S(1)}, u32[]{:S(2)}, u32[]{:S(2)}) collective-permute-start(bf16[256,768]{1,0:T(8,128)(2,1)S(1)} %get-tuple-element.109), channel_id=1, source_target_pairs={{0,32},{16,48},{32,0},{48,16},{1,33},{17,49},{33,1},{49,17},{2,34}... | collective-permute-start | bytes 1179656 | tf_op jit(solution)/shard_map/ppermute | solution.py:162
  104.2 19.0 %collective-permute-start.14 = (bf16[256,768]{1,0:T(8,128)(2,1)S(1)}, bf16[256,768]{1,0:T(8,128)(2,1)S(1)}, u32[]{:S(2)}, u32[]{:S(2)}) collective-permute-start(bf16[256,768]{1,0:T(8,128)(2,1)S(1)} %get-tuple-element.110), channel_id=1, source_target_pairs={{0,48},{16,0},{32,16},{48,32},{1,49},{17,1},{33,17},{49,33},{2,50}... | collective-permute-start | bytes 1179656 | tf_op jit(solution)/shard_map/ppermute | solution.py:162
  137.8 25.0 %collective-permute-start.15 = (bf16[256,768]{1,0:T(8,128)(2,1)}, bf16[256,768]{1,0:T(8,128)(2,1)}, u32[]{:S(2)}, u32[]{:S(2)}) collective-permute-start(bf16[256,768]{1,0:T(8,128)(2,1)} %get-tuple-element.112), channel_id=1, source_target_pairs={{0,16},{16,32},{32,48},{48,0},{1,17},{17,33},{33,49},{49,1},{2,18}... | collective-permute-start | bytes 1179656 | tf_op jit(solution)/shard_map/ppermute | solution.py:162
  139.4 23.4 %collective-permute-start.16 = (bf16[256,768]{1,0:T(8,128)(2,1)}, bf16[256,768]{1,0:T(8,128)(2,1)}, u32[]{:S(2)}, u32[]{:S(2)}) collective-permute-start(bf16[256,768]{1,0:T(8,128)(2,1)} %get-tuple-element.113), channel_id=1, source_target_pairs={{0,32},{16,48},{32,0},{48,16},{1,33},{17,49},{33,1},{49,17},{2,34}... | collective-permute-start | bytes 1179656 | tf_op jit(solution)/shard_map/ppermute | solution.py:162
  142.4 20.4 %collective-permute-start.17 = (bf16[256,768]{1,0:T(8,128)(2,1)}, bf16[256,768]{1,0:T(8,128)(2,1)}, u32[]{:S(2)}, u32[]{:S(2)}) collective-permute-start(bf16[256,768]{1,0:T(8,128)(2,1)} %get-tuple-element.114), channel_id=1, source_target_pairs={{0,48},{16,0},{32,16},{48,32},{1,49},{17,1},{33,17},{49,33},{2,50}... | collective-permute-start | bytes 1179656 | tf_op jit(solution)/shard_map/ppermute | solution.py:162
  145.2 6.5 %copy-start.21 = (bf16[4096,256]{1,0:T(8,128)(2,1)S(1)}, bf16[4096,256]{1,0:T(8,128)(2,1)}, u32[]{:S(2)}) copy-start(bf16[4096,256]{1,0:T(8,128)(2,1)} %all-gather.7.cloned.1.call-done) | copy-start | bytes 6291460
  145.2 6.5 %copy-start.23 = (bf16[768,512]{1,0:T(8,128)(2,1)S(1)}, bf16[768,512]{1,0:T(8,128)(2,1)}, u32[]{:S(2)}) copy-start(bf16[768,512]{1,0:T(8,128)(2,1)} %get-tuple-element.116.mlp_in) | copy-start | bytes 2359300
  155.0 7.9 %copy-start.3 = (bf16[7680,256]{1,0:T(8,128)(2,1)S(1)}, bf16[7680,256]{1,0:T(8,128)(2,1)}, u32[]{:S(2)}) copy-start(bf16[7680,256]{1,0:T(8,128)(2,1)} %all-gather.5.cloned.1.call-done) | copy-start | bytes 11796484
  155.0 7.9 %copy-start.13 = (bf16[256,768]{1,0:T(8,128)(2,1)S(1)}, bf16[256,768]{1,0:T(8,128)(2,1)}, u32[]{:S(2)}) copy-start(bf16[256,768]{1,0:T(8,128)(2,1)} %copy-done.12) | copy-start | bytes 1179652
  166.5 5.2 %copy-start.18 = (bf16[768,512]{1,0:T(8,128)(2,1)S(1)}, bf16[768,512]{1,0:T(8,128)(2,1)}, u32[]{:S(2)}) copy-start(bf16[768,512]{1,0:T(8,128)(2,1)} %get-tuple-element.124.attn_in) | copy-start | bytes 2359300
  175.2 8.7 %copy-start.4 = (bf16[7680,256]{1,0:T(8,128)(2,1)S(1)}, bf16[7680,256]{1,0:T(8,128)(2,1)}, u32[]{:S(2)}) copy-start(bf16[7680,256]{1,0:T(8,128)(2,1)} %all-gather.5.cloned.1.call-done) | copy-start | bytes 11796484
  175.2 4.4 %collective-permute-start.19 = (f32[768,512]{1,0:T(8,128)}, f32[768,512]{1,0:T(8,128)S(1)}, u32[]{:S(2)}, u32[]{:S(2)}) collective-permute-start(f32[768,512]{1,0:T(8,128)} %copy-done.16), channel_id=1, source_target_pairs={{0,64},{64,0},{1,65},{65,1},{2,66},{66,2},{3,67},{67,3},{4,68},{68... | collective-permute-start | bytes 4718600 | tf_op jit(solution)/shard_map/ppermute | solution.py:166
  182.1 8.4 %copy-start.44 = (bf16[768,1024]{1,0:T(8,128)(2,1)S(1)}, bf16[768,1024]{1,0:T(8,128)(2,1)}, u32[]{:S(2)}) copy-start(bf16[768,1024]{1,0:T(8,128)(2,1)} %get-tuple-element.135.active) | copy-start | bytes 4718596
  183.9 6.6 %copy-start.25 = (bf16[256,768]{1,0:T(8,128)(2,1)S(1)}, bf16[256,768]{1,0:T(8,128)(2,1)}, u32[]{:S(2)}) copy-start(bf16[256,768]{1,0:T(8,128)(2,1)} %copy-done.24) | copy-start | bytes 1179652
  183.9 6.6 %copy-start.39 = (bf16[768,512]{1,0:T(8,128)(2,1)S(1)}, bf16[768,512]{1,0:T(8,128)(2,1)}, u32[]{:S(2)}) copy-start(bf16[768,512]{1,0:T(8,128)(2,1)} %get-tuple-element.103.mlp_in) | copy-start | bytes 2359300
  183.9 6.6 %copy-start.42 = (f32[768,1024]{1,0:T(8,128)S(1)}, f32[768,1024]{1,0:T(8,128)}, u32[]{:S(2)}) copy-start(f32[768,1024]{1,0:T(8,128)} %get-tuple-element.136.slope) | copy-start | bytes 9437188
  186.4 19.5 %collective-permute-start.20 = (bf16[64,768]{1,0:T(8,128)(2,1)}, bf16[64,768]{1,0:T(8,128)(2,1)S(1)}, u32[]{:S(2)}, u32[]{:S(2)}) collective-permute-start(bf16[64,768]{1,0:T(8,128)(2,1)} %get-tuple-element.131), channel_id=1, source_target_pairs={{0,16},{16,32},{32,48},{48,0},{1,17},{17,33},{33,49},{49,1},{2,18}... | collective-permute-start | bytes 294920 | tf_op jit(solution)/shard_map/ppermute | solution.py:162
  188.1 17.8 %collective-permute-start.21 = (bf16[64,768]{1,0:T(8,128)(2,1)S(1)}, bf16[64,768]{1,0:T(8,128)(2,1)S(1)}, u32[]{:S(2)}, u32[]{:S(2)}) collective-permute-start(bf16[64,768]{1,0:T(8,128)(2,1)S(1)} %get-tuple-element.132), channel_id=1, source_target_pairs={{0,32},{16,48},{32,0},{48,16},{1,33},{17,49},{33,1},{49,17},{2,34}... | collective-permute-start | bytes 294920 | tf_op jit(solution)/shard_map/ppermute | solution.py:162
  188.1 17.8 %collective-permute-start.22 = (bf16[64,768]{1,0:T(8,128)(2,1)S(1)}, bf16[64,768]{1,0:T(8,128)(2,1)S(1)}, u32[]{:S(2)}, u32[]{:S(2)}) collective-permute-start(bf16[64,768]{1,0:T(8,128)(2,1)S(1)} %get-tuple-element.133), channel_id=1, source_target_pairs={{0,48},{16,0},{32,16},{48,32},{1,49},{17,1},{33,17},{49,33},{2,50}... | collective-permute-start | bytes 294920 | tf_op jit(solution)/shard_map/ppermute | solution.py:162
  201.4 43.3 %all-to-all-start.1 = ((bf16[16,320,256]{2,1,0:T(8,128)(2,1)}), bf16[16,320,256]{2,1,0:T(8,128)(2,1)}, u32[]{:S(2)}, u32[]{:S(2)}) async-start(bf16[16,320,256]{2,1,0:T(8,128)(2,1)} %copy-done.11), calls=%async_computation.1 | async-start | bytes 5242880 | tf_op jit(solution)/shard_map/all_to_all | solution.py:735
  208.9 25.3 %copy-start.15 = (f32[768,512]{1,0:T(8,128)S(1)}, f32[768,512]{1,0:T(8,128)}, u32[]{:S(2)}) copy-start(f32[768,512]{1,0:T(8,128)} %copy-done.14) | copy-start | bytes 4718596
  218.2 9.6 %collective-permute-start.23 = (bf16[192,768]{1,0:T(8,128)(2,1)S(1)}, bf16[192,768]{1,0:T(8,128)(2,1)S(1)}, u32[]{:S(2)}, u32[]{:S(2)}) collective-permute-start(bf16[192,768]{1,0:T(8,128)(2,1)S(1)} %get-tuple-element.147), channel_id=1, source_target_pairs={{0,16},{16,32},{32,48},{48,0},{1,17},{17,33},{33,49},{49,1},{2,18}... | collective-permute-start | bytes 884744 | tf_op jit(solution)/shard_map/ppermute | solution.py:162
  218.2 14.2 %collective-permute-start.24 = (bf16[192,768]{1,0:T(8,128)(2,1)S(1)}, bf16[192,768]{1,0:T(8,128)(2,1)S(1)}, u32[]{:S(2)}, u32[]{:S(2)}) collective-permute-start(bf16[192,768]{1,0:T(8,128)(2,1)S(1)} %get-tuple-element.148), channel_id=1, source_target_pairs={{0,32},{16,48},{32,0},{48,16},{1,33},{17,49},{33,1},{49,17},{2,34}... | collective-permute-start | bytes 884744 | tf_op jit(solution)/shard_map/ppermute | solution.py:162
  220.3 14.0 %collective-permute-start.25 = (bf16[192,768]{1,0:T(8,128)(2,1)S(1)}, bf16[192,768]{1,0:T(8,128)(2,1)S(1)}, u32[]{:S(2)}, u32[]{:S(2)}) collective-permute-start(bf16[192,768]{1,0:T(8,128)(2,1)S(1)} %get-tuple-element.149), channel_id=1, source_target_pairs={{0,48},{16,0},{32,16},{48,32},{1,49},{17,1},{33,17},{49,33},{2,50}... | collective-permute-start | bytes 884744 | tf_op jit(solution)/shard_map/ppermute | solution.py:162
  221.2 45.8 %collective-permute-start.18 = (f32[768,512]{1,0:T(8,128)}, f32[768,512]{1,0:T(8,128)}, u32[]{:S(2)}, u32[]{:S(2)}) collective-permute-start(f32[768,512]{1,0:T(8,128)} %get-tuple-element.119), channel_id=1, source_target_pairs={{0,64},{64,0},{1,65},{65,1},{2,66},{66,2},{3,67},{67,3},{4,68},{68... | collective-permute-start | bytes 4718600 | tf_op jit(solution)/shard_map/ppermute | solution.py:166
  234.2 5.2 %copy-start.37 = (bf16[768,512]{1,0:T(8,128)(2,1)S(1)}, bf16[768,512]{1,0:T(8,128)(2,1)}, u32[]{:S(2)}) copy-start(bf16[768,512]{1,0:T(8,128)(2,1)} %get-tuple-element.152.attn_in) | copy-start | bytes 2359300
  237.9 29.7 %collective-permute-start.26 = (f32[768,512]{1,0:T(8,128)}, f32[768,512]{1,0:T(8,128)}, u32[]{:S(2)}, u32[]{:S(2)}) collective-permute-start(f32[768,512]{1,0:T(8,128)} %get-tuple-element.151.own), channel_id=1, source_target_pairs={{0,64},{64,0},{1,65},{65,1},{2,66},{66,2},{3,67},{67,3},{4,68},{68... | collective-permute-start | bytes 4718600 | tf_op jit(solution)/shard_map/ppermute | solution.py:166
  246.8 32.5 %copy-start.10 = (bf16[768,512]{1,0:T(8,128)(2,1)S(1)}, bf16[768,512]{1,0:T(8,128)(2,1)}, u32[]{:S(2)}) copy-start(bf16[768,512]{1,0:T(8,128)(2,1)} %get-tuple-element.106.refs_9_.states) | copy-start | bytes 2359300
  246.8 18.9 %all-to-all-start.2 = ((bf16[16,112,256]{2,1,0:T(8,128)(2,1)}), bf16[16,112,256]{2,1,0:T(8,128)(2,1)}, u32[]{:S(2)}, u32[]{:S(2)}) async-start(bf16[16,112,256]{2,1,0:T(8,128)(2,1)} %shard_map.171), calls=%async_computation.2 | async-start | bytes 1835008 | tf_op jit(solution)/shard_map/all_to_all | solution.py:735
  252.5 16.3 %collective-permute-start.30 = (bf16[320,256]{1,0:T(8,128)(2,1)S(1)}, bf16[320,256]{1,0:T(8,128)(2,1)S(1)}, u32[]{:S(2)}, u32[]{:S(2)}) collective-permute-start(bf16[320,256]{1,0:T(8,128)(2,1)S(1)} %reduce_sum.24.refs_4_), channel_id=1, source_target_pairs={{0,16},{16,32},{32,48},{48,0},{1,17},{17,33},{33,49},{49,1},{2,18}... | collective-permute-start | bytes 491528 | tf_op jit(solution)/shard_map/ppermute | solution.py:162
  252.6 18.2 %collective-permute-start.31 = (bf16[320,256]{1,0:T(8,128)(2,1)S(1)}, bf16[320,256]{1,0:T(8,128)(2,1)S(1)}, u32[]{:S(2)}, u32[]{:S(2)}) collective-permute-start(bf16[320,256]{1,0:T(8,128)(2,1)S(1)} %reduce_sum.24.refs_4_), channel_id=1, source_target_pairs={{0,32},{16,48},{32,0},{48,16},{1,33},{17,49},{33,1},{49,17},{2,34}... | collective-permute-start | bytes 491528 | tf_op jit(solution)/shard_map/ppermute | solution.py:162
  254.2 22.1 %collective-permute-start.32 = (bf16[320,256]{1,0:T(8,128)(2,1)S(1)}, bf16[320,256]{1,0:T(8,128)(2,1)S(1)}, u32[]{:S(2)}, u32[]{:S(2)}) collective-permute-start(bf16[320,256]{1,0:T(8,128)(2,1)S(1)} %reduce_sum.24.refs_4_), channel_id=1, source_target_pairs={{0,48},{16,0},{32,16},{48,32},{1,49},{17,1},{33,17},{49,33},{2,50}... | collective-permute-start | bytes 491528 | tf_op jit(solution)/shard_map/ppermute | solution.py:162
  267.0 11.3 %collective-permute-start.33 = (bf16[112,256]{1,0:T(8,128)(2,1)S(1)}, bf16[112,256]{1,0:T(8,128)(2,1)S(1)}, u32[]{:S(2)}, u32[]{:S(2)}) collective-permute-start(bf16[112,256]{1,0:T(8,128)(2,1)S(1)} %reduce_sum.25.refs_8_), channel_id=1, source_target_pairs={{0,16},{16,32},{32,48},{48,0},{1,17},{17,33},{33,49},{49,1},{2,18}... | collective-permute-start | bytes 172040 | tf_op jit(solution)/shard_map/ppermute | solution.py:162
  267.6 18.7 %collective-permute-start.34 = (bf16[112,256]{1,0:T(8,128)(2,1)S(1)}, bf16[112,256]{1,0:T(8,128)(2,1)S(1)}, u32[]{:S(2)}, u32[]{:S(2)}) collective-permute-start(bf16[112,256]{1,0:T(8,128)(2,1)S(1)} %reduce_sum.25.refs_8_), channel_id=1, source_target_pairs={{0,32},{16,48},{32,0},{48,16},{1,33},{17,49},{33,1},{49,17},{2,34}... | collective-permute-start | bytes 172040 | tf_op jit(solution)/shard_map/ppermute | solution.py:162
  269.4 16.9 %collective-permute-start.35 = (bf16[112,256]{1,0:T(8,128)(2,1)S(1)}, bf16[112,256]{1,0:T(8,128)(2,1)S(1)}, u32[]{:S(2)}, u32[]{:S(2)}) collective-permute-start(bf16[112,256]{1,0:T(8,128)(2,1)S(1)} %reduce_sum.25.refs_8_), channel_id=1, source_target_pairs={{0,48},{16,0},{32,16},{48,32},{1,49},{17,1},{33,17},{49,33},{2,50}... | collective-permute-start | bytes 172040 | tf_op jit(solution)/shard_map/ppermute | solution.py:162
  275.9 10.4 %collective-permute-start.27 = (bf16[432,256]{1,0:T(8,128)(2,1)}, bf16[432,256]{1,0:T(8,128)(2,1)S(1)}, u32[]{:S(2)}, u32[]{:S(2)}) collective-permute-start(bf16[432,256]{1,0:T(8,128)(2,1)} %bitcast.72), channel_id=1, source_target_pairs={{0,16},{16,32},{32,48},{48,0},{1,17},{17,33},{33,49},{49,1},{2,18}... | collective-permute-start | bytes 663560 | tf_op jit(solution)/shard_map/ppermute | solution.py:162
  276.9 9.4 %collective-permute-start.28 = (bf16[432,256]{1,0:T(8,128)(2,1)}, bf16[432,256]{1,0:T(8,128)(2,1)S(1)}, u32[]{:S(2)}, u32[]{:S(2)}) collective-permute-start(bf16[432,256]{1,0:T(8,128)(2,1)} %bitcast.73), channel_id=1, source_target_pairs={{0,32},{16,48},{32,0},{48,16},{1,33},{17,49},{33,1},{49,17},{2,34}... | collective-permute-start | bytes 663560 | tf_op jit(solution)/shard_map/ppermute | solution.py:162
  278.4 10.4 %collective-permute-start.29 = (bf16[432,256]{1,0:T(8,128)(2,1)}, bf16[432,256]{1,0:T(8,128)(2,1)S(1)}, u32[]{:S(2)}, u32[]{:S(2)}) collective-permute-start(bf16[432,256]{1,0:T(8,128)(2,1)} %bitcast.74), channel_id=1, source_target_pairs={{0,48},{16,0},{32,16},{48,32},{1,49},{17,1},{33,17},{49,33},{2,50}... | collective-permute-start | bytes 663560 | tf_op jit(solution)/shard_map/ppermute | solution.py:162
  282.5 6.2 %copy-start.26 = (bf16[1,432,256]{2,1,0:T(8,128)(2,1)S(1)}, bf16[1,432,256]{2,1,0:T(8,128)(2,1)}, u32[]{:S(2)}) copy-start(bf16[1,432,256]{2,1,0:T(8,128)(2,1)} %reduce-scatter.4.cloned.1.call-done) | copy-start | bytes 663556
  282.5 6.2 %copy-start.28 = (bf16[320,256]{1,0:T(8,128)(2,1)S(1)}, bf16[320,256]{1,0:T(8,128)(2,1)}, u32[]{:S(2)}) copy-start(bf16[320,256]{1,0:T(8,128)(2,1)} %copy-done.27) | copy-start | bytes 491524
  282.5 6.2 %copy-start.30 = (bf16[320,256]{1,0:T(8,128)(2,1)S(1)}, bf16[320,256]{1,0:T(8,128)(2,1)}, u32[]{:S(2)}) copy-start(bf16[320,256]{1,0:T(8,128)(2,1)} %copy-done.29) | copy-start | bytes 491524
  282.5 6.2 %copy-start.32 = (bf16[320,256]{1,0:T(8,128)(2,1)S(1)}, bf16[320,256]{1,0:T(8,128)(2,1)}, u32[]{:S(2)}) copy-start(bf16[320,256]{1,0:T(8,128)(2,1)} %copy-done.31) | copy-start | bytes 491524
  289.5 3.7 %collective-permute-start.36 = (bf16[432,256]{1,0:T(8,128)(2,1)S(1)}, bf16[432,256]{1,0:T(8,128)(2,1)S(1)}, u32[]{:S(2)}, u32[]{:S(2)}) collective-permute-start(bf16[432,256]{1,0:T(8,128)(2,1)S(1)} %get-tuple-element.158), channel_id=1, source_target_pairs={{0,64},{64,0},{1,65},{65,1},{2,66},{66,2},{3,67},{67,3},{4,68},{68... | collective-permute-start | bytes 663560 | tf_op jit(solution)/shard_map/ppermute | solution.py:166
  (28 other events, 34.8 us)
Sparse Core Ops, SparseCore 0:
  16.6 56.6 all-gather.4
  76.0 43.6 all-gather.6
  175.3 100.5 reduce-scatter.3
where the time goes:
time: 303 us; the launch traced here: 302 us
  Pallas kernels  99.2 us (33%)
  waiting for transfers between devices  77 us (25%)
  starting transfers between devices  69.6 us (23%)
  local copies, waits for them, and re-layouts  33.2 us (11%)
  between operations  14.2 us (5%)
  other arithmetic  8.61 us (3%)
    pallas_call x22, Pallas kernels, call(): pl.pallas_call(body, out_shape=[(pltpu.HBM if out[4:] else struct)(out[0]...  99.2 us
    ppermute x30, waiting for transfers between devices, shift_z(): return lax.ppermute(value, 'seq', [(z, (z + step) % 4) for z in range(4)])  42.5 us
    ppermute x30, starting transfers between devices, shift_z(): return lax.ppermute(value, 'seq', [(z, (z + step) % 4) for z in range(4)])  40.9 us
    unnamed x98, local copies, waits for them, and re-layouts  31.2 us
    all_to_all x2, waiting for transfers between devices, scatter_sum(): got = lax.all_to_all(pack, 'shard', 0, 0, tiled=True)  13.5 us
    ppermute x7, starting transfers between devices, swap_core(): return lax.ppermute(value, 'section', [(0, 1), (1, 0)])  11.7 us
    all_to_all x2, starting transfers between devices, scatter_sum(): got = lax.all_to_all(pack, 'shard', 0, 0, tiled=True)  10.1 us
    all_to_all x1, waiting for transfers between devices, gather_now(): return lax.all_to_all(copies, 'shard', 0, 0, tiled=True)  8.38 us
  transfers between devices with their start and end apart: 43, of which 19 were waited for; matrix products, arithmetic and copies ran while one was open for 3% of the time, Pallas kernels for 29%

commit v1 on v0

--- a/solution.py
+++ b/solution.py
@@ -30,6 +30,10 @@
 
 def struct(shape, dtype):
     return jax.ShapeDtypeStruct(shape, dtype)
+
+
+def in_hbm(array):
+    return pltpu.with_memory_space_constraint(array, pltpu.HBM)
 
 
 def call(body, place, grid, ins, outs, scratch=(), flops=10**9, moved=4 * 10**6):
@@ -97,7 +101,7 @@
     return (shape, dtype, (1,) + shape[1:], lambda m, _: (m,) + (0,) * rank)
 
 
-def pack_body(place, qkv, proj, up, down, mine, other, held):
+def pack_body(place, qkv, proj, up, down, norms, mine, other, held):
     low = lax.broadcasted_iota(jnp.int32, (32, 128), 1) < 64
     for half in range(2):
         for pair in range(8):
@@ -119,42 +123,46 @@
         for part in range(3):
             at = 512 * part + 256 * half
             held[half, 320 + 32 * part : 352 + 32 * part, :] = qkv[:, at : at + 256]
+        held[half, 416:432, 0:128] = norms[...]
+        held[half, 416:432, 128:256] = norms[...]
     core = place[1]
     mine[...] = held[core]
     other[...] = held[1 - core]
 
 
-def pack_weights(place, qkv, proj, up, down):
+def pack_weights(place, qkv, proj, up, down, norms):
     return call(
         pack_body,
         place,
         (1,),
-        [whole(qkv), whole(proj), whole(up), whole(down)],
-        [whole_out((416, 256), BF), whole_out((416, 256), BF)],
-        [pltpu.VMEM((2, 416, 256), BF)],
-    )
-
-
-def sort_body(place, mine, received, norms, early, middle, late):
+        [whole(qkv), whole(proj), whole(up), whole(down), whole(norms)],
+        [whole_out((432, 256), BF), whole_out((432, 256), BF)],
+        [pltpu.VMEM((2, 432, 256), BF)],
+    )
+
+
+def sort_body(place, mine, received, early, middle, late):
     first = place[1] == 0
     kept = mine[...]
     came = received[...]
     layer0 = jnp.where(first, kept, came)
     layer1 = jnp.where(first, came, kept)
-    early[0:96, :] = layer0[320:416]
-    early[96:112, :] = norms[...]
+    norms = jnp.concatenate([layer0[416:432, 0:128], layer1[416:432, 0:128]], axis=1)
+    for peer in range(16):
+        early[peer, 0:96, :] = layer0[320:416]
+        early[peer, 96:112, :] = norms
     middle[0:320, :] = layer0[0:320]
     middle[320:480, :] = layer1[256:416]
     late[...] = layer1[0:256]
 
 
-def sort_weights(place, mine, received, norms):
+def sort_weights(place, mine, received):
     return call(
         sort_body,
         place,
         (1,),
-        [whole(mine), whole(received), whole(norms)],
-        [whole_out((depth, 256), BF) for depth in (112, 480, 256)],
+        [whole(mine), whole(received)],
+        [whole_out(shape, BF) for shape in ((16, 112, 256), (480, 256), (256, 256))],
     )
 
 
@@ -166,9 +174,8 @@
     return lax.ppermute(value, "section", [(0, 1), (1, 0)])
 
 
-def gather_now(value):
-    copies = jnp.broadcast_to(value, (16,) + value.shape)
-    return lax.all_to_all(copies, "shard", 0, 0, tiled=True)
+def to_owners(pack):
+    return lax.all_to_all(pack, "shard", 0, 0, tiled=True)
 
 
 def after(value, *others):
@@ -473,8 +480,8 @@
 def mlp_back(place, grad, active, slope, mlp_in, weights, heads=None):
     ins = [
         whole(grad),
-        (active, (TOKENS, 256), lambda b, _: (0, b)),
-        (slope, (TOKENS, 256), lambda b, _: (0, b)),
+        (in_hbm(active), (TOKENS, 256), lambda b, _: (0, b)),
+        (in_hbm(slope), (TOKENS, 256), lambda b, _: (0, b)),
         whole(mlp_in),
         (weights, (16, 32, 256), lambda b, _: (0, b, 0)),
         (weights, (4, 128, 256), lambda b, _: (b, 1, 0)),
@@ -537,7 +544,7 @@
         (MICRO,),
         [lanes(piece) for piece in came]
         + [lanes(piece) for piece in places]
-        + [by_micro(kept), by_micro(heads_out), by_micro(log_total)],
+        + [by_micro(in_hbm(array)) for array in (kept, heads_out, log_total)],
         [lanes_out((192,), BF) for _ in SHIFTS],
         [
             pltpu.VMEM((4, 1, BLOCK), jnp.int32),
@@ -620,7 +627,7 @@
     )
 
 
-def mixed_back_body(place, *refs):
+def mixed_back_body(with_heads, place, *refs):
     came = refs[0:4]
     wq, wk, wv, norms, turns, states, mlp_grad = refs[4:11]
     out, mixed_ref, sums = refs[11:14]
@@ -637,6 +644,8 @@
                 ).astype(BF)
                 block = jnp.concatenate([turned, block[16:]], axis=0)
             mixed_ref[part, pl.ds(at, HEAD), :] = block
+        if with_heads:
+            refs[14][pl.ds(at, HEAD), :] = came[step][192:256]
     attn_grad = jnp.zeros((BLOCK, D), F32)
     for part, weight in enumerate((wq, wk, wv)):
         attn_grad = attn_grad + dims(mixed_ref[part], weight[...].reshape(D, 256), 0, 1)
@@ -655,11 +664,12 @@
 
 
 def mixed_back(place, came, weights, norms, turns, states, mlp_grad):
-    ins = [(piece, (192, BLOCK), lambda m, _: (0, m)) for piece in came]
+    with_heads = came[0].shape[0] == 256
+    ins = [lanes(piece) for piece in came]
     ins += qkv_rows(weights)
     ins += [whole(norms), lanes(turns), rows(states), rows(mlp_grad)]
     return call(
-        mixed_back_body,
+        functools.partial(mixed_back_body, with_heads),
         place,
         (MICRO,),
         ins,
@@ -667,7 +677,8 @@
             rows_out(D, F32),
             lanes_out((3, 256), BF),
             whole_out((8, D), F32),
-        ],
+        ]
+        + [lanes_out((256,), BF)] * with_heads,
         flops=1_500_000_000,
         moved=6_000_000,
     )
@@ -732,8 +743,7 @@
 
 
 def scatter_sum(pack):
-    got = lax.all_to_all(pack, "shard", 0, 0, tiled=True)
-    return jnp.sum(got.astype(F32), axis=0).astype(BF)
+    return jnp.sum(to_owners(pack).astype(F32), axis=0).astype(BF)
 
 
 def choose_body(place, *refs):
@@ -823,22 +833,19 @@
     first = core == 0
     place = jnp.stack([chip_z, core, shard // 4, shard % 4]).astype(jnp.int32)
 
+    own_norms = jnp.concatenate([norm_gain[0], norm_bias[0]], axis=0).reshape(1, 128)
     mine, other = pack_weights(
-        place, qkv_weight[0], proj_weight[0], up_weight[0], down_weight[0]
-    )
-    own_norms = jnp.concatenate([norm_gain[0], norm_bias[0]], axis=0).reshape(1, 128)
-    other_norms = swap_core(jnp.broadcast_to(own_norms, (16, 128)))[0:1]
-    both_norms = jnp.where(
-        first,
-        jnp.concatenate([own_norms, other_norms], axis=1),
-        jnp.concatenate([other_norms, own_norms], axis=1),
-    )
-    early, middle, late = sort_weights(
-        place, mine, swap_core(other), jnp.broadcast_to(both_norms, (16, 256))
-    )
+        place,
+        qkv_weight[0],
+        proj_weight[0],
+        up_weight[0],
+        down_weight[0],
+        jnp.broadcast_to(own_norms, (16, 128)),
+    )
+    early, middle, late = sort_weights(place, mine, swap_core(other))
     places_row = positions.reshape(1, TOKENS)
     gathered, places = lax.optimization_barrier(
-        (gather_now(early), regroup([places_row] * 4))
+        (to_owners(early), regroup([places_row] * 4))
     )
     middle_all = lax.all_gather(middle, "shard")
     late_all = lax.all_gather(late, "shard")
@@ -897,11 +904,11 @@
             sent = attend_back(place, came, places, kept, heads_out, log_total)
             sum_a = scatter_sum(pack)
             came = regroup(sent)
-        through, mixed, norm_sums = mixed_back(
+        through, mixed, norm_sums, *heads_of = mixed_back(
             place, came, qkv_of[layer], norms[layer], turns, states, mlp_grad
         )
         if layer == 1:
-            pack = weight_back(place, attn_in, mixed, norm_sums, (pack, heads, grad))
+            pack = weight_back(place, attn_in, mixed, norm_sums, (pack, *heads_of, grad))
             total = lax.psum_scatter(pack, "shard", scatter_dimension=0, tiled=False)
             through = after(through, pack)
         else:

time: 303 us -> 297 us (0.980)
  local copies, waits for them, and re-layouts: 33.2 us -> 24.9 us
  waiting for transfers between devices: 77 us -> 69.9 us
  starting transfers between devices: 69.6 us -> 74.8 us
  Pallas kernels: 99.2 us -> 103 us
    ppermute x30, waiting for transfers between devices: 42.5 us -> 33.7 us  [shift_z(): return lax.ppermute(value, 'seq', [(z, (z + step) % 4) for z in range(4)])]
    unnamed x98 -> x94, local copies, waits for them, and re-layouts: 31.2 us -> 24 us
    pallas_call x22, Pallas kernels: 99.2 us -> 103 us  [call(): pl.pallas_call(body, out_shape=[(pltpu.HBM if out[4:] else struct)(out[0]...]
    all_to_all x3, starting transfers between devices: 17 us -> 20 us  [to_owners(): return lax.all_to_all(pack, 'shard', 0, 0, tiled=True)]
    ppermute x7 -> x6, waiting for transfers between devices: 8.1 us -> 7.79 us  [swap_core(): return lax.ppermute(value, 'section', [(0, 1), (1, 0)])]
    ppermute x7 -> x6, starting transfers between devices: 11.7 us -> 11.7 us  [swap_core(): return lax.ppermute(value, 'section', [(0, 1), (1, 0)])]
  transfers between devices with their start and end apart: 43 -> 42, of which waited for: 19 -> 20; matrix products, arithmetic and copies ran while one was open for 3% -> 3% of each run, Pallas kernels for 29% -> 31%
where the time goes in v1:
time: 297 us; the launch traced here: 295 us
  Pallas kernels  103 us (35%)
  starting transfers between devices  74.8 us (25%)
  waiting for transfers between devices  69.9 us (24%)
  local copies, waits for them, and re-layouts  24.9 us (8%)
  between operations  14.3 us (5%)
  other arithmetic  8.62 us (3%)
    pallas_call x22, Pallas kernels, call(): pl.pallas_call(body, out_shape=[(pltpu.HBM if out[4:] else struct)(out[0]...  103 us
    ppermute x30, starting transfers between devices, shift_z(): return lax.ppermute(value, 'seq', [(z, (z + step) % 4) for z in range(4)])  42.9 us
    ppermute x30, waiting for transfers between devices, shift_z(): return lax.ppermute(value, 'seq', [(z, (z + step) % 4) for z in range(4)])  33.7 us
    unnamed x94, local copies, waits for them, and re-layouts  24 us
    all_to_all x3, waiting for transfers between devices, to_owners(): return lax.all_to_all(pack, 'shard', 0, 0, tiled=True)  21.5 us
    all_to_all x3, starting transfers between devices, to_owners(): return lax.all_to_all(pack, 'shard', 0, 0, tiled=True)  20 us
    ppermute x6, starting transfers between devices, swap_core(): return lax.ppermute(value, 'section', [(0, 1), (1, 0)])  11.7 us
    ppermute x6, waiting for transfers between devices, swap_core(): return lax.ppermute(value, 'section', [(0, 1), (1, 0)])  7.79 us
  transfers between devices with their start and end apart: 42, of which 20 were waited for; matrix products, arithmetic and copies ran while one was open for 3% of the time, Pallas kernels for 31%

profile of v1, /device:TPU:1, one launch (start us, length us, event | category | flops | bytes accessed | tf_op | source)
XLA Modules:
  0.0 295.4 jit_solution(16784638360323868577)
XLA Ops:
  12.2 1.5 collective-permute-start
  14.8 1.7 shard_map.153
  16.5 7.0 %all-to-all-start = ((bf16[16,112,256]{2,1,0:T(8,128)(2,1)}), bf16[16,112,256]{2,1,0:T(8,128)(2,1)S(1)}, u32[]{:S(2)}, u32[]{:S(2)}) async-start(bf16[16,112,256]{2,1,0:T(8,128)(2,1)} %get-tuple-element.88), calls=%async_computation | async-start | bytes 1835008 | tf_op jit(solution)/shard_map/all_to_all | solution.py:178
  23.6 1.7 collective-permute-start.1
  25.3 3.3 %collective-permute-start.2 = (s32[1,768]{1,0:T(1,128)S(1)}, s32[1,768]{1,0:T(1,128)S(1)}, u32[]{:S(2)}, u32[]{:S(2)}) collective-permute-start(s32[1,768]{1,0:T(1,128)S(1)} %bitcast.61), channel_id=1, source_target_pairs={{0,32},{16,48},{32,0},{48,16},{1,33},{17,49},{33,1},{49,17},{2,34}... | collective-permute-start | bytes 9224 | tf_op jit(solution)/shard_map/ppermute | solution.py:170
  29.7 1.6 collective-permute-done.3.refs_7_
  31.3 6.4 %all-to-all-done.refs_1_.refs_2_.refs_3_.refs_4_.refs_5_.refs_6_ = bf16[16,112,256]{2,1,0:T(8,128)(2,1)S(1)} async-done(((bf16[16,112,256]{2,1,0:T(8,128)(2,1)}), bf16[16,112,256]{2,1,0:T(8,128)(2,1)S(1)}, u32[]{:S(2)}, u32[]{:S(2)}) %all-to-all-start) | async-done | bytes 917536 | tf_op jit(solution)/shard_map/all_to_all | solution.py:178
  38.0 3.8 %shard_map.154 = (bf16[192,768]{1,0:T(8,128)(2,1)S(1)}, bf16[192,768]{1,0:T(8,128)(2,1)}, bf16[192,768]{1,0:T(8,128)(2,1)S(1)}, bf16[192,768]{1,0:T(8,128)(2,1)S...) custom-call(s32[4]{0:T(128)S(1)} %pad_add_fusion.place, bf16[768,512]{1,0:T(8,128)(2,1)S(1)} %bitcast.56, ...), custom_call_target="tpu_custom_call" | custom-call | flops 1200000000 | bytes 6000000 | tf_op jit(solution)/shard_map/pallas_call | solution.py:42
  42.5 2.0 collective-permute-start.4
  44.5 3.7 %collective-permute-start.5 = (bf16[192,768]{1,0:T(8,128)(2,1)S(1)}, bf16[192,768]{1,0:T(8,128)(2,1)S(1)}, u32[]{:S(2)}, u32[]{:S(2)}) collective-permute-start(bf16[192,768]{1,0:T(8,128)(2,1)S(1)} %get-tuple-element.92), channel_id=1, source_target_pairs={{0,32},{16,48},{32,0},{48,16},{1,33},{17,49},{33,1},{49,17},{2,34}... | collective-permute-start | bytes 884744 | tf_op jit(solution)/shard_map/ppermute | solution.py:170
  48.6 2.7 collective-permute-done.4.refs_1_
  51.3 5.3 %collective-permute-done.5.refs_2_ = bf16[192,768]{1,0:T(8,128)(2,1)S(1)} collective-permute-done((bf16[192,768]{1,0:T(8,128)(2,1)S(1)}, bf16[192,768]{1,0:T(8,128)(2,1)S(1)}, u32[]{:S(2)}, u32[]{:S(2)}) %collective-permute-start.5) | collective-permute-done | bytes 294944 | tf_op jit(solution)/shard_map/ppermute | solution.py:170
  57.6 7.1 %shard_map.155 = (bf16[64,768]{1,0:T(8,128)(2,1)S(1)}, bf16[64,768]{1,0:T(8,128)(2,1)S(1)}, bf16[64,768]{1,0:T(8,128)(2,1)S(1)}, bf16[64,768]{1,0:T(8,128)(2,1)S...) custom-call(s32[4]{0:T(128)S(1)} %pad_add_fusion.place, ...), custom_call_target="tpu_custom_call" | custom-call | flops 8000000000 | bytes 4000000 | tf_op jit(solution)/shard_map/pallas_call | solution.py:42
  64.7 3.9 %collective-permute-start.7 = (bf16[64,768]{1,0:T(8,128)(2,1)S(1)}, bf16[64,768]{1,0:T(8,128)(2,1)S(1)}, u32[]{:S(2)}, u32[]{:S(2)}) collective-permute-start(bf16[64,768]{1,0:T(8,128)(2,1)S(1)} %get-tuple-element.99), channel_id=1, source_target_pairs={{0,16},{16,32},{32,48},{48,0},{1,17},{17,33},{33,49},{49,1},{2,18}... | collective-permute-start | bytes 294920 | tf_op jit(solution)/shard_map/ppermute | solution.py:170
  68.6 2.4 collective-permute-start.9
  71.0 2.0 all-gather.5.cloned.1.call-done
  73.0 2.1 copy-done
  76.3 6.6 %shard_map.156 = (f32[768,512]{1,0:T(8,128)S(1)}, bf16[768,1024]{1,0:T(8,128)(2,1)}, f32[768,1024]{1,0:T(8,128)}) custom-call(s32[4]{0:T(128)S(1)} %pad_add_fusion.place, bf16[768,512]{1,0:T(8,128)(2,1)S(1)} %copy-done.43, bf16[16,480,256]{2,1,0:T(8,128)(2,1)S(1)} %bitcast.38, bf16[16,480,256]{2,1,0:T(8,128)(2,1)S(1)} %bitcast.39), custom_call_target="tpu_custom_call" | custom-call | flops 6000000000 | bytes 12000000 | tf_op jit(solution)/shard_map/pallas_call | solution.py:42
  82.9 2.8 shard_map.157
  85.7 2.1 collective-permute-start.10
  87.8 3.3 %collective-permute-done.10.refs_2_ = f32[768,512]{1,0:T(8,128)} collective-permute-done((f32[768,512]{1,0:T(8,128)}, f32[768,512]{1,0:T(8,128)}, u32[]{:S(2)}, u32[]{:S(2)}) %collective-permute-start.10) | collective-permute-done | bytes 1572896 | tf_op jit(solution)/shard_map/ppermute | solution.py:174
  91.1 2.1 copy-done.2
  93.3 5.8 %shard_map.158 = (bf16[256,768]{1,0:T(8,128)(2,1)S(1)}, bf16[256,768]{1,0:T(8,128)(2,1)S(1)}, bf16[256,768]{1,0:T(8,128)(2,1)S(1)}, bf16[256,768]{1,0:T(8,128)(2...) custom-call(s32[4]{0:T(128)S(1)} %pad_add_fusion.place, ...), custom_call_target="tpu_custom_call" | custom-call | flops 1200000000 | bytes 6000000 | tf_op jit(solution)/shard_map/pallas_call | solution.py:42
  99.8 2.0 collective-permute-start.12
  102.9 7.9 %collective-permute-done.11.refs_1_ = bf16[256,768]{1,0:T(8,128)(2,1)S(1)} collective-permute-done((bf16[256,768]{1,0:T(8,128)(2,1)S(1)}, bf16[256,768]{1,0:T(8,128)(2,1)S(1)}, u32[]{:S(2)}, u32[]{:S(2)}) %collective-permute-start.11) | collective-permute-done | bytes 393248 | tf_op jit(solution)/shard_map/ppermute | solution.py:170
  110.7 8.3 %collective-permute-done.12.refs_2_ = bf16[256,768]{1,0:T(8,128)(2,1)S(1)} collective-permute-done((bf16[256,768]{1,0:T(8,128)(2,1)S(1)}, bf16[256,768]{1,0:T(8,128)(2,1)S(1)}, u32[]{:S(2)}, u32[]{:S(2)}) %collective-permute-start.12) | collective-permute-done | bytes 393248 | tf_op jit(solution)/shard_map/ppermute | solution.py:170
  119.5 13.9 %shard_map.159 = (bf16[256,768]{1,0:T(8,128)(2,1)S(1)}, bf16[256,768]{1,0:T(8,128)(2,1)}, bf16[256,768]{1,0:T(8,128)(2,1)}, bf16[256,768]{1,0:T(8,128)(2,1)}) custom-call(s32[4]{0:T(128)S(1)} %pad_add_fusion.place, bf16[256,768]{1,0:T(8,128)(2,1)S(1)} %get-tuple-element.107.refs_0_, bf16[256,768]{1,0:T(8,128)(2,1)S(1)} %collective-permute-done.11.refs_1_, ...), custom_call_target="tpu_custom_call" | custom-call | flops 17999998976 | bytes 5000000 | tf_op jit(solution)/shard_map/pallas_call | solution.py:42
  133.4 2.0 collective-permute-start.14
  135.5 2.5 collective-permute-start.15
  138.0 1.6 copy-done.25
  140.7 6.5 %shard_map.160 = (f32[768,512]{1,0:T(8,128)S(1)}, bf16[768,1024]{1,0:T(8,128)(2,1)}, f32[768,1024]{1,0:T(8,128)}) custom-call(s32[4]{0:T(128)S(1)} %pad_add_fusion.place, bf16[768,512]{1,0:T(8,128)(2,1)S(1)} %copy-done.27, bf16[16,256,256]{2,1,0:T(8,128)(2,1)S(1)} %bitcast.66, bf16[16,256,256]{2,1,0:T(8,128)(2,1)S(1)} %bitcast.67), custom_call_target="tpu_custom_call" | custom-call | flops 6000000000 | bytes 12000000 | tf_op jit(solution)/shard_map/pallas_call | solution.py:42
  148.4 8.9 %shard_map.162 = (f32[768,512]{1,0:T(8,128)S(1)}, bf16[16,256,256]{2,1,0:T(8,128)(2,1)S(1)}) custom-call(s32[4]{0:T(128)S(1)} %pad_add_fusion.place, bf16[768,512]{1,0:T(8,128)(2,1)S(1)} %bitcast.53, bf16[768,1024]{1,0:T(8,128)(2,1)} %get-tuple-element.120.active, f32[768,1024]{1,0:T(8,128)} %get-tuple-element.121.slope, bf16[768,512]{1,0:T(8,128)(2,1)S(1)} %copy-done.28, ...), custom_call_target="tpu_custom_call" | custom-call | flops 8000000000 | bytes 14000000 | tf_op jit(solution)/shard_map/pallas_call | solution.py:42
  157.4 4.1 %shard_map.163 = (f32[768,512]{1,0:T(8,128)S(1)}, bf16[3,256,768]{2,1,0:T(8,128)(2,1)S(1)}, f32[8,512]{1,0:T(8,128)S(1)}, bf16[256,768]{1,0:T(8,128)(2,1)S(1)}) custom-call(s32[4]{0:T(128)S(1)} %pad_add_fusion.place, bf16[256,768]{1,0:T(8,128)(2,1)S(1)} %get-tuple-element.111.refs_0_, bf16[256,768]{1,0:T(8,128)(2,1)S(1)} %collective-permute-done.14.refs_1_, ...), custom_call_target="tpu_custom_call" | custom-call | flops 1500000000 | bytes 6000000 | tf_op jit(solution)/shard_map/pallas_call | solution.py:42
  162.7 1.6 shard_map.164
  164.3 1.8 copy-done.6
  166.2 1.5 collective-permute-start.18
  167.7 3.2 %collective-permute-done.18.came = f32[768,512]{1,0:T(8,128)S(1)} collective-permute-done((f32[768,512]{1,0:T(8,128)}, f32[768,512]{1,0:T(8,128)S(1)}, u32[]{:S(2)}, u32[]{:S(2)}) %collective-permute-start.18) | collective-permute-done | bytes 1572896 | tf_op jit(solution)/shard_map/ppermute | solution.py:174
  173.5 1.7 shard_map.165.grad
  175.3 2.4 shard_map.166
  179.4 1.9 collective-permute-start.21
  181.4 9.1 %shard_map.167 = (f32[768,512]{1,0:T(8,128)S(1)}, bf16[16,320,256]{2,1,0:T(8,128)(2,1)S(1)}) custom-call(s32[4]{0:T(128)S(1)} %pad_add_fusion.place, bf16[768,512]{1,0:T(8,128)(2,1)S(1)} %shard_map.165.grad, bf16[768,1024]{1,0:T(8,128)(2,1)} %get-tuple-element.135.active, f32[768,1024]{1,0:T(8,128)} %get-tuple-element.136.slope, ...), custom_call_target="tpu_custom_call" | custom-call | flops 8000000000 | bytes 14000000 | tf_op jit(solution)/shard_map/pallas_call | solution.py:42
  193.1 6.3 %all-to-all-start.1 = ((bf16[16,320,256]{2,1,0:T(8,128)(2,1)}), bf16[16,320,256]{2,1,0:T(8,128)(2,1)}, u32[]{:S(2)}, u32[]{:S(2)}) async-start(bf16[16,320,256]{2,1,0:T(8,128)(2,1)} %copy-done.12), calls=%async_computation.1 | async-start | bytes 5242880 | tf_op jit(solution)/shard_map/all_to_all | solution.py:178
  199.5 10.7 %shard_map.168 = (bf16[192,768]{1,0:T(8,128)(2,1)S(1)}, bf16[192,768]{1,0:T(8,128)(2,1)S(1)}, bf16[192,768]{1,0:T(8,128)(2,1)S(1)}, bf16[192,768]{1,0:T(8,128)(2,1)S(1)}) custom-call(s32[4]{0:T(128)S(1)} %pad_add_fusion.place, bf16[64,768]{1,0:T(8,128)(2,1)S(1)} %get-tuple-element.139.refs_0_, bf16[64,768]{1,0:T(8,128)(2,1)S(1)} %collective-permute-done.19.refs_1_, ...), custom_call_target="tpu_custom_call" | custom-call | flops 16000000000 | bytes 5000000 | tf_op jit(solution)/shard_map/pallas_call | solution.py:42
  210.2 2.0 collective-permute-start.23
  213.5 3.6 %shard_map.161 = (f32[768,512]{1,0:T(8,128)}, bf16[256,768]{1,0:T(8,128)(2,1)}) custom-call(s32[4]{0:T(128)S(1)} %pad_add_fusion.place, bf16[256,768]{1,0:T(8,128)(2,1)S(1)} %copy-done.16, bf16[256,768]{1,0:T(8,128)(2,1)S(1)} %copy-done.18, bf16[256,768]{1,0:T(8,128)(2,1)} %collective-permute-done.15.refs_2_, ...), custom_call_target="tpu_custom_call" | custom-call | flops 800000000 | bytes 4000000 | tf_op jit(solution)/shard_map/pallas_call | solution.py:42
  217.0 2.4 collective-permute-start.17
  219.6 4.6 %collective-permute-done.23.refs_2_ = bf16[192,768]{1,0:T(8,128)(2,1)S(1)} collective-permute-done((bf16[192,768]{1,0:T(8,128)(2,1)S(1)}, bf16[192,768]{1,0:T(8,128)(2,1)S(1)}, u32[]{:S(2)}, u32[]{:S(2)}) %collective-permute-start.23) | collective-permute-done | bytes 294944 | tf_op jit(solution)/shard_map/ppermute | solution.py:170
  224.2 2.0 collective-permute-done.24.refs_3_
  226.2 3.6 %shard_map.169 = (f32[768,512]{1,0:T(8,128)}, bf16[3,256,768]{2,1,0:T(8,128)(2,1)S(1)}, f32[8,512]{1,0:T(8,128)S(1)}) custom-call(s32[4]{0:T(128)S(1)} %pad_add_fusion.place, bf16[192,768]{1,0:T(8,128)(2,1)S(1)} %get-tuple-element.146.refs_0_, bf16[192,768]{1,0:T(8,128)(2,1)S(1)} %collective-permute-done.22.refs_1_, ...), custom_call_target="tpu_custom_call" | custom-call | flops 1500000000 | bytes 6000000 | tf_op jit(solution)/shard_map/pallas_call | solution.py:42
  229.8 1.6 collective-permute-start.25
  231.4 2.3 shard_map.171
  233.7 4.2 %all-to-all-done.1 = bf16[16,320,256]{2,1,0:T(8,128)(2,1)} async-done(((bf16[16,320,256]{2,1,0:T(8,128)(2,1)}), bf16[16,320,256]{2,1,0:T(8,128)(2,1)}, u32[]{:S(2)}, u32[]{:S(2)}) %all-to-all-start.1) | async-done | bytes 2621472 | tf_op jit(solution)/shard_map/all_to_all | solution.py:178
  237.9 2.1 reduce_sum.24.refs_4_
  240.1 6.8 %all-to-all-start.2 = ((bf16[16,112,256]{2,1,0:T(8,128)(2,1)}), bf16[16,112,256]{2,1,0:T(8,128)(2,1)}, u32[]{:S(2)}, u32[]{:S(2)}) async-start(bf16[16,112,256]{2,1,0:T(8,128)(2,1)} %shard_map.171), calls=%async_computation.2 | async-start | bytes 1835008 | tf_op jit(solution)/shard_map/all_to_all | solution.py:178
  248.1 1.6 collective-permute-start.31
  249.7 10.9 %all-to-all-done.2 = bf16[16,112,256]{2,1,0:T(8,128)(2,1)} async-done(((bf16[16,112,256]{2,1,0:T(8,128)(2,1)}), bf16[16,112,256]{2,1,0:T(8,128)(2,1)}, u32[]{:S(2)}, u32[]{:S(2)}) %all-to-all-start.2) | async-done | bytes 917536 | tf_op jit(solution)/shard_map/all_to_all | solution.py:178
  262.7 2.1 collective-permute-start.34
  264.8 4.8 %reduce-scatter.4.cloned.1.call-done = bf16[1,432,256]{2,1,0:T(8,128)(2,1)} async-done(((bf16[16,432,256]{2,1,0:T(8,128)(2,1)}), bf16[1,432,256]{2,1,0:T(8,128)(2,1)}) %reduce-scatter.4.cloned.1.call-update) | async-done | bytes 221200
  270.7 1.7 collective-permute-start.27
  273.1 1.6 collective-permute-start.28
  274.7 3.2 %fusion = bf16[768,512]{1,0:T(8,128)(2,1)} fusion(bf16[768,512]{1,0:T(8,128)(2,1)S(1)} %copy-done.11, f32[768,512]{1,0:T(8,128)} %get-tuple-element.119, f32[768,512]{1,0:T(8,128)} %collective-permute-done.17, pred[]{:T(512)S(6)} %eq.5), kind=kLoop, calls=%fused_computation.1 | loop fusion | flops 1966080 | bytes 4718593 | tf_op jit(solution)/shard_map/jit(_where)/select_n | solution.py:890
  277.9 3.7 %shard_map.170 = bf16[768,512]{1,0:T(8,128)(2,1)S(1)} custom-call(s32[4]{0:T(128)S(1)} %pad_add_fusion.place, bf16[768,512]{1,0:T(8,128)(2,1)S(1)} %bitcast.59, bf16[768,512]{1,0:T(8,128)(2,1)S(1)} %shard_map.165.grad, f32[768,512]{1,0:T(8,128)} %get-tuple-element.151.own, f32[768,512]{1,0:T(8,128)} %collective-permute-done.25.came), custom_call_target="tpu_custom_call" | custom-call | flops 100000000 | bytes 5000000 | tf_op jit(solution)/shard_map/pallas_call | solution.py:42
  283.0 2.7 collective-permute-start.35
  286.8 1.5 shard_map.173
  (159 shorter events, 33.0 us)
Async XLA Ops:
  7.2 65.9 %all-gather.5.cloned.1.call-start = ((), (), s32[]{:S(2)}) async-start(), calls=%async_computation.4 | async-start | bytes 4177920 | tf_op jit(solution)/shard_map/all_gather | solution.py:850
  12.2 2.6 collective-permute-start
  16.5 7.1 %copy-start.24 = (s32[3,1,256]{2,1,0:T(1,128)S(1)}, s32[3,1,256]{2,1,0:T(1,128)}, u32[]{:S(2)}) copy-start(s32[3,1,256]{2,1,0:T(1,128)} %param.10) | copy-start | bytes 9220
  16.5 21.5 %copy-start.8 = (bf16[3,1,256,512]{3,2,1,0:T(8,128)(2,1)S(1)}, bf16[3,1,256,512]{3,2,1,0:T(8,128)(2,1)}, u32[]{:S(2)}) copy-start(bf16[3,1,256,512]{3,2,1,0:T(8,128)(2,1)} %param.9) | copy-start | bytes 2359300
  16.5 21.2 %all-to-all-start = ((bf16[16,112,256]{2,1,0:T(8,128)(2,1)}), bf16[16,112,256]{2,1,0:T(8,128)(2,1)S(1)}, u32[]{:S(2)}, u32[]{:S(2)}) async-start(bf16[16,112,256]{2,1,0:T(8,128)(2,1)} %get-tuple-element.88), calls=%async_computation | async-start | bytes 1835008 | tf_op jit(solution)/shard_map/all_to_all | solution.py:178
  23.5 114.5 %all-gather.7.cloned.1.call-start = ((), (), s32[]{:S(2)}) async-start(), calls=%async_computation.5 | async-start | bytes 2228224 | tf_op jit(solution)/shard_map/all_gather | solution.py:851
  23.6 6.0 %collective-permute-start.1 = (s32[1,768]{1,0:T(1,128)S(1)}, s32[1,768]{1,0:T(1,128)S(1)}, u32[]{:S(2)}, u32[]{:S(2)}) collective-permute-start(s32[1,768]{1,0:T(1,128)S(1)} %bitcast.60), channel_id=1, source_target_pairs={{0,16},{16,32},{32,48},{48,0},{1,17},{17,33},{33,49},{49,1},{2,18}... | collective-permute-start | bytes 9224 | tf_op jit(solution)/shard_map/ppermute | solution.py:170
  25.3 4.4 %collective-permute-start.2 = (s32[1,768]{1,0:T(1,128)S(1)}, s32[1,768]{1,0:T(1,128)S(1)}, u32[]{:S(2)}, u32[]{:S(2)}) collective-permute-start(s32[1,768]{1,0:T(1,128)S(1)} %bitcast.61), channel_id=1, source_target_pairs={{0,32},{16,48},{32,0},{48,16},{1,33},{17,49},{33,1},{49,17},{2,34}... | collective-permute-start | bytes 9224 | tf_op jit(solution)/shard_map/ppermute | solution.py:170
  28.6 2.7 collective-permute-start.3
  31.3 88.2 %copy-start.40 = (s32[1,768]{1,0:T(1,128)}, s32[1,768]{1,0:T(1,128)S(1)}, u32[]{:S(2)}) copy-start(s32[1,768]{1,0:T(1,128)S(1)} %collective-permute-done.3.refs_7_) | copy-start | bytes 9220
  42.5 8.8 %collective-permute-start.4 = (bf16[192,768]{1,0:T(8,128)(2,1)}, bf16[192,768]{1,0:T(8,128)(2,1)S(1)}, u32[]{:S(2)}, u32[]{:S(2)}) collective-permute-start(bf16[192,768]{1,0:T(8,128)(2,1)} %get-tuple-element.91), channel_id=1, source_target_pairs={{0,16},{16,32},{32,48},{48,0},{1,17},{17,33},{33,49},{49,1},{2,18}... | collective-permute-start | bytes 884744 | tf_op jit(solution)/shard_map/ppermute | solution.py:170
  44.5 12.1 %collective-permute-start.5 = (bf16[192,768]{1,0:T(8,128)(2,1)S(1)}, bf16[192,768]{1,0:T(8,128)(2,1)S(1)}, u32[]{:S(2)}, u32[]{:S(2)}) collective-permute-start(bf16[192,768]{1,0:T(8,128)(2,1)S(1)} %get-tuple-element.92), channel_id=1, source_target_pairs={{0,32},{16,48},{32,0},{48,16},{1,33},{17,49},{33,1},{49,17},{2,34}... | collective-permute-start | bytes 884744 | tf_op jit(solution)/shard_map/ppermute | solution.py:170
  48.2 8.4 %collective-permute-start.6 = (bf16[192,768]{1,0:T(8,128)(2,1)S(1)}, bf16[192,768]{1,0:T(8,128)(2,1)S(1)}, u32[]{:S(2)}, u32[]{:S(2)}) collective-permute-start(bf16[192,768]{1,0:T(8,128)(2,1)S(1)} %get-tuple-element.93), channel_id=1, source_target_pairs={{0,48},{16,0},{32,16},{48,32},{1,49},{17,1},{33,17},{49,33},{2,50}... | collective-permute-start | bytes 884744 | tf_op jit(solution)/shard_map/ppermute | solution.py:170
  48.6 221.0 %reduce-scatter.4.cloned.1.call-start = ((), (), s32[]{:S(2)}) async-start(), calls=%async_computation.6 | async-start | bytes 3760128
  64.7 18.2 %collective-permute-start.7 = (bf16[64,768]{1,0:T(8,128)(2,1)S(1)}, bf16[64,768]{1,0:T(8,128)(2,1)S(1)}, u32[]{:S(2)}, u32[]{:S(2)}) collective-permute-start(bf16[64,768]{1,0:T(8,128)(2,1)S(1)} %get-tuple-element.99), channel_id=1, source_target_pairs={{0,16},{16,32},{32,48},{48,0},{1,17},{17,33},{33,49},{49,1},{2,18}... | collective-permute-start | bytes 294920 | tf_op jit(solution)/shard_map/ppermute | solution.py:170
  68.6 14.3 %collective-permute-start.8 = (bf16[64,768]{1,0:T(8,128)(2,1)S(1)}, bf16[64,768]{1,0:T(8,128)(2,1)S(1)}, u32[]{:S(2)}, u32[]{:S(2)}) collective-permute-start(bf16[64,768]{1,0:T(8,128)(2,1)S(1)} %get-tuple-element.100), channel_id=1, source_target_pairs={{0,32},{16,48},{32,0},{48,16},{1,33},{17,49},{33,1},{49,17},{2,34}... | collective-permute-start | bytes 294920 | tf_op jit(solution)/shard_map/ppermute | solution.py:170
  68.6 14.3 %collective-permute-start.9 = (bf16[64,768]{1,0:T(8,128)(2,1)S(1)}, bf16[64,768]{1,0:T(8,128)(2,1)S(1)}, u32[]{:S(2)}, u32[]{:S(2)}) collective-permute-start(bf16[64,768]{1,0:T(8,128)(2,1)S(1)} %get-tuple-element.101), channel_id=1, source_target_pairs={{0,48},{16,0},{32,16},{48,32},{1,49},{17,1},{33,17},{49,33},{2,50}... | collective-permute-start | bytes 294920 | tf_op jit(solution)/shard_map/ppermute | solution.py:170
  76.3 6.6 %copy-start.1 = (bf16[7680,256]{1,0:T(8,128)(2,1)S(1)}, bf16[7680,256]{1,0:T(8,128)(2,1)}, u32[]{:S(2)}) copy-start(bf16[7680,256]{1,0:T(8,128)(2,1)} %all-gather.5.cloned.1.call-done) | copy-start | bytes 11796484
  82.9 8.3 %copy-start.7 = (bf16[3,1,256,512]{3,2,1,0:T(8,128)(2,1)S(1)}, bf16[3,1,256,512]{3,2,1,0:T(8,128)(2,1)}, u32[]{:S(2)}) copy-start(bf16[3,1,256,512]{3,2,1,0:T(8,128)(2,1)} %param.11) | copy-start | bytes 2359300
  85.7 13.4 %copy-start.29 = (bf16[256,768]{1,0:T(8,128)(2,1)}, bf16[256,768]{1,0:T(8,128)(2,1)S(1)}, u32[]{:S(2)}) copy-start(bf16[256,768]{1,0:T(8,128)(2,1)S(1)} %get-tuple-element.137.refs_0_) | copy-start | bytes 1179652
  85.7 5.4 %collective-permute-start.10 = (f32[768,512]{1,0:T(8,128)}, f32[768,512]{1,0:T(8,128)}, u32[]{:S(2)}, u32[]{:S(2)}) collective-permute-start(f32[768,512]{1,0:T(8,128)} %get-tuple-element.105.refs_1_), channel_id=1, source_target_pairs={{0,64},{64,0},{1,65},{65,1},{2,66},{66,2},{3,67},{67,3},{4,68},{68... | collective-permute-start | bytes 4718600 | tf_op jit(solution)/shard_map/ppermute | solution.py:174
  99.1 11.7 %collective-permute-start.11 = (bf16[256,768]{1,0:T(8,128)(2,1)S(1)}, bf16[256,768]{1,0:T(8,128)(2,1)S(1)}, u32[]{:S(2)}, u32[]{:S(2)}) collective-permute-start(bf16[256,768]{1,0:T(8,128)(2,1)S(1)} %get-tuple-element.108), channel_id=1, source_target_pairs={{0,16},{16,32},{32,48},{48,0},{1,17},{17,33},{33,49},{49,1},{2,18}... | collective-permute-start | bytes 1179656 | tf_op jit(solution)/shard_map/ppermute | solution.py:170
  99.8 19.2 %collective-permute-start.12 = (bf16[256,768]{1,0:T(8,128)(2,1)S(1)}, bf16[256,768]{1,0:T(8,128)(2,1)S(1)}, u32[]{:S(2)}, u32[]{:S(2)}) collective-permute-start(bf16[256,768]{1,0:T(8,128)(2,1)S(1)} %get-tuple-element.109), channel_id=1, source_target_pairs={{0,32},{16,48},{32,0},{48,16},{1,33},{17,49},{33,1},{49,17},{2,34}... | collective-permute-start | bytes 1179656 | tf_op jit(solution)/shard_map/ppermute | solution.py:170
  101.8 17.6 %collective-permute-start.13 = (bf16[256,768]{1,0:T(8,128)(2,1)S(1)}, bf16[256,768]{1,0:T(8,128)(2,1)S(1)}, u32[]{:S(2)}, u32[]{:S(2)}) collective-permute-start(bf16[256,768]{1,0:T(8,128)(2,1)S(1)} %get-tuple-element.110), channel_id=1, source_target_pairs={{0,48},{16,0},{32,16},{48,32},{1,49},{17,1},{33,17},{49,33},{2,50}... | collective-permute-start | bytes 1179656 | tf_op jit(solution)/shard_map/ppermute | solution.py:170
  133.4 23.9 %copy-start.15 = (bf16[256,768]{1,0:T(8,128)(2,1)}, bf16[256,768]{1,0:T(8,128)(2,1)S(1)}, u32[]{:S(2)}) copy-start(bf16[256,768]{1,0:T(8,128)(2,1)S(1)} %get-tuple-element.111.refs_0_) | copy-start | bytes 1179652
  133.4 23.9 %collective-permute-start.14 = (bf16[256,768]{1,0:T(8,128)(2,1)}, bf16[256,768]{1,0:T(8,128)(2,1)S(1)}, u32[]{:S(2)}, u32[]{:S(2)}) collective-permute-start(bf16[256,768]{1,0:T(8,128)(2,1)} %get-tuple-element.112), channel_id=1, source_target_pairs={{0,16},{16,32},{32,48},{48,0},{1,17},{17,33},{33,49},{49,1},{2,18}... | collective-permute-start | bytes 1179656 | tf_op jit(solution)/shard_map/ppermute | solution.py:170
  135.5 21.8 %collective-permute-start.15 = (bf16[256,768]{1,0:T(8,128)(2,1)}, bf16[256,768]{1,0:T(8,128)(2,1)}, u32[]{:S(2)}, u32[]{:S(2)}) collective-permute-start(bf16[256,768]{1,0:T(8,128)(2,1)} %get-tuple-element.113), channel_id=1, source_target_pairs={{0,32},{16,48},{32,0},{48,16},{1,33},{17,49},{33,1},{49,17},{2,34}... | collective-permute-start | bytes 1179656 | tf_op jit(solution)/shard_map/ppermute | solution.py:170
  138.0 19.3 %collective-permute-start.16 = (bf16[256,768]{1,0:T(8,128)(2,1)}, bf16[256,768]{1,0:T(8,128)(2,1)}, u32[]{:S(2)}, u32[]{:S(2)}) collective-permute-start(bf16[256,768]{1,0:T(8,128)(2,1)} %get-tuple-element.114), channel_id=1, source_target_pairs={{0,48},{16,0},{32,16},{48,32},{1,49},{17,1},{33,17},{49,33},{2,50}... | collective-permute-start | bytes 1179656 | tf_op jit(solution)/shard_map/ppermute | solution.py:170
  140.7 7.6 %copy-start.26 = (bf16[4096,256]{1,0:T(8,128)(2,1)S(1)}, bf16[4096,256]{1,0:T(8,128)(2,1)}, u32[]{:S(2)}) copy-start(bf16[4096,256]{1,0:T(8,128)(2,1)} %all-gather.7.cloned.1.call-done) | copy-start | bytes 6291460
  140.7 7.6 %copy-start.28 = (bf16[768,512]{1,0:T(8,128)(2,1)S(1)}, bf16[768,512]{1,0:T(8,128)(2,1)}, u32[]{:S(2)}) copy-start(bf16[768,512]{1,0:T(8,128)(2,1)} %get-tuple-element.116.mlp_in) | copy-start | bytes 2359300
  148.4 9.0 %copy-start.3 = (bf16[7680,256]{1,0:T(8,128)(2,1)S(1)}, bf16[7680,256]{1,0:T(8,128)(2,1)}, u32[]{:S(2)}) copy-start(bf16[7680,256]{1,0:T(8,128)(2,1)} %all-gather.5.cloned.1.call-done) | copy-start | bytes 11796484
  148.4 9.0 %copy-start.9 = (bf16[768,512]{1,0:T(8,128)(2,1)S(1)}, bf16[768,512]{1,0:T(8,128)(2,1)}, u32[]{:S(2)}) copy-start(bf16[768,512]{1,0:T(8,128)(2,1)} %get-tuple-element.106.refs_9_.states) | copy-start | bytes 2359300
  157.4 5.4 %copy-start.23 = (bf16[768,512]{1,0:T(8,128)(2,1)S(1)}, bf16[768,512]{1,0:T(8,128)(2,1)}, u32[]{:S(2)}) copy-start(bf16[768,512]{1,0:T(8,128)(2,1)} %get-tuple-element.124.attn_in) | copy-start | bytes 2359300
  166.2 9.1 %copy-start.4 = (bf16[7680,256]{1,0:T(8,128)(2,1)S(1)}, bf16[7680,256]{1,0:T(8,128)(2,1)}, u32[]{:S(2)}) copy-start(bf16[7680,256]{1,0:T(8,128)(2,1)} %all-gather.5.cloned.1.call-done) | copy-start | bytes 11796484
  166.2 4.8 %collective-permute-start.18 = (f32[768,512]{1,0:T(8,128)}, f32[768,512]{1,0:T(8,128)S(1)}, u32[]{:S(2)}, u32[]{:S(2)}) collective-permute-start(f32[768,512]{1,0:T(8,128)} %copy-done.21), channel_id=1, source_target_pairs={{0,64},{64,0},{1,65},{65,1},{2,66},{66,2},{3,67},{67,3},{4,68},{68... | collective-permute-start | bytes 4718600 | tf_op jit(solution)/shard_map/ppermute | solution.py:174
  175.3 6.1 %copy-start.30 = (bf16[256,768]{1,0:T(8,128)(2,1)S(1)}, bf16[256,768]{1,0:T(8,128)(2,1)}, u32[]{:S(2)}) copy-start(bf16[256,768]{1,0:T(8,128)(2,1)} %copy-done.29) | copy-start | bytes 1179652
  175.3 6.1 %copy-start.44 = (bf16[768,512]{1,0:T(8,128)(2,1)S(1)}, bf16[768,512]{1,0:T(8,128)(2,1)}, u32[]{:S(2)}) copy-start(bf16[768,512]{1,0:T(8,128)(2,1)} %get-tuple-element.103.mlp_in) | copy-start | bytes 2359300
  177.7 21.7 %collective-permute-start.19 = (bf16[64,768]{1,0:T(8,128)(2,1)}, bf16[64,768]{1,0:T(8,128)(2,1)S(1)}, u32[]{:S(2)}, u32[]{:S(2)}) collective-permute-start(bf16[64,768]{1,0:T(8,128)(2,1)} %get-tuple-element.131), channel_id=1, source_target_pairs={{0,16},{16,32},{32,48},{48,0},{1,17},{17,33},{33,49},{49,1},{2,18}... | collective-permute-start | bytes 294920 | tf_op jit(solution)/shard_map/ppermute | solution.py:170
  179.0 20.4 %collective-permute-start.20 = (bf16[64,768]{1,0:T(8,128)(2,1)S(1)}, bf16[64,768]{1,0:T(8,128)(2,1)S(1)}, u32[]{:S(2)}, u32[]{:S(2)}) collective-permute-start(bf16[64,768]{1,0:T(8,128)(2,1)S(1)} %get-tuple-element.132), channel_id=1, source_target_pairs={{0,32},{16,48},{32,0},{48,16},{1,33},{17,49},{33,1},{49,17},{2,34}... | collective-permute-start | bytes 294920 | tf_op jit(solution)/shard_map/ppermute | solution.py:170
  179.4 20.0 %collective-permute-start.21 = (bf16[64,768]{1,0:T(8,128)(2,1)S(1)}, bf16[64,768]{1,0:T(8,128)(2,1)S(1)}, u32[]{:S(2)}, u32[]{:S(2)}) collective-permute-start(bf16[64,768]{1,0:T(8,128)(2,1)S(1)} %get-tuple-element.133), channel_id=1, source_target_pairs={{0,48},{16,0},{32,16},{48,32},{1,49},{17,1},{33,17},{49,33},{2,50}... | collective-permute-start | bytes 294920 | tf_op jit(solution)/shard_map/ppermute | solution.py:170
  193.1 6.3 %copy-start.41 = (s32[1,768]{1,0:T(1,128)S(1)}, s32[1,768]{1,0:T(1,128)}, u32[]{:S(2)}) copy-start(s32[1,768]{1,0:T(1,128)} %copy-done.40) | copy-start | bytes 9220
  193.1 44.8 %all-to-all-start.1 = ((bf16[16,320,256]{2,1,0:T(8,128)(2,1)}), bf16[16,320,256]{2,1,0:T(8,128)(2,1)}, u32[]{:S(2)}, u32[]{:S(2)}) async-start(bf16[16,320,256]{2,1,0:T(8,128)(2,1)} %copy-done.12), calls=%async_computation.1 | async-start | bytes 5242880 | tf_op jit(solution)/shard_map/all_to_all | solution.py:178
  199.4 14.0 %copy-start.5 = (bf16[7680,256]{1,0:T(8,128)(2,1)S(1)}, bf16[7680,256]{1,0:T(8,128)(2,1)}, u32[]{:S(2)}) copy-start(bf16[7680,256]{1,0:T(8,128)(2,1)} %all-gather.5.cloned.1.call-done) | copy-start | bytes 11796484
  199.4 14.0 %copy-start.14 = (f32[768,512]{1,0:T(8,128)S(1)}, f32[768,512]{1,0:T(8,128)}, u32[]{:S(2)}) copy-start(f32[768,512]{1,0:T(8,128)} %copy-done.13) | copy-start | bytes 4718596
  199.5 14.0 %copy-start.16 = (bf16[256,768]{1,0:T(8,128)(2,1)S(1)}, bf16[256,768]{1,0:T(8,128)(2,1)}, u32[]{:S(2)}) copy-start(bf16[256,768]{1,0:T(8,128)(2,1)} %copy-done.15) | copy-start | bytes 1179652
  199.5 14.0 %copy-start.18 = (bf16[256,768]{1,0:T(8,128)(2,1)S(1)}, bf16[256,768]{1,0:T(8,128)(2,1)}, u32[]{:S(2)}) copy-start(bf16[256,768]{1,0:T(8,128)(2,1)} %copy-done.17) | copy-start | bytes 1179652
  210.1 9.5 %collective-permute-start.22 = (bf16[192,768]{1,0:T(8,128)(2,1)S(1)}, bf16[192,768]{1,0:T(8,128)(2,1)S(1)}, u32[]{:S(2)}, u32[]{:S(2)}) collective-permute-start(bf16[192,768]{1,0:T(8,128)(2,1)S(1)} %get-tuple-element.147), channel_id=1, source_target_pairs={{0,16},{16,32},{32,48},{48,0},{1,17},{17,33},{33,49},{49,1},{2,18}... | collective-permute-start | bytes 884744 | tf_op jit(solution)/shard_map/ppermute | solution.py:170
  210.2 14.0 %collective-permute-start.23 = (bf16[192,768]{1,0:T(8,128)(2,1)S(1)}, bf16[192,768]{1,0:T(8,128)(2,1)S(1)}, u32[]{:S(2)}, u32[]{:S(2)}) collective-permute-start(bf16[192,768]{1,0:T(8,128)(2,1)S(1)} %get-tuple-element.148), channel_id=1, source_target_pairs={{0,32},{16,48},{32,0},{48,16},{1,33},{17,49},{33,1},{49,17},{2,34}... | collective-permute-start | bytes 884744 | tf_op jit(solution)/shard_map/ppermute | solution.py:170
  212.3 14.0 %collective-permute-start.24 = (bf16[192,768]{1,0:T(8,128)(2,1)S(1)}, bf16[192,768]{1,0:T(8,128)(2,1)S(1)}, u32[]{:S(2)}, u32[]{:S(2)}) collective-permute-start(bf16[192,768]{1,0:T(8,128)(2,1)S(1)} %get-tuple-element.149), channel_id=1, source_target_pairs={{0,48},{16,0},{32,16},{48,32},{1,49},{17,1},{33,17},{49,33},{2,50}... | collective-permute-start | bytes 884744 | tf_op jit(solution)/shard_map/ppermute | solution.py:170
  213.4 12.8 %copy-start.20 = (f32[768,512]{1,0:T(8,128)S(1)}, f32[768,512]{1,0:T(8,128)}, u32[]{:S(2)}) copy-start(f32[768,512]{1,0:T(8,128)} %copy-done.19) | copy-start | bytes 4718596
  217.0 44.9 %collective-permute-start.17 = (f32[768,512]{1,0:T(8,128)}, f32[768,512]{1,0:T(8,128)}, u32[]{:S(2)}, u32[]{:S(2)}) collective-permute-start(f32[768,512]{1,0:T(8,128)} %get-tuple-element.119), channel_id=1, source_target_pairs={{0,64},{64,0},{1,65},{65,1},{2,66},{66,2},{3,67},{67,3},{4,68},{68... | collective-permute-start | bytes 4718600 | tf_op jit(solution)/shard_map/ppermute | solution.py:174
  229.8 32.2 %collective-permute-start.25 = (f32[768,512]{1,0:T(8,128)}, f32[768,512]{1,0:T(8,128)}, u32[]{:S(2)}, u32[]{:S(2)}) collective-permute-start(f32[768,512]{1,0:T(8,128)} %get-tuple-element.151.own), channel_id=1, source_target_pairs={{0,64},{64,0},{1,65},{65,1},{2,66},{66,2},{3,67},{67,3},{4,68},{68... | collective-permute-start | bytes 4718600 | tf_op jit(solution)/shard_map/ppermute | solution.py:174
  240.1 34.6 %copy-start.11 = (bf16[768,512]{1,0:T(8,128)(2,1)S(1)}, bf16[768,512]{1,0:T(8,128)(2,1)}, u32[]{:S(2)}) copy-start(bf16[768,512]{1,0:T(8,128)(2,1)} %get-tuple-element.106.refs_9_.states) | copy-start | bytes 2359300
  240.1 20.6 %all-to-all-start.2 = ((bf16[16,112,256]{2,1,0:T(8,128)(2,1)}), bf16[16,112,256]{2,1,0:T(8,128)(2,1)}, u32[]{:S(2)}, u32[]{:S(2)}) async-start(bf16[16,112,256]{2,1,0:T(8,128)(2,1)} %shard_map.171), calls=%async_computation.2 | async-start | bytes 1835008 | tf_op jit(solution)/shard_map/all_to_all | solution.py:178
  246.8 15.8 %collective-permute-start.29 = (bf16[320,256]{1,0:T(8,128)(2,1)S(1)}, bf16[320,256]{1,0:T(8,128)(2,1)S(1)}, u32[]{:S(2)}, u32[]{:S(2)}) collective-permute-start(bf16[320,256]{1,0:T(8,128)(2,1)S(1)} %reduce_sum.24.refs_4_), channel_id=1, source_target_pairs={{0,16},{16,32},{32,48},{48,0},{1,17},{17,33},{33,49},{49,1},{2,18}... | collective-permute-start | bytes 491528 | tf_op jit(solution)/shard_map/ppermute | solution.py:170
  246.9 17.9 %collective-permute-start.30 = (bf16[320,256]{1,0:T(8,128)(2,1)S(1)}, bf16[320,256]{1,0:T(8,128)(2,1)S(1)}, u32[]{:S(2)}, u32[]{:S(2)}) collective-permute-start(bf16[320,256]{1,0:T(8,128)(2,1)S(1)} %reduce_sum.24.refs_4_), channel_id=1, source_target_pairs={{0,32},{16,48},{32,0},{48,16},{1,33},{17,49},{33,1},{49,17},{2,34}... | collective-permute-start | bytes 491528 | tf_op jit(solution)/shard_map/ppermute | solution.py:170
  248.1 21.9 %collective-permute-start.31 = (bf16[320,256]{1,0:T(8,128)(2,1)S(1)}, bf16[320,256]{1,0:T(8,128)(2,1)S(1)}, u32[]{:S(2)}, u32[]{:S(2)}) collective-permute-start(bf16[320,256]{1,0:T(8,128)(2,1)S(1)} %reduce_sum.24.refs_4_), channel_id=1, source_target_pairs={{0,48},{16,0},{32,16},{48,32},{1,49},{17,1},{33,17},{49,33},{2,50}... | collective-permute-start | bytes 491528 | tf_op jit(solution)/shard_map/ppermute | solution.py:170
  262.0 10.5 %collective-permute-start.32 = (bf16[112,256]{1,0:T(8,128)(2,1)S(1)}, bf16[112,256]{1,0:T(8,128)(2,1)S(1)}, u32[]{:S(2)}, u32[]{:S(2)}) collective-permute-start(bf16[112,256]{1,0:T(8,128)(2,1)S(1)} %reduce_sum.25.refs_8_), channel_id=1, source_target_pairs={{0,16},{16,32},{32,48},{48,0},{1,17},{17,33},{33,49},{49,1},{2,18}... | collective-permute-start | bytes 172040 | tf_op jit(solution)/shard_map/ppermute | solution.py:170
  262.1 19.6 %collective-permute-start.33 = (bf16[112,256]{1,0:T(8,128)(2,1)S(1)}, bf16[112,256]{1,0:T(8,128)(2,1)S(1)}, u32[]{:S(2)}, u32[]{:S(2)}) collective-permute-start(bf16[112,256]{1,0:T(8,128)(2,1)S(1)} %reduce_sum.25.refs_8_), channel_id=1, source_target_pairs={{0,32},{16,48},{32,0},{48,16},{1,33},{17,49},{33,1},{49,17},{2,34}... | collective-permute-start | bytes 172040 | tf_op jit(solution)/shard_map/ppermute | solution.py:170
  262.7 19.0 %collective-permute-start.34 = (bf16[112,256]{1,0:T(8,128)(2,1)S(1)}, bf16[112,256]{1,0:T(8,128)(2,1)S(1)}, u32[]{:S(2)}, u32[]{:S(2)}) collective-permute-start(bf16[112,256]{1,0:T(8,128)(2,1)S(1)} %reduce_sum.25.refs_8_), channel_id=1, source_target_pairs={{0,48},{16,0},{32,16},{48,32},{1,49},{17,1},{33,17},{49,33},{2,50}... | collective-permute-start | bytes 172040 | tf_op jit(solution)/shard_map/ppermute | solution.py:170
  269.5 12.1 %collective-permute-start.26 = (bf16[432,256]{1,0:T(8,128)(2,1)}, bf16[432,256]{1,0:T(8,128)(2,1)S(1)}, u32[]{:S(2)}, u32[]{:S(2)}) collective-permute-start(bf16[432,256]{1,0:T(8,128)(2,1)} %bitcast.70), channel_id=1, source_target_pairs={{0,16},{16,32},{32,48},{48,0},{1,17},{17,33},{33,49},{49,1},{2,18}... | collective-permute-start | bytes 663560 | tf_op jit(solution)/shard_map/ppermute | solution.py:170
  270.7 11.0 %collective-permute-start.27 = (bf16[432,256]{1,0:T(8,128)(2,1)}, bf16[432,256]{1,0:T(8,128)(2,1)S(1)}, u32[]{:S(2)}, u32[]{:S(2)}) collective-permute-start(bf16[432,256]{1,0:T(8,128)(2,1)} %bitcast.71), channel_id=1, source_target_pairs={{0,32},{16,48},{32,0},{48,16},{1,33},{17,49},{33,1},{49,17},{2,34}... | collective-permute-start | bytes 663560 | tf_op jit(solution)/shard_map/ppermute | solution.py:170
  273.1 9.2 %collective-permute-start.28 = (bf16[432,256]{1,0:T(8,128)(2,1)}, bf16[432,256]{1,0:T(8,128)(2,1)S(1)}, u32[]{:S(2)}, u32[]{:S(2)}) collective-permute-start(bf16[432,256]{1,0:T(8,128)(2,1)} %bitcast.72), channel_id=1, source_target_pairs={{0,48},{16,0},{32,16},{48,32},{1,49},{17,1},{33,17},{49,33},{2,50}... | collective-permute-start | bytes 663560 | tf_op jit(solution)/shard_map/ppermute | solution.py:170
  283.0 3.8 %collective-permute-start.35 = (bf16[432,256]{1,0:T(8,128)(2,1)S(1)}, bf16[432,256]{1,0:T(8,128)(2,1)S(1)}, u32[]{:S(2)}, u32[]{:S(2)}) collective-permute-start(bf16[432,256]{1,0:T(8,128)(2,1)S(1)} %get-tuple-element.158), channel_id=1, source_target_pairs={{0,64},{64,0},{1,65},{65,1},{2,66},{66,2},{3,67},{67,3},{4,68},{68... | collective-permute-start | bytes 663560 | tf_op jit(solution)/shard_map/ppermute | solution.py:174
  (25 other events, 46.2 us)
Sparse Core Ops, SparseCore 0:
  16.6 56.3 all-gather.4
  75.7 43.6 all-gather.6
  166.3 103.1 reduce-scatter.3

commit v2 on v1

--- a/solution.py
+++ b/solution.py
@@ -135,7 +135,7 @@
         pack_body,
         place,
         (1,),
-        [whole(qkv), whole(proj), whole(up), whole(down), whole(norms)],
+        [whole(in_hbm(array)) for array in (qkv, proj, up, down)] + [whole(norms)],
         [whole_out((432, 256), BF), whole_out((432, 256), BF)],
         [pltpu.VMEM((2, 432, 256), BF)],
     )
@@ -309,8 +309,8 @@
         (4,),
         [
             whole(mlp_in),
-            (weights, (16, 32, 256), lambda b, _: (0, b, 0)),
-            (weights, (4, 128, 256), lambda b, _: (b, 1, 0)),
+            (in_hbm(weights), (16, 32, 256), lambda b, _: (0, b, 0)),
+            (in_hbm(weights), (4, 128, 256), lambda b, _: (b, 1, 0)),
         ],
         [
             whole_out((TOKENS, D), F32),
@@ -438,13 +438,14 @@
     )
 
 
-def put_proj(core, heads, grad, pack, first):
-    product = jnp.dot(heads[...], grad[...], preferred_element_type=F32).astype(BF)
-    for side in range(2):
-        span = pl.ds(first + 32 * side, 32)
-        part = product[:, 256 * side : 256 * side + 256].reshape(8, 32, 256)
-        pack[pl.ds(8 * core, 8), span, :] = part
-        pack[pl.ds(8 - 8 * core, 8), span, :] = jnp.zeros_like(part)
+def put_proj(core, heads, other_heads, half_grad, pack, first):
+    for side, held in ((core, heads), (1 - core, other_heads)):
+        part = jnp.dot(held[...], half_grad[...], preferred_element_type=F32)
+        pack[pl.ds(8 * side, 8), first : first + 32, :] = part.astype(BF).reshape(8, 32, 256)
+
+
+def half_columns(grad):
+    return (grad, (TOKENS, 256), lambda m, place: (0, place[1]))
 
 
 def mlp_back_body(with_proj, place, grad, active, slope, mlp_in, up, down, *refs):
@@ -462,7 +463,7 @@
     def _():
         out[...] = product
         if with_proj:
-            put_proj(place[1], refs[0], grad, pack, 256)
+            put_proj(place[1], *refs[:3], pack, 256)
 
     @pl.when(step > 0)
     def _():
@@ -477,21 +478,21 @@
         ].reshape(4, 64, 256)
 
 
-def mlp_back(place, grad, active, slope, mlp_in, weights, heads=None):
+def mlp_back(place, grad, active, slope, mlp_in, weights, heads=()):
     ins = [
         whole(grad),
         (in_hbm(active), (TOKENS, 256), lambda b, _: (0, b)),
         (in_hbm(slope), (TOKENS, 256), lambda b, _: (0, b)),
         whole(mlp_in),
-        (weights, (16, 32, 256), lambda b, _: (0, b, 0)),
-        (weights, (4, 128, 256), lambda b, _: (b, 1, 0)),
+        (in_hbm(weights), (16, 32, 256), lambda b, _: (0, b, 0)),
+        (in_hbm(weights), (4, 128, 256), lambda b, _: (b, 1, 0)),
     ]
     depth = 256
-    if heads is not None:
-        ins.append(whole(heads))
-        depth = 320
-    return call(
-        functools.partial(mlp_back_body, heads is not None),
+    if heads:
+        ins += [whole(array) for array in heads] + [half_columns(grad)]
+        depth = 288
+    return call(
+        functools.partial(mlp_back_body, bool(heads)),
         place,
         (4,),
         ins,
@@ -688,10 +689,9 @@
     pack = refs[-1]
     first = 0
     if with_rest:
-        rest, heads, grad = refs[:3]
-        pack[:, 0:256, :] = rest[...]
-        put_proj(place[1], heads, grad, pack, 256)
-        first = 320
+        pack[:, 0:256, :] = refs[0][...]
+        put_proj(place[1], *refs[1:4], pack, 256)
+        first = 288
     for part in range(3):
         product = dims(attn_in[...], mixed[part], 0, 1)
         at = first + 32 * part
@@ -712,8 +712,10 @@
         functools.partial(weight_back_body, bool(rest)),
         place,
         (1,),
-        [whole(attn_in), whole(mixed), whole(sums)] + [whole(array) for array in rest],
-        [whole_out((16, 432 if rest else 112, 256), BF)],
+        [whole(attn_in), whole(mixed), whole(sums)]
+        + [whole(array) for array in rest[:3]]
+        + [half_columns(array) for array in rest[3:]],
+        [(kept_in_hbm if rest else tuple)(whole_out((16, 400 if rest else 112, 256), BF))],
         flops=2_000_000_000,
         moved=6_000_000,
     )[0]
@@ -767,7 +769,7 @@
         place,
         (1,),
         [whole(piece) for piece in pieces],
-        [whole_out((432, 256), F32), whole_out((432, 256), BF)],
+        [whole_out((400, 256), F32), whole_out((400, 256), BF)],
     )
 
 
@@ -776,13 +778,12 @@
     total[core] = keep[...]
     total[1 - core] = got[...].astype(F32)
     low = lax.broadcasted_iota(jnp.int32, (32, 128), 1) < 64
-    sums[...] = total[0, 416:424, 0:128] + total[1, 416:424, 0:128]
+    sums[...] = total[0, 384:392, 0:128] + total[1, 384:392, 0:128]
     for half in range(2):
         for part in range(3):
             at = 512 * part + 256 * half
-            qkv[:, at : at + 256] = total[half, 320 + 32 * part : 352 + 32 * part]
-        at = 256 + 32 * half
-        proj[:, 256 * half : 256 * half + 256] = total[0, at : at + 32] + total[1, at : at + 32]
+            qkv[:, at : at + 256] = total[half, 288 + 32 * part : 320 + 32 * part]
+        proj[:, 256 * half : 256 * half + 256] = total[half, 256:288]
         for side in range(2):
             down[64 * half : 64 * half + 64, 256 * side : 256 * side + 256] = total[
                 half, 128 + 64 * side : 192 + 64 * side
@@ -812,7 +813,7 @@
             whole_out((128, 512), F32),
             whole_out((8, 128), F32),
         ],
-        [pltpu.VMEM((2, 432, 256), F32)],
+        [pltpu.VMEM((2, 400, 256), F32)],
     )
 
 
@@ -885,7 +886,7 @@
         part, heads = after_layer(place, came, 3 * layer, proj_of[layer], mlp_out)
         parts = (part, swap_core(part))
         extra = (parts, grad, proj_of[1])
-        saved.append((states, attn_in, mlp_in, active, slope, heads))
+        saved.append((states, attn_in, mlp_in, active, slope, (heads, swap_core(heads))))
     result = (states.astype(F32) + (parts[0] + parts[1])).astype(BF)
     layer_out = jnp.where(first, saved[1][0], result)
 
@@ -908,7 +909,7 @@
             place, came, qkv_of[layer], norms[layer], turns, states, mlp_grad
         )
         if layer == 1:
-            pack = weight_back(place, attn_in, mixed, norm_sums, (pack, *heads_of, grad))
+            pack = weight_back(place, attn_in, mixed, norm_sums, (pack, heads_of[0], swap_core(heads_of[0]), grad))
             total = lax.psum_scatter(pack, "shard", scatter_dimension=0, tiled=False)
             through = after(through, pack)
         else:

time: 297 us -> 289 us (0.973)
  local copies, waits for them, and re-layouts: 24.9 us -> 16 us
  waiting for transfers between devices: 69.9 us -> 64.4 us
  Pallas kernels: 103 us -> 108 us
    unnamed x94 -> x70, local copies, waits for them, and re-layouts: 24 us -> 15.1 us
    pallas_call x22, Pallas kernels: 103 us -> 108 us  [call(): pl.pallas_call(body, out_shape=[(pltpu.HBM if out[4:] else struct)(out[0]...]
    all_to_all x3, waiting for transfers between devices: 21.5 us -> 17.4 us  [to_owners(): return lax.all_to_all(pack, 'shard', 0, 0, tiled=True)]
    ppermute x6 -> x8, waiting for transfers between devices: 7.79 us -> 8.98 us  [swap_core(): return lax.ppermute(value, 'section', [(0, 1), (1, 0)])]
    ppermute x6 -> x8, starting transfers between devices: 11.7 us -> 12.1 us  [swap_core(): return lax.ppermute(value, 'section', [(0, 1), (1, 0)])]
  transfers between devices with their start and end apart: 42 -> 44, of which waited for: 20 -> 22; matrix products, arithmetic and copies ran while one was open for 3% -> 3% of each run, Pallas kernels for 31% -> 33%
where the time goes in v2:
time: 289 us; the launch traced here: 288 us
  Pallas kernels  108 us (37%)
  starting transfers between devices  77.2 us (27%)
  waiting for transfers between devices  64.4 us (22%)
  local copies, waits for them, and re-layouts  16 us (6%)
  between operations  14.2 us (5%)
  other arithmetic  8.52 us (3%)
    pallas_call x22, Pallas kernels, call(): pl.pallas_call(body, out_shape=[(pltpu.HBM if out[4:] else struct)(out[0]...  108 us
    ppermute x30, starting transfers between devices, shift_z(): return lax.ppermute(value, 'seq', [(z, (z + step) % 4) for z in range(4)])  45.7 us
    ppermute x30, waiting for transfers between devices, shift_z(): return lax.ppermute(value, 'seq', [(z, (z + step) % 4) for z in range(4)])  33.5 us
    all_to_all x3, starting transfers between devices, to_owners(): return lax.all_to_all(pack, 'shard', 0, 0, tiled=True)  19.3 us
    all_to_all x3, waiting for transfers between devices, to_owners(): return lax.all_to_all(pack, 'shard', 0, 0, tiled=True)  17.4 us
    unnamed x70, local copies, waits for them, and re-layouts  15.1 us
    ppermute x8, starting transfers between devices, swap_core(): return lax.ppermute(value, 'section', [(0, 1), (1, 0)])  12.1 us
    ppermute x8, waiting for transfers between devices, swap_core(): return lax.ppermute(value, 'section', [(0, 1), (1, 0)])  8.98 us
  transfers between devices with their start and end apart: 44, of which 22 were waited for; matrix products, arithmetic and copies ran while one was open for 3% of the time, Pallas kernels for 33%

profile of v2, /device:TPU:1, one launch (start us, length us, event | category | flops | bytes accessed | tf_op | source)
XLA Modules:
  0.0 288.0 jit_solution(11465556833528965421)
XLA Ops:
  8.1 1.7 shard_map.152
  9.8 1.5 collective-permute-start
  12.4 1.7 shard_map.153
  14.1 7.0 %all-to-all-start = ((bf16[16,112,256]{2,1,0:T(8,128)(2,1)}), bf16[16,112,256]{2,1,0:T(8,128)(2,1)S(1)}, u32[]{:S(2)}, u32[]{:S(2)}) async-start(bf16[16,112,256]{2,1,0:T(8,128)(2,1)} %get-tuple-element.88), calls=%async_computation | async-start | bytes 1835008 | tf_op jit(solution)/shard_map/all_to_all | solution.py:178
  21.2 1.7 collective-permute-start.1
  22.9 3.3 %collective-permute-start.2 = (s32[1,768]{1,0:T(1,128)S(1)}, s32[1,768]{1,0:T(1,128)S(1)}, u32[]{:S(2)}, u32[]{:S(2)}) collective-permute-start(s32[1,768]{1,0:T(1,128)S(1)} %bitcast.61), channel_id=1, source_target_pairs={{0,32},{16,48},{32,0},{48,16},{1,33},{17,49},{33,1},{49,17},{2,34}... | collective-permute-start | bytes 9224 | tf_op jit(solution)/shard_map/ppermute | solution.py:170
  27.3 1.6 collective-permute-done.3.refs_7_
  28.9 6.4 %all-to-all-done.refs_1_.refs_2_.refs_3_.refs_4_.refs_5_.refs_6_ = bf16[16,112,256]{2,1,0:T(8,128)(2,1)S(1)} async-done(((bf16[16,112,256]{2,1,0:T(8,128)(2,1)}), bf16[16,112,256]{2,1,0:T(8,128)(2,1)S(1)}, u32[]{:S(2)}, u32[]{:S(2)}) %all-to-all-start) | async-done | bytes 917536 | tf_op jit(solution)/shard_map/all_to_all | solution.py:178
  35.6 3.8 %shard_map.154 = (bf16[192,768]{1,0:T(8,128)(2,1)S(1)}, bf16[192,768]{1,0:T(8,128)(2,1)}, bf16[192,768]{1,0:T(8,128)(2,1)S(1)}, bf16[192,768]{1,0:T(8,128)(2,1)S...) custom-call(s32[4]{0:T(128)S(1)} %pad_add_fusion.place, bf16[768,512]{1,0:T(8,128)(2,1)S(1)} %bitcast.56, ...), custom_call_target="tpu_custom_call" | custom-call | flops 1200000000 | bytes 6000000 | tf_op jit(solution)/shard_map/pallas_call | solution.py:42
  40.1 2.0 collective-permute-start.4
  42.1 3.7 %collective-permute-start.5 = (bf16[192,768]{1,0:T(8,128)(2,1)S(1)}, bf16[192,768]{1,0:T(8,128)(2,1)S(1)}, u32[]{:S(2)}, u32[]{:S(2)}) collective-permute-start(bf16[192,768]{1,0:T(8,128)(2,1)S(1)} %get-tuple-element.92), channel_id=1, source_target_pairs={{0,32},{16,48},{32,0},{48,16},{1,33},{17,49},{33,1},{49,17},{2,34}... | collective-permute-start | bytes 884744 | tf_op jit(solution)/shard_map/ppermute | solution.py:170
  46.2 2.7 collective-permute-done.4.refs_1_
  48.9 5.3 %collective-permute-done.5.refs_2_ = bf16[192,768]{1,0:T(8,128)(2,1)S(1)} collective-permute-done((bf16[192,768]{1,0:T(8,128)(2,1)S(1)}, bf16[192,768]{1,0:T(8,128)(2,1)S(1)}, u32[]{:S(2)}, u32[]{:S(2)}) %collective-permute-start.5) | collective-permute-done | bytes 294944 | tf_op jit(solution)/shard_map/ppermute | solution.py:170
  55.2 7.1 %shard_map.155 = (bf16[64,768]{1,0:T(8,128)(2,1)S(1)}, bf16[64,768]{1,0:T(8,128)(2,1)S(1)}, bf16[64,768]{1,0:T(8,128)(2,1)S(1)}, bf16[64,768]{1,0:T(8,128)(2,1)S...) custom-call(s32[4]{0:T(128)S(1)} %pad_add_fusion.place, ...), custom_call_target="tpu_custom_call" | custom-call | flops 8000000000 | bytes 4000000 | tf_op jit(solution)/shard_map/pallas_call | solution.py:42
  62.3 3.9 %collective-permute-start.7 = (bf16[64,768]{1,0:T(8,128)(2,1)S(1)}, bf16[64,768]{1,0:T(8,128)(2,1)S(1)}, u32[]{:S(2)}, u32[]{:S(2)}) collective-permute-start(bf16[64,768]{1,0:T(8,128)(2,1)S(1)} %get-tuple-element.99), channel_id=1, source_target_pairs={{0,16},{16,32},{32,48},{48,0},{1,17},{17,33},{33,49},{49,1},{2,18}... | collective-permute-start | bytes 294920 | tf_op jit(solution)/shard_map/ppermute | solution.py:170
  66.2 2.4 collective-permute-start.9
  68.6 2.0 all-gather.5.cloned.1.call-done
  71.8 7.8 %shard_map.156 = (f32[768,512]{1,0:T(8,128)S(1)}, bf16[768,1024]{1,0:T(8,128)(2,1)}, f32[768,1024]{1,0:T(8,128)}) custom-call(s32[4]{0:T(128)S(1)} %pad_add_fusion.place, bf16[768,512]{1,0:T(8,128)(2,1)S(1)} %copy-done.31, bf16[16,480,256]{2,1,0:T(8,128)(2,1)} %bitcast.38, bf16[16,480,256]{2,1,0:T(8,128)(2,1)} %bitcast.39), custom_call_target="tpu_custom_call" | custom-call | flops 6000000000 | bytes 12000000 | tf_op jit(solution)/shard_map/pallas_call | solution.py:42
  79.6 2.8 shard_map.157
  82.5 2.1 collective-permute-start.10
  84.6 3.3 %collective-permute-done.10.refs_2_ = f32[768,512]{1,0:T(8,128)} collective-permute-done((f32[768,512]{1,0:T(8,128)}, f32[768,512]{1,0:T(8,128)}, u32[]{:S(2)}, u32[]{:S(2)}) %collective-permute-start.10) | collective-permute-done | bytes 1572896 | tf_op jit(solution)/shard_map/ppermute | solution.py:174
  87.9 2.1 copy-done.1
  90.0 5.8 %shard_map.158 = (bf16[256,768]{1,0:T(8,128)(2,1)S(1)}, bf16[256,768]{1,0:T(8,128)(2,1)S(1)}, bf16[256,768]{1,0:T(8,128)(2,1)S(1)}, bf16[256,768]{1,0:T(8,128)(2...) custom-call(s32[4]{0:T(128)S(1)} %pad_add_fusion.place, ...), custom_call_target="tpu_custom_call" | custom-call | flops 1200000000 | bytes 6000000 | tf_op jit(solution)/shard_map/pallas_call | solution.py:42
  96.6 1.9 collective-permute-start.12
  99.6 7.7 %collective-permute-done.11.refs_1_ = bf16[256,768]{1,0:T(8,128)(2,1)S(1)} collective-permute-done((bf16[256,768]{1,0:T(8,128)(2,1)S(1)}, bf16[256,768]{1,0:T(8,128)(2,1)S(1)}, u32[]{:S(2)}, u32[]{:S(2)}) %collective-permute-start.11) | collective-permute-done | bytes 393248 | tf_op jit(solution)/shard_map/ppermute | solution.py:170
  107.4 8.5 %collective-permute-done.12.refs_2_ = bf16[256,768]{1,0:T(8,128)(2,1)S(1)} collective-permute-done((bf16[256,768]{1,0:T(8,128)(2,1)S(1)}, bf16[256,768]{1,0:T(8,128)(2,1)S(1)}, u32[]{:S(2)}, u32[]{:S(2)}) %collective-permute-start.12) | collective-permute-done | bytes 393248 | tf_op jit(solution)/shard_map/ppermute | solution.py:170
  116.1 13.9 %shard_map.159 = (bf16[256,768]{1,0:T(8,128)(2,1)S(1)}, bf16[256,768]{1,0:T(8,128)(2,1)}, bf16[256,768]{1,0:T(8,128)(2,1)}, bf16[256,768]{1,0:T(8,128)(2,1)}) custom-call(s32[4]{0:T(128)S(1)} %pad_add_fusion.place, bf16[256,768]{1,0:T(8,128)(2,1)S(1)} %get-tuple-element.107.refs_0_, bf16[256,768]{1,0:T(8,128)(2,1)S(1)} %collective-permute-done.11.refs_1_, ...), custom_call_target="tpu_custom_call" | custom-call | flops 17999998976 | bytes 5000000 | tf_op jit(solution)/shard_map/pallas_call | solution.py:42
  130.0 2.2 collective-permute-start.14
  132.2 2.5 collective-permute-start.15
  135.9 7.6 %shard_map.160 = (f32[768,512]{1,0:T(8,128)S(1)}, bf16[768,1024]{1,0:T(8,128)(2,1)}, f32[768,1024]{1,0:T(8,128)}) custom-call(s32[4]{0:T(128)S(1)} %pad_add_fusion.place, bf16[768,512]{1,0:T(8,128)(2,1)S(1)} %copy-done.23, bf16[16,256,256]{2,1,0:T(8,128)(2,1)} %bitcast.75, bf16[16,256,256]{2,1,0:T(8,128)(2,1)} %bitcast.76), custom_call_target="tpu_custom_call" | custom-call | flops 6000000000 | bytes 12000000 | tf_op jit(solution)/shard_map/pallas_call | solution.py:42
  144.6 9.0 %shard_map.162 = (f32[768,512]{1,0:T(8,128)S(1)}, bf16[16,256,256]{2,1,0:T(8,128)(2,1)S(1)}) custom-call(s32[4]{0:T(128)S(1)} %pad_add_fusion.place, bf16[768,512]{1,0:T(8,128)(2,1)S(1)} %bitcast.53, bf16[768,1024]{1,0:T(8,128)(2,1)} %get-tuple-element.120.active, f32[768,1024]{1,0:T(8,128)} %get-tuple-element.121.slope, bf16[768,512]{1,0:T(8,128)(2,1)S(1)} %copy-done.24, ...), custom_call_target="tpu_custom_call" | custom-call | flops 8000000000 | bytes 14000000 | tf_op jit(solution)/shard_map/pallas_call | solution.py:42
  153.7 4.1 %shard_map.163 = (f32[768,512]{1,0:T(8,128)S(1)}, bf16[3,256,768]{2,1,0:T(8,128)(2,1)S(1)}, f32[8,512]{1,0:T(8,128)S(1)}, bf16[256,768]{1,0:T(8,128)(2,1)S(1)}) custom-call(s32[4]{0:T(128)S(1)} %pad_add_fusion.place, bf16[256,768]{1,0:T(8,128)(2,1)S(1)} %get-tuple-element.111.refs_0_, bf16[256,768]{1,0:T(8,128)(2,1)S(1)} %collective-permute-done.14.refs_1_, ...), custom_call_target="tpu_custom_call" | custom-call | flops 1500000000 | bytes 6000000 | tf_op jit(solution)/shard_map/pallas_call | solution.py:42
  159.1 1.5 collective-permute-start.18
  160.5 1.3 collective-permute-done.18.refs_2_
  161.9 3.4 %shard_map.164 = bf16[16,400,256]{2,1,0:T(8,128)(2,1)} custom-call(s32[4]{0:T(128)S(1)} %pad_add_fusion.place, bf16[768,512]{1,0:T(8,128)(2,1)S(1)} %copy-done.21, bf16[3,256,768]{2,1,0:T(8,128)(2,1)S(1)} %get-tuple-element.125.mixed, f32[8,512]{1,0:T(8,128)S(1)} %get-tuple-element.126.sums, bf16[16,256,256]{2,1,0:T(8,128)(2,1)S(1)} %get-tuple-element.127.refs_0_, ...), custom_call_target="tpu_custom_call" | custom-call | flops 2000000000 | bytes 6000000 | tf_op jit(solution)/shard_map/pallas_call | solution.py:42
  165.9 3.1 %collective-permute-done.19.came = f32[768,512]{1,0:T(8,128)S(1)} collective-permute-done((f32[768,512]{1,0:T(8,128)}, f32[768,512]{1,0:T(8,128)S(1)}, u32[]{:S(2)}, u32[]{:S(2)}) %collective-permute-start.19) | collective-permute-done | bytes 1572896 | tf_op jit(solution)/shard_map/ppermute | solution.py:174
  170.2 1.4 copy-done.20
  171.6 1.7 shard_map.165.grad.refs_2_
  173.4 1.6 shard_map.166
  176.8 2.0 collective-permute-start.22
  178.7 9.3 %shard_map.167 = (f32[768,512]{1,0:T(8,128)S(1)}, bf16[16,288,256]{2,1,0:T(8,128)(2,1)S(1)}) custom-call(s32[4]{0:T(128)S(1)} %pad_add_fusion.place, bf16[768,512]{1,0:T(8,128)(2,1)S(1)} %shard_map.165.grad.refs_2_, bf16[768,1024]{1,0:T(8,128)(2,1)} %get-tuple-element.135.active, f32[768,1024]{1,0:T(8,128)} %get-tuple-element.136.slope, ...), custom_call_target="tpu_custom_call" | custom-call | flops 8000000000 | bytes 14000000 | tf_op jit(solution)/shard_map/pallas_call | solution.py:42
  188.1 1.5 copy-done.10
  190.7 6.2 %all-to-all-start.1 = ((bf16[16,288,256]{2,1,0:T(8,128)(2,1)}), bf16[16,288,256]{2,1,0:T(8,128)(2,1)}, u32[]{:S(2)}, u32[]{:S(2)}) async-start(bf16[16,288,256]{2,1,0:T(8,128)(2,1)} %copy-done.10), calls=%async_computation.1 | async-start | bytes 4718592 | tf_op jit(solution)/shard_map/all_to_all | solution.py:178
  196.9 10.7 %shard_map.168 = (bf16[192,768]{1,0:T(8,128)(2,1)S(1)}, bf16[192,768]{1,0:T(8,128)(2,1)S(1)}, bf16[192,768]{1,0:T(8,128)(2,1)S(1)}, bf16[192,768]{1,0:T(8,128)(2,1)S(1)}) custom-call(s32[4]{0:T(128)S(1)} %pad_add_fusion.place, bf16[64,768]{1,0:T(8,128)(2,1)S(1)} %get-tuple-element.139.refs_0_, bf16[64,768]{1,0:T(8,128)(2,1)S(1)} %collective-permute-done.20.refs_1_, ...), custom_call_target="tpu_custom_call" | custom-call | flops 16000000000 | bytes 5000000 | tf_op jit(solution)/shard_map/pallas_call | solution.py:42
  207.7 2.0 collective-permute-start.25
  210.9 3.6 %shard_map.161 = (f32[768,512]{1,0:T(8,128)}, bf16[256,768]{1,0:T(8,128)(2,1)}) custom-call(s32[4]{0:T(128)S(1)} %pad_add_fusion.place, bf16[256,768]{1,0:T(8,128)(2,1)S(1)} %copy-done.14, bf16[256,768]{1,0:T(8,128)(2,1)S(1)} %copy-done.16, bf16[256,768]{1,0:T(8,128)(2,1)} %collective-permute-done.15.refs_2_, ...), custom_call_target="tpu_custom_call" | custom-call | flops 800000000 | bytes 4000000 | tf_op jit(solution)/shard_map/pallas_call | solution.py:42
  214.5 2.4 collective-permute-start.17
  217.1 4.5 %collective-permute-done.25.refs_2_ = bf16[192,768]{1,0:T(8,128)(2,1)S(1)} collective-permute-done((bf16[192,768]{1,0:T(8,128)(2,1)S(1)}, bf16[192,768]{1,0:T(8,128)(2,1)S(1)}, u32[]{:S(2)}, u32[]{:S(2)}) %collective-permute-start.25) | collective-permute-done | bytes 294944 | tf_op jit(solution)/shard_map/ppermute | solution.py:170
  221.6 2.2 collective-permute-done.26.refs_3_
  223.7 3.6 %shard_map.169 = (f32[768,512]{1,0:T(8,128)}, bf16[3,256,768]{2,1,0:T(8,128)(2,1)S(1)}, f32[8,512]{1,0:T(8,128)S(1)}) custom-call(s32[4]{0:T(128)S(1)} %pad_add_fusion.place, bf16[192,768]{1,0:T(8,128)(2,1)S(1)} %get-tuple-element.146.refs_0_, bf16[192,768]{1,0:T(8,128)(2,1)S(1)} %collective-permute-done.24.refs_1_, ...), custom_call_target="tpu_custom_call" | custom-call | flops 1500000000 | bytes 6000000 | tf_op jit(solution)/shard_map/pallas_call | solution.py:42
  227.3 1.6 collective-permute-start.27
  228.9 2.3 shard_map.171
  231.8 2.0 reduce_sum.24.refs_4_
  233.8 6.1 %all-to-all-start.2 = ((bf16[16,112,256]{2,1,0:T(8,128)(2,1)}), bf16[16,112,256]{2,1,0:T(8,128)(2,1)}, u32[]{:S(2)}, u32[]{:S(2)}) async-start(bf16[16,112,256]{2,1,0:T(8,128)(2,1)} %shard_map.171), calls=%async_computation.2 | async-start | bytes 1835008 | tf_op jit(solution)/shard_map/all_to_all | solution.py:178
  240.5 3.1 %collective-permute-start.32 = (bf16[288,256]{1,0:T(8,128)(2,1)S(1)}, bf16[288,256]{1,0:T(8,128)(2,1)S(1)}, u32[]{:S(2)}, u32[]{:S(2)}) collective-permute-start(bf16[288,256]{1,0:T(8,128)(2,1)S(1)} %reduce_sum.24.refs_4_), channel_id=1, source_target_pairs={{0,32},{16,48},{32,0},{48,16},{1,33},{17,49},{33,1},{49,17},{2,34}... | collective-permute-start | bytes 442376 | tf_op jit(solution)/shard_map/ppermute | solution.py:170
  243.6 10.4 %all-to-all-done.2 = bf16[16,112,256]{2,1,0:T(8,128)(2,1)} async-done(((bf16[16,112,256]{2,1,0:T(8,128)(2,1)}), bf16[16,112,256]{2,1,0:T(8,128)(2,1)}, u32[]{:S(2)}, u32[]{:S(2)}) %all-to-all-start.2) | async-done | bytes 917536 | tf_op jit(solution)/shard_map/all_to_all | solution.py:178
  254.0 1.3 reduce_sum.25.refs_8_
  256.5 3.1 %collective-permute-start.35 = (bf16[112,256]{1,0:T(8,128)(2,1)S(1)}, bf16[112,256]{1,0:T(8,128)(2,1)S(1)}, u32[]{:S(2)}, u32[]{:S(2)}) collective-permute-start(bf16[112,256]{1,0:T(8,128)(2,1)S(1)} %reduce_sum.25.refs_8_), channel_id=1, source_target_pairs={{0,32},{16,48},{32,0},{48,16},{1,33},{17,49},{33,1},{49,17},{2,34}... | collective-permute-start | bytes 172040 | tf_op jit(solution)/shard_map/ppermute | solution.py:170
  260.3 2.4 reduce-scatter.4.cloned.1.call-done
  264.5 2.9 %collective-permute-start.29 = (bf16[400,256]{1,0:T(8,128)(2,1)}, bf16[400,256]{1,0:T(8,128)(2,1)S(1)}, u32[]{:S(2)}, u32[]{:S(2)}) collective-permute-start(bf16[400,256]{1,0:T(8,128)(2,1)} %bitcast.67), channel_id=1, source_target_pairs={{0,32},{16,48},{32,0},{48,16},{1,33},{17,49},{33,1},{49,17},{2,34}... | collective-permute-start | bytes 614408 | tf_op jit(solution)/shard_map/ppermute | solution.py:170
  267.6 3.2 %fusion = bf16[768,512]{1,0:T(8,128)(2,1)} fusion(bf16[768,512]{1,0:T(8,128)(2,1)S(1)} %copy-done.9, f32[768,512]{1,0:T(8,128)} %get-tuple-element.119, f32[768,512]{1,0:T(8,128)} %collective-permute-done.17, pred[]{:T(512)S(6)} %eq.5), kind=kLoop, calls=%fused_computation.1 | loop fusion | flops 1966080 | bytes 4718593 | tf_op jit(solution)/shard_map/jit(_where)/select_n | solution.py:891
  270.8 3.7 %shard_map.170 = bf16[768,512]{1,0:T(8,128)(2,1)S(1)} custom-call(s32[4]{0:T(128)S(1)} %pad_add_fusion.place, bf16[768,512]{1,0:T(8,128)(2,1)S(1)} %bitcast.59, bf16[768,512]{1,0:T(8,128)(2,1)S(1)} %shard_map.165.grad.refs_2_, f32[768,512]{1,0:T(8,128)} %get-tuple-element.151.own, f32[768,512]{1,0:T(8,128)} %collective-permute-done.27.came), custom_call_target="tpu_custom_call" | custom-call | flops 100000000 | bytes 5000000 | tf_op jit(solution)/shard_map/pallas_call | solution.py:42
  275.7 2.5 collective-permute-start.37
  279.4 1.5 shard_map.173
  (139 shorter events, 26.5 us)
Async XLA Ops:
  7.2 63.4 %all-gather.5.cloned.1.call-start = ((), (), s32[]{:S(2)}) async-start(), calls=%async_computation.4 | async-start | bytes 4177920 | tf_op jit(solution)/shard_map/all_gather | solution.py:851
  9.8 2.6 collective-permute-start
  14.1 7.1 %copy-start.22 = (s32[3,1,256]{2,1,0:T(1,128)S(1)}, s32[3,1,256]{2,1,0:T(1,128)}, u32[]{:S(2)}) copy-start(s32[3,1,256]{2,1,0:T(1,128)} %param.10) | copy-start | bytes 9220
  14.1 21.5 %copy-start.6 = (bf16[3,1,256,512]{3,2,1,0:T(8,128)(2,1)S(1)}, bf16[3,1,256,512]{3,2,1,0:T(8,128)(2,1)}, u32[]{:S(2)}) copy-start(bf16[3,1,256,512]{3,2,1,0:T(8,128)(2,1)} %param.9) | copy-start | bytes 2359300
  14.1 21.2 %all-to-all-start = ((bf16[16,112,256]{2,1,0:T(8,128)(2,1)}), bf16[16,112,256]{2,1,0:T(8,128)(2,1)S(1)}, u32[]{:S(2)}, u32[]{:S(2)}) async-start(bf16[16,112,256]{2,1,0:T(8,128)(2,1)} %get-tuple-element.88), calls=%async_computation | async-start | bytes 1835008 | tf_op jit(solution)/shard_map/all_to_all | solution.py:178
  21.1 113.6 %all-gather.7.cloned.1.call-start = ((), (), s32[]{:S(2)}) async-start(), calls=%async_computation.5 | async-start | bytes 2228224 | tf_op jit(solution)/shard_map/all_gather | solution.py:852
  21.2 6.0 %collective-permute-start.1 = (s32[1,768]{1,0:T(1,128)S(1)}, s32[1,768]{1,0:T(1,128)S(1)}, u32[]{:S(2)}, u32[]{:S(2)}) collective-permute-start(s32[1,768]{1,0:T(1,128)S(1)} %bitcast.60), channel_id=1, source_target_pairs={{0,16},{16,32},{32,48},{48,0},{1,17},{17,33},{33,49},{49,1},{2,18}... | collective-permute-start | bytes 9224 | tf_op jit(solution)/shard_map/ppermute | solution.py:170
  22.9 4.4 %collective-permute-start.2 = (s32[1,768]{1,0:T(1,128)S(1)}, s32[1,768]{1,0:T(1,128)S(1)}, u32[]{:S(2)}, u32[]{:S(2)}) collective-permute-start(s32[1,768]{1,0:T(1,128)S(1)} %bitcast.61), channel_id=1, source_target_pairs={{0,32},{16,48},{32,0},{48,16},{1,33},{17,49},{33,1},{49,17},{2,34}... | collective-permute-start | bytes 9224 | tf_op jit(solution)/shard_map/ppermute | solution.py:170
  26.2 2.7 collective-permute-start.3
  40.1 8.8 %collective-permute-start.4 = (bf16[192,768]{1,0:T(8,128)(2,1)}, bf16[192,768]{1,0:T(8,128)(2,1)S(1)}, u32[]{:S(2)}, u32[]{:S(2)}) collective-permute-start(bf16[192,768]{1,0:T(8,128)(2,1)} %get-tuple-element.91), channel_id=1, source_target_pairs={{0,16},{16,32},{32,48},{48,0},{1,17},{17,33},{33,49},{49,1},{2,18}... | collective-permute-start | bytes 884744 | tf_op jit(solution)/shard_map/ppermute | solution.py:170
  42.1 12.1 %collective-permute-start.5 = (bf16[192,768]{1,0:T(8,128)(2,1)S(1)}, bf16[192,768]{1,0:T(8,128)(2,1)S(1)}, u32[]{:S(2)}, u32[]{:S(2)}) collective-permute-start(bf16[192,768]{1,0:T(8,128)(2,1)S(1)} %get-tuple-element.92), channel_id=1, source_target_pairs={{0,32},{16,48},{32,0},{48,16},{1,33},{17,49},{33,1},{49,17},{2,34}... | collective-permute-start | bytes 884744 | tf_op jit(solution)/shard_map/ppermute | solution.py:170
  45.8 8.4 %collective-permute-start.6 = (bf16[192,768]{1,0:T(8,128)(2,1)S(1)}, bf16[192,768]{1,0:T(8,128)(2,1)S(1)}, u32[]{:S(2)}, u32[]{:S(2)}) collective-permute-start(bf16[192,768]{1,0:T(8,128)(2,1)S(1)} %get-tuple-element.93), channel_id=1, source_target_pairs={{0,48},{16,0},{32,16},{48,32},{1,49},{17,1},{33,17},{49,33},{2,50}... | collective-permute-start | bytes 884744 | tf_op jit(solution)/shard_map/ppermute | solution.py:170
  46.2 216.5 %reduce-scatter.4.cloned.1.call-start = ((), (), s32[]{:S(2)}) async-start(), calls=%async_computation.6 | async-start | bytes 3481600
  62.3 17.3 %collective-permute-start.7 = (bf16[64,768]{1,0:T(8,128)(2,1)S(1)}, bf16[64,768]{1,0:T(8,128)(2,1)S(1)}, u32[]{:S(2)}, u32[]{:S(2)}) collective-permute-start(bf16[64,768]{1,0:T(8,128)(2,1)S(1)} %get-tuple-element.99), channel_id=1, source_target_pairs={{0,16},{16,32},{32,48},{48,0},{1,17},{17,33},{33,49},{49,1},{2,18}... | collective-permute-start | bytes 294920 | tf_op jit(solution)/shard_map/ppermute | solution.py:170
  66.2 13.4 %collective-permute-start.8 = (bf16[64,768]{1,0:T(8,128)(2,1)S(1)}, bf16[64,768]{1,0:T(8,128)(2,1)S(1)}, u32[]{:S(2)}, u32[]{:S(2)}) collective-permute-start(bf16[64,768]{1,0:T(8,128)(2,1)S(1)} %get-tuple-element.100), channel_id=1, source_target_pairs={{0,32},{16,48},{32,0},{48,16},{1,33},{17,49},{33,1},{49,17},{2,34}... | collective-permute-start | bytes 294920 | tf_op jit(solution)/shard_map/ppermute | solution.py:170
  66.2 13.4 %collective-permute-start.9 = (bf16[64,768]{1,0:T(8,128)(2,1)S(1)}, bf16[64,768]{1,0:T(8,128)(2,1)S(1)}, u32[]{:S(2)}, u32[]{:S(2)}) collective-permute-start(bf16[64,768]{1,0:T(8,128)(2,1)S(1)} %get-tuple-element.101), channel_id=1, source_target_pairs={{0,48},{16,0},{32,16},{48,32},{1,49},{17,1},{33,17},{49,33},{2,50}... | collective-permute-start | bytes 294920 | tf_op jit(solution)/shard_map/ppermute | solution.py:170
  71.8 7.9 %copy-start = (bf16[7680,256]{1,0:T(8,128)(2,1)S(1)}, bf16[7680,256]{1,0:T(8,128)(2,1)}, u32[]{:S(2)}) copy-start(bf16[7680,256]{1,0:T(8,128)(2,1)} %all-gather.5.cloned.1.call-done) | copy-start | bytes 11796484
  79.6 8.3 %copy-start.5 = (bf16[3,1,256,512]{3,2,1,0:T(8,128)(2,1)S(1)}, bf16[3,1,256,512]{3,2,1,0:T(8,128)(2,1)}, u32[]{:S(2)}) copy-start(bf16[3,1,256,512]{3,2,1,0:T(8,128)(2,1)} %param.11) | copy-start | bytes 2359300
  82.5 5.4 %collective-permute-start.10 = (f32[768,512]{1,0:T(8,128)}, f32[768,512]{1,0:T(8,128)}, u32[]{:S(2)}, u32[]{:S(2)}) collective-permute-start(f32[768,512]{1,0:T(8,128)} %get-tuple-element.105.refs_1_), channel_id=1, source_target_pairs={{0,64},{64,0},{1,65},{65,1},{2,66},{66,2},{3,67},{67,3},{4,68},{68... | collective-permute-start | bytes 4718600 | tf_op jit(solution)/shard_map/ppermute | solution.py:174
  95.8 11.6 %collective-permute-start.11 = (bf16[256,768]{1,0:T(8,128)(2,1)S(1)}, bf16[256,768]{1,0:T(8,128)(2,1)S(1)}, u32[]{:S(2)}, u32[]{:S(2)}) collective-permute-start(bf16[256,768]{1,0:T(8,128)(2,1)S(1)} %get-tuple-element.108), channel_id=1, source_target_pairs={{0,16},{16,32},{32,48},{48,0},{1,17},{17,33},{33,49},{49,1},{2,18}... | collective-permute-start | bytes 1179656 | tf_op jit(solution)/shard_map/ppermute | solution.py:170
  96.6 19.2 %collective-permute-start.12 = (bf16[256,768]{1,0:T(8,128)(2,1)S(1)}, bf16[256,768]{1,0:T(8,128)(2,1)S(1)}, u32[]{:S(2)}, u32[]{:S(2)}) collective-permute-start(bf16[256,768]{1,0:T(8,128)(2,1)S(1)} %get-tuple-element.109), channel_id=1, source_target_pairs={{0,32},{16,48},{32,0},{48,16},{1,33},{17,49},{33,1},{49,17},{2,34}... | collective-permute-start | bytes 1179656 | tf_op jit(solution)/shard_map/ppermute | solution.py:170
  98.5 17.6 %collective-permute-start.13 = (bf16[256,768]{1,0:T(8,128)(2,1)S(1)}, bf16[256,768]{1,0:T(8,128)(2,1)S(1)}, u32[]{:S(2)}, u32[]{:S(2)}) collective-permute-start(bf16[256,768]{1,0:T(8,128)(2,1)S(1)} %get-tuple-element.110), channel_id=1, source_target_pairs={{0,48},{16,0},{32,16},{48,32},{1,49},{17,1},{33,17},{49,33},{2,50}... | collective-permute-start | bytes 1179656 | tf_op jit(solution)/shard_map/ppermute | solution.py:170
  130.0 23.6 %copy-start.13 = (bf16[256,768]{1,0:T(8,128)(2,1)}, bf16[256,768]{1,0:T(8,128)(2,1)S(1)}, u32[]{:S(2)}) copy-start(bf16[256,768]{1,0:T(8,128)(2,1)S(1)} %get-tuple-element.111.refs_0_) | copy-start | bytes 1179652
  130.0 23.6 %collective-permute-start.14 = (bf16[256,768]{1,0:T(8,128)(2,1)}, bf16[256,768]{1,0:T(8,128)(2,1)S(1)}, u32[]{:S(2)}, u32[]{:S(2)}) collective-permute-start(bf16[256,768]{1,0:T(8,128)(2,1)} %get-tuple-element.112), channel_id=1, source_target_pairs={{0,16},{16,32},{32,48},{48,0},{1,17},{17,33},{33,49},{49,1},{2,18}... | collective-permute-start | bytes 1179656 | tf_op jit(solution)/shard_map/ppermute | solution.py:170
  132.2 21.4 %collective-permute-start.15 = (bf16[256,768]{1,0:T(8,128)(2,1)}, bf16[256,768]{1,0:T(8,128)(2,1)}, u32[]{:S(2)}, u32[]{:S(2)}) collective-permute-start(bf16[256,768]{1,0:T(8,128)(2,1)} %get-tuple-element.113), channel_id=1, source_target_pairs={{0,32},{16,48},{32,0},{48,16},{1,33},{17,49},{33,1},{49,17},{2,34}... | collective-permute-start | bytes 1179656 | tf_op jit(solution)/shard_map/ppermute | solution.py:170
  134.7 19.0 %collective-permute-start.16 = (bf16[256,768]{1,0:T(8,128)(2,1)}, bf16[256,768]{1,0:T(8,128)(2,1)}, u32[]{:S(2)}, u32[]{:S(2)}) collective-permute-start(bf16[256,768]{1,0:T(8,128)(2,1)} %get-tuple-element.114), channel_id=1, source_target_pairs={{0,48},{16,0},{32,16},{48,32},{1,49},{17,1},{33,17},{49,33},{2,50}... | collective-permute-start | bytes 1179656 | tf_op jit(solution)/shard_map/ppermute | solution.py:170
  135.9 8.8 %copy-start.24 = (bf16[768,512]{1,0:T(8,128)(2,1)S(1)}, bf16[768,512]{1,0:T(8,128)(2,1)}, u32[]{:S(2)}) copy-start(bf16[768,512]{1,0:T(8,128)(2,1)} %get-tuple-element.116.mlp_in) | copy-start | bytes 2359300
  144.6 9.1 %copy-start.2 = (bf16[7680,256]{1,0:T(8,128)(2,1)S(1)}, bf16[7680,256]{1,0:T(8,128)(2,1)}, u32[]{:S(2)}) copy-start(bf16[7680,256]{1,0:T(8,128)(2,1)} %all-gather.5.cloned.1.call-done) | copy-start | bytes 11796484
  144.6 9.1 %copy-start.7 = (bf16[768,512]{1,0:T(8,128)(2,1)S(1)}, bf16[768,512]{1,0:T(8,128)(2,1)}, u32[]{:S(2)}) copy-start(bf16[768,512]{1,0:T(8,128)(2,1)} %get-tuple-element.106.refs_9_.states) | copy-start | bytes 2359300
  153.7 4.2 %copy-start.15 = (bf16[256,768]{1,0:T(8,128)(2,1)}, bf16[256,768]{1,0:T(8,128)(2,1)S(1)}, u32[]{:S(2)}) copy-start(bf16[256,768]{1,0:T(8,128)(2,1)S(1)} %collective-permute-done.14.refs_1_) | copy-start | bytes 1179652
  153.7 8.2 %copy-start.21 = (bf16[768,512]{1,0:T(8,128)(2,1)S(1)}, bf16[768,512]{1,0:T(8,128)(2,1)}, u32[]{:S(2)}) copy-start(bf16[768,512]{1,0:T(8,128)(2,1)} %get-tuple-element.124.attn_in) | copy-start | bytes 2359300
  159.1 2.8 collective-permute-start.18
  165.3 3.7 %collective-permute-start.19 = (f32[768,512]{1,0:T(8,128)}, f32[768,512]{1,0:T(8,128)S(1)}, u32[]{:S(2)}, u32[]{:S(2)}) collective-permute-start(f32[768,512]{1,0:T(8,128)} %copy-done.19), channel_id=1, source_target_pairs={{0,64},{64,0},{1,65},{65,1},{2,66},{66,2},{3,67},{67,3},{4,68},{68... | collective-permute-start | bytes 4718600 | tf_op jit(solution)/shard_map/ppermute | solution.py:174
  165.8 7.5 %copy-start.3 = (bf16[7680,256]{1,0:T(8,128)(2,1)S(1)}, bf16[7680,256]{1,0:T(8,128)(2,1)}, u32[]{:S(2)}) copy-start(bf16[7680,256]{1,0:T(8,128)(2,1)} %all-gather.5.cloned.1.call-done) | copy-start | bytes 11796484
  165.8 12.9 %collective-permute-start.23 = (bf16[256,768]{1,0:T(8,128)(2,1)}, bf16[256,768]{1,0:T(8,128)(2,1)S(1)}, u32[]{:S(2)}, u32[]{:S(2)}) collective-permute-start(bf16[256,768]{1,0:T(8,128)(2,1)} %get-tuple-element.137.refs_0_), channel_id=1, source_target_pairs={{0,64},{64,0},{1,65},{65,1},{2,66},{66,2},{3,67},{67,3},{4,68},{68... | collective-permute-start | bytes 1179656 | tf_op jit(solution)/shard_map/ppermute | solution.py:174
  173.3 5.4 %copy-start.32 = (bf16[768,512]{1,0:T(8,128)(2,1)S(1)}, bf16[768,512]{1,0:T(8,128)(2,1)}, u32[]{:S(2)}) copy-start(bf16[768,512]{1,0:T(8,128)(2,1)} %get-tuple-element.103.mlp_in) | copy-start | bytes 2359300
  174.9 21.9 %collective-permute-start.20 = (bf16[64,768]{1,0:T(8,128)(2,1)S(1)}, bf16[64,768]{1,0:T(8,128)(2,1)S(1)}, u32[]{:S(2)}, u32[]{:S(2)}) collective-permute-start(bf16[64,768]{1,0:T(8,128)(2,1)S(1)} %get-tuple-element.131), channel_id=1, source_target_pairs={{0,16},{16,32},{32,48},{48,0},{1,17},{17,33},{33,49},{49,1},{2,18}... | collective-permute-start | bytes 294920 | tf_op jit(solution)/shard_map/ppermute | solution.py:170
  176.2 20.7 %collective-permute-start.21 = (bf16[64,768]{1,0:T(8,128)(2,1)S(1)}, bf16[64,768]{1,0:T(8,128)(2,1)S(1)}, u32[]{:S(2)}, u32[]{:S(2)}) collective-permute-start(bf16[64,768]{1,0:T(8,128)(2,1)S(1)} %get-tuple-element.132), channel_id=1, source_target_pairs={{0,32},{16,48},{32,0},{48,16},{1,33},{17,49},{33,1},{49,17},{2,34}... | collective-permute-start | bytes 294920 | tf_op jit(solution)/shard_map/ppermute | solution.py:170
  176.8 20.1 %collective-permute-start.22 = (bf16[64,768]{1,0:T(8,128)(2,1)S(1)}, bf16[64,768]{1,0:T(8,128)(2,1)S(1)}, u32[]{:S(2)}, u32[]{:S(2)}) collective-permute-start(bf16[64,768]{1,0:T(8,128)(2,1)S(1)} %get-tuple-element.133), channel_id=1, source_target_pairs={{0,48},{16,0},{32,16},{48,32},{1,49},{17,1},{33,17},{49,33},{2,50}... | collective-permute-start | bytes 294920 | tf_op jit(solution)/shard_map/ppermute | solution.py:170
  190.7 41.1 %all-to-all-start.1 = ((bf16[16,288,256]{2,1,0:T(8,128)(2,1)}), bf16[16,288,256]{2,1,0:T(8,128)(2,1)}, u32[]{:S(2)}, u32[]{:S(2)}) async-start(bf16[16,288,256]{2,1,0:T(8,128)(2,1)} %copy-done.10), calls=%async_computation.1 | async-start | bytes 4718592 | tf_op jit(solution)/shard_map/all_to_all | solution.py:178
  196.9 13.9 %copy-start.4 = (bf16[7680,256]{1,0:T(8,128)(2,1)S(1)}, bf16[7680,256]{1,0:T(8,128)(2,1)}, u32[]{:S(2)}) copy-start(bf16[7680,256]{1,0:T(8,128)(2,1)} %all-gather.5.cloned.1.call-done) | copy-start | bytes 11796484
  196.9 13.9 %copy-start.12 = (f32[768,512]{1,0:T(8,128)S(1)}, f32[768,512]{1,0:T(8,128)}, u32[]{:S(2)}) copy-start(f32[768,512]{1,0:T(8,128)} %copy-done.11) | copy-start | bytes 4718596
  196.9 13.9 %copy-start.14 = (bf16[256,768]{1,0:T(8,128)(2,1)S(1)}, bf16[256,768]{1,0:T(8,128)(2,1)}, u32[]{:S(2)}) copy-start(bf16[256,768]{1,0:T(8,128)(2,1)} %copy-done.13) | copy-start | bytes 1179652
  196.9 13.9 %copy-start.16 = (bf16[256,768]{1,0:T(8,128)(2,1)S(1)}, bf16[256,768]{1,0:T(8,128)(2,1)}, u32[]{:S(2)}) copy-start(bf16[256,768]{1,0:T(8,128)(2,1)} %copy-done.15) | copy-start | bytes 1179652
  207.6 9.5 %collective-permute-start.24 = (bf16[192,768]{1,0:T(8,128)(2,1)S(1)}, bf16[192,768]{1,0:T(8,128)(2,1)S(1)}, u32[]{:S(2)}, u32[]{:S(2)}) collective-permute-start(bf16[192,768]{1,0:T(8,128)(2,1)S(1)} %get-tuple-element.147), channel_id=1, source_target_pairs={{0,16},{16,32},{32,48},{48,0},{1,17},{17,33},{33,49},{49,1},{2,18}... | collective-permute-start | bytes 884744 | tf_op jit(solution)/shard_map/ppermute | solution.py:170
  207.7 13.9 %collective-permute-start.25 = (bf16[192,768]{1,0:T(8,128)(2,1)S(1)}, bf16[192,768]{1,0:T(8,128)(2,1)S(1)}, u32[]{:S(2)}, u32[]{:S(2)}) collective-permute-start(bf16[192,768]{1,0:T(8,128)(2,1)S(1)} %get-tuple-element.148), channel_id=1, source_target_pairs={{0,32},{16,48},{32,0},{48,16},{1,33},{17,49},{33,1},{49,17},{2,34}... | collective-permute-start | bytes 884744 | tf_op jit(solution)/shard_map/ppermute | solution.py:170
  209.7 14.0 %collective-permute-start.26 = (bf16[192,768]{1,0:T(8,128)(2,1)S(1)}, bf16[192,768]{1,0:T(8,128)(2,1)S(1)}, u32[]{:S(2)}, u32[]{:S(2)}) collective-permute-start(bf16[192,768]{1,0:T(8,128)(2,1)S(1)} %get-tuple-element.149), channel_id=1, source_target_pairs={{0,48},{16,0},{32,16},{48,32},{1,49},{17,1},{33,17},{49,33},{2,50}... | collective-permute-start | bytes 884744 | tf_op jit(solution)/shard_map/ppermute | solution.py:170
  210.9 12.8 %copy-start.18 = (f32[768,512]{1,0:T(8,128)S(1)}, f32[768,512]{1,0:T(8,128)}, u32[]{:S(2)}) copy-start(f32[768,512]{1,0:T(8,128)} %copy-done.17) | copy-start | bytes 4718596
  214.5 40.9 %collective-permute-start.17 = (f32[768,512]{1,0:T(8,128)}, f32[768,512]{1,0:T(8,128)}, u32[]{:S(2)}, u32[]{:S(2)}) collective-permute-start(f32[768,512]{1,0:T(8,128)} %get-tuple-element.119), channel_id=1, source_target_pairs={{0,64},{64,0},{1,65},{65,1},{2,66},{66,2},{3,67},{67,3},{4,68},{68... | collective-permute-start | bytes 4718600 | tf_op jit(solution)/shard_map/ppermute | solution.py:174
  223.7 5.2 %copy-start.30 = (bf16[768,512]{1,0:T(8,128)(2,1)S(1)}, bf16[768,512]{1,0:T(8,128)(2,1)}, u32[]{:S(2)}) copy-start(bf16[768,512]{1,0:T(8,128)(2,1)} %get-tuple-element.152.attn_in) | copy-start | bytes 2359300
  227.3 29.2 %collective-permute-start.27 = (f32[768,512]{1,0:T(8,128)}, f32[768,512]{1,0:T(8,128)}, u32[]{:S(2)}, u32[]{:S(2)}) collective-permute-start(f32[768,512]{1,0:T(8,128)} %get-tuple-element.151.own), channel_id=1, source_target_pairs={{0,64},{64,0},{1,65},{65,1},{2,66},{66,2},{3,67},{67,3},{4,68},{68... | collective-permute-start | bytes 4718600 | tf_op jit(solution)/shard_map/ppermute | solution.py:174
  233.8 33.8 %copy-start.9 = (bf16[768,512]{1,0:T(8,128)(2,1)S(1)}, bf16[768,512]{1,0:T(8,128)(2,1)}, u32[]{:S(2)}) copy-start(bf16[768,512]{1,0:T(8,128)(2,1)} %get-tuple-element.106.refs_9_.states) | copy-start | bytes 2359300
  233.8 20.2 %all-to-all-start.2 = ((bf16[16,112,256]{2,1,0:T(8,128)(2,1)}), bf16[16,112,256]{2,1,0:T(8,128)(2,1)}, u32[]{:S(2)}, u32[]{:S(2)}) async-start(bf16[16,112,256]{2,1,0:T(8,128)(2,1)} %shard_map.171), calls=%async_computation.2 | async-start | bytes 1835008 | tf_op jit(solution)/shard_map/all_to_all | solution.py:178
  240.0 19.6 %collective-permute-start.31 = (bf16[288,256]{1,0:T(8,128)(2,1)S(1)}, bf16[288,256]{1,0:T(8,128)(2,1)S(1)}, u32[]{:S(2)}, u32[]{:S(2)}) collective-permute-start(bf16[288,256]{1,0:T(8,128)(2,1)S(1)} %reduce_sum.24.refs_4_), channel_id=1, source_target_pairs={{0,16},{16,32},{32,48},{48,0},{1,17},{17,33},{33,49},{49,1},{2,18}... | collective-permute-start | bytes 442376 | tf_op jit(solution)/shard_map/ppermute | solution.py:170
  240.5 19.1 %collective-permute-start.32 = (bf16[288,256]{1,0:T(8,128)(2,1)S(1)}, bf16[288,256]{1,0:T(8,128)(2,1)S(1)}, u32[]{:S(2)}, u32[]{:S(2)}) collective-permute-start(bf16[288,256]{1,0:T(8,128)(2,1)S(1)} %reduce_sum.24.refs_4_), channel_id=1, source_target_pairs={{0,32},{16,48},{32,0},{48,16},{1,33},{17,49},{33,1},{49,17},{2,34}... | collective-permute-start | bytes 442376 | tf_op jit(solution)/shard_map/ppermute | solution.py:170
  243.6 20.2 %collective-permute-start.33 = (bf16[288,256]{1,0:T(8,128)(2,1)S(1)}, bf16[288,256]{1,0:T(8,128)(2,1)S(1)}, u32[]{:S(2)}, u32[]{:S(2)}) collective-permute-start(bf16[288,256]{1,0:T(8,128)(2,1)S(1)} %reduce_sum.24.refs_4_), channel_id=1, source_target_pairs={{0,48},{16,0},{32,16},{48,32},{1,49},{17,1},{33,17},{49,33},{2,50}... | collective-permute-start | bytes 442376 | tf_op jit(solution)/shard_map/ppermute | solution.py:170
  255.4 12.0 %collective-permute-start.34 = (bf16[112,256]{1,0:T(8,128)(2,1)S(1)}, bf16[112,256]{1,0:T(8,128)(2,1)S(1)}, u32[]{:S(2)}, u32[]{:S(2)}) collective-permute-start(bf16[112,256]{1,0:T(8,128)(2,1)S(1)} %reduce_sum.25.refs_8_), channel_id=1, source_target_pairs={{0,16},{16,32},{32,48},{48,0},{1,17},{17,33},{33,49},{49,1},{2,18}... | collective-permute-start | bytes 172040 | tf_op jit(solution)/shard_map/ppermute | solution.py:170
  256.5 18.1 %collective-permute-start.35 = (bf16[112,256]{1,0:T(8,128)(2,1)S(1)}, bf16[112,256]{1,0:T(8,128)(2,1)S(1)}, u32[]{:S(2)}, u32[]{:S(2)}) collective-permute-start(bf16[112,256]{1,0:T(8,128)(2,1)S(1)} %reduce_sum.25.refs_8_), channel_id=1, source_target_pairs={{0,32},{16,48},{32,0},{48,16},{1,33},{17,49},{33,1},{49,17},{2,34}... | collective-permute-start | bytes 172040 | tf_op jit(solution)/shard_map/ppermute | solution.py:170
  259.6 14.9 %collective-permute-start.36 = (bf16[112,256]{1,0:T(8,128)(2,1)S(1)}, bf16[112,256]{1,0:T(8,128)(2,1)S(1)}, u32[]{:S(2)}, u32[]{:S(2)}) collective-permute-start(bf16[112,256]{1,0:T(8,128)(2,1)S(1)} %reduce_sum.25.refs_8_), channel_id=1, source_target_pairs={{0,48},{16,0},{32,16},{48,32},{1,49},{17,1},{33,17},{49,33},{2,50}... | collective-permute-start | bytes 172040 | tf_op jit(solution)/shard_map/ppermute | solution.py:170
  262.7 11.9 %collective-permute-start.28 = (bf16[400,256]{1,0:T(8,128)(2,1)}, bf16[400,256]{1,0:T(8,128)(2,1)S(1)}, u32[]{:S(2)}, u32[]{:S(2)}) collective-permute-start(bf16[400,256]{1,0:T(8,128)(2,1)} %bitcast.66), channel_id=1, source_target_pairs={{0,16},{16,32},{32,48},{48,0},{1,17},{17,33},{33,49},{49,1},{2,18}... | collective-permute-start | bytes 614408 | tf_op jit(solution)/shard_map/ppermute | solution.py:170
  264.5 10.3 %collective-permute-start.29 = (bf16[400,256]{1,0:T(8,128)(2,1)}, bf16[400,256]{1,0:T(8,128)(2,1)S(1)}, u32[]{:S(2)}, u32[]{:S(2)}) collective-permute-start(bf16[400,256]{1,0:T(8,128)(2,1)} %bitcast.67), channel_id=1, source_target_pairs={{0,32},{16,48},{32,0},{48,16},{1,33},{17,49},{33,1},{49,17},{2,34}... | collective-permute-start | bytes 614408 | tf_op jit(solution)/shard_map/ppermute | solution.py:170
  267.4 7.6 %collective-permute-start.30 = (bf16[400,256]{1,0:T(8,128)(2,1)}, bf16[400,256]{1,0:T(8,128)(2,1)S(1)}, u32[]{:S(2)}, u32[]{:S(2)}) collective-permute-start(bf16[400,256]{1,0:T(8,128)(2,1)} %bitcast.68), channel_id=1, source_target_pairs={{0,48},{16,0},{32,16},{48,32},{1,49},{17,1},{33,17},{49,33},{2,50}... | collective-permute-start | bytes 614408 | tf_op jit(solution)/shard_map/ppermute | solution.py:170
  270.8 4.2 %copy-start.29 = (bf16[288,256]{1,0:T(8,128)(2,1)S(1)}, bf16[288,256]{1,0:T(8,128)(2,1)}, u32[]{:S(2)}) copy-start(bf16[288,256]{1,0:T(8,128)(2,1)} %copy-done.28) | copy-start | bytes 442372
  275.7 3.6 %collective-permute-start.37 = (bf16[400,256]{1,0:T(8,128)(2,1)S(1)}, bf16[400,256]{1,0:T(8,128)(2,1)S(1)}, u32[]{:S(2)}, u32[]{:S(2)}) collective-permute-start(bf16[400,256]{1,0:T(8,128)(2,1)S(1)} %get-tuple-element.158), channel_id=1, source_target_pairs={{0,64},{64,0},{1,65},{65,1},{2,66},{66,2},{3,67},{67,3},{4,68},{68... | collective-permute-start | bytes 614408 | tf_op jit(solution)/shard_map/ppermute | solution.py:174
  (15 other events, 23.3 us)
Sparse Core Ops, SparseCore 0:
  14.2 56.3 all-gather.4
  73.3 43.6 all-gather.6
  165.5 97.1 reduce-scatter.3

commit v3 on v2

--- a/solution.py
+++ b/solution.py
@@ -675,7 +675,7 @@
         (MICRO,),
         ins,
         [
-            rows_out(D, F32),
+            kept_in_hbm(rows_out(D, F32)),
             lanes_out((3, 256), BF),
             whole_out((8, D), F32),
         ]
@@ -911,14 +911,16 @@
         if layer == 1:
             pack = weight_back(place, attn_in, mixed, norm_sums, (pack, heads_of[0], swap_core(heads_of[0]), grad))
             total = lax.psum_scatter(pack, "shard", scatter_dimension=0, tiled=False)
-            through = after(through, pack)
         else:
             pack, sum_a = lax.optimization_barrier(
                 (weight_back(place, attn_in, mixed, norm_sums), sum_a)
             )
             pieces_a = regroup([sum_a] * 4)
             pieces_b = regroup([scatter_sum(pack)] * 4)
-        grad = end_back(place, states, grad, through, swap_core(through))
+        swapped = swap_core(through)
+        if layer == 1:
+            swapped = after(swapped, pack)
+        grad = end_back(place, states, grad, through, swapped)
         grads[layer] = grad
     grads_out = jnp.where(first, grads[0], grads[1])
 

time: 289 us -> 289 us (level)
  transfers between devices with their start and end apart: 44 -> 44, of which waited for: 22 -> 21; matrix products, arithmetic and copies ran while one was open for 3% -> 3% of each run, Pallas kernels for 33% -> 33%
where the time goes in v3:
time: 289 us; the launch traced here: 287 us
  Pallas kernels  108 us (37%)
  starting transfers between devices  77.2 us (27%)
  waiting for transfers between devices  64.7 us (22%)
  local copies, waits for them, and re-layouts  14.8 us (5%)
  between operations  14.2 us (5%)
  other arithmetic  8.5 us (3%)
    pallas_call x22, Pallas kernels, call(): pl.pallas_call(body, out_shape=[(pltpu.HBM if out[4:] else struct)(out[0]...  108 us
    ppermute x30, starting transfers between devices, shift_z(): return lax.ppermute(value, 'seq', [(z, (z + step) % 4) for z in range(4)])  45.6 us
    ppermute x30, waiting for transfers between devices, shift_z(): return lax.ppermute(value, 'seq', [(z, (z + step) % 4) for z in range(4)])  34.1 us
    all_to_all x3, starting transfers between devices, to_owners(): return lax.all_to_all(pack, 'shard', 0, 0, tiled=True)  19.7 us
    all_to_all x3, waiting for transfers between devices, to_owners(): return lax.all_to_all(pack, 'shard', 0, 0, tiled=True)  16.9 us
    unnamed x70, local copies, waits for them, and re-layouts  13.8 us
    ppermute x8, starting transfers between devices, swap_core(): return lax.ppermute(value, 'section', [(0, 1), (1, 0)])  11.8 us
    ppermute x8, waiting for transfers between devices, swap_core(): return lax.ppermute(value, 'section', [(0, 1), (1, 0)])  8.99 us
  transfers between devices with their start and end apart: 44, of which 21 were waited for; matrix products, arithmetic and copies ran while one was open for 3% of the time, Pallas kernels for 33%

profile of v3, /device:TPU:1, one launch (start us, length us, event | category | flops | bytes accessed | tf_op | source)
XLA Modules:
  0.0 287.4 jit_solution(898750854664114758)
XLA Ops:
  8.1 1.7 shard_map.152
  9.8 1.5 collective-permute-start
  12.4 1.7 shard_map.153
  14.1 7.0 %all-to-all-start = ((bf16[16,112,256]{2,1,0:T(8,128)(2,1)}), bf16[16,112,256]{2,1,0:T(8,128)(2,1)S(1)}, u32[]{:S(2)}, u32[]{:S(2)}) async-start(bf16[16,112,256]{2,1,0:T(8,128)(2,1)} %get-tuple-element.88), calls=%async_computation | async-start | bytes 1835008 | tf_op jit(solution)/shard_map/all_to_all | solution.py:178
  21.2 1.7 collective-permute-start.1
  22.9 3.3 %collective-permute-start.2 = (s32[1,768]{1,0:T(1,128)S(1)}, s32[1,768]{1,0:T(1,128)S(1)}, u32[]{:S(2)}, u32[]{:S(2)}) collective-permute-start(s32[1,768]{1,0:T(1,128)S(1)} %bitcast.61), channel_id=1, source_target_pairs={{0,32},{16,48},{32,0},{48,16},{1,33},{17,49},{33,1},{49,17},{2,34}... | collective-permute-start | bytes 9224 | tf_op jit(solution)/shard_map/ppermute | solution.py:170
  27.3 1.6 collective-permute-done.3.refs_7_
  28.9 6.4 %all-to-all-done.refs_1_.refs_2_.refs_3_.refs_4_.refs_5_.refs_6_ = bf16[16,112,256]{2,1,0:T(8,128)(2,1)S(1)} async-done(((bf16[16,112,256]{2,1,0:T(8,128)(2,1)}), bf16[16,112,256]{2,1,0:T(8,128)(2,1)S(1)}, u32[]{:S(2)}, u32[]{:S(2)}) %all-to-all-start) | async-done | bytes 917536 | tf_op jit(solution)/shard_map/all_to_all | solution.py:178
  35.6 3.8 %shard_map.154 = (bf16[192,768]{1,0:T(8,128)(2,1)S(1)}, bf16[192,768]{1,0:T(8,128)(2,1)}, bf16[192,768]{1,0:T(8,128)(2,1)S(1)}, bf16[192,768]{1,0:T(8,128)(2,1)S...) custom-call(s32[4]{0:T(128)S(1)} %pad_add_fusion.place, bf16[768,512]{1,0:T(8,128)(2,1)S(1)} %bitcast.56, ...), custom_call_target="tpu_custom_call" | custom-call | flops 1200000000 | bytes 6000000 | tf_op jit(solution)/shard_map/pallas_call | solution.py:42
  40.1 2.0 collective-permute-start.4
  42.1 3.7 %collective-permute-start.5 = (bf16[192,768]{1,0:T(8,128)(2,1)S(1)}, bf16[192,768]{1,0:T(8,128)(2,1)S(1)}, u32[]{:S(2)}, u32[]{:S(2)}) collective-permute-start(bf16[192,768]{1,0:T(8,128)(2,1)S(1)} %get-tuple-element.92), channel_id=1, source_target_pairs={{0,32},{16,48},{32,0},{48,16},{1,33},{17,49},{33,1},{49,17},{2,34}... | collective-permute-start | bytes 884744 | tf_op jit(solution)/shard_map/ppermute | solution.py:170
  46.2 2.7 collective-permute-done.4.refs_1_
  48.9 5.3 %collective-permute-done.5.refs_2_ = bf16[192,768]{1,0:T(8,128)(2,1)S(1)} collective-permute-done((bf16[192,768]{1,0:T(8,128)(2,1)S(1)}, bf16[192,768]{1,0:T(8,128)(2,1)S(1)}, u32[]{:S(2)}, u32[]{:S(2)}) %collective-permute-start.5) | collective-permute-done | bytes 294944 | tf_op jit(solution)/shard_map/ppermute | solution.py:170
  55.2 7.1 %shard_map.155 = (bf16[64,768]{1,0:T(8,128)(2,1)S(1)}, bf16[64,768]{1,0:T(8,128)(2,1)S(1)}, bf16[64,768]{1,0:T(8,128)(2,1)S(1)}, bf16[64,768]{1,0:T(8,128)(2,1)S...) custom-call(s32[4]{0:T(128)S(1)} %pad_add_fusion.place, ...), custom_call_target="tpu_custom_call" | custom-call | flops 8000000000 | bytes 4000000 | tf_op jit(solution)/shard_map/pallas_call | solution.py:42
  62.3 3.9 %collective-permute-start.7 = (bf16[64,768]{1,0:T(8,128)(2,1)S(1)}, bf16[64,768]{1,0:T(8,128)(2,1)S(1)}, u32[]{:S(2)}, u32[]{:S(2)}) collective-permute-start(bf16[64,768]{1,0:T(8,128)(2,1)S(1)} %get-tuple-element.99), channel_id=1, source_target_pairs={{0,16},{16,32},{32,48},{48,0},{1,17},{17,33},{33,49},{49,1},{2,18}... | collective-permute-start | bytes 294920 | tf_op jit(solution)/shard_map/ppermute | solution.py:170
  66.2 2.4 collective-permute-start.9
  68.6 2.0 all-gather.5.cloned.1.call-done
  71.8 7.8 %shard_map.156 = (f32[768,512]{1,0:T(8,128)S(1)}, bf16[768,1024]{1,0:T(8,128)(2,1)}, f32[768,1024]{1,0:T(8,128)}) custom-call(s32[4]{0:T(128)S(1)} %pad_add_fusion.place, bf16[768,512]{1,0:T(8,128)(2,1)S(1)} %copy-done.31, bf16[16,480,256]{2,1,0:T(8,128)(2,1)} %bitcast.38, bf16[16,480,256]{2,1,0:T(8,128)(2,1)} %bitcast.39), custom_call_target="tpu_custom_call" | custom-call | flops 6000000000 | bytes 12000000 | tf_op jit(solution)/shard_map/pallas_call | solution.py:42
  79.6 2.8 shard_map.157
  82.5 2.1 collective-permute-start.10
  84.6 3.3 %collective-permute-done.10.refs_2_ = f32[768,512]{1,0:T(8,128)} collective-permute-done((f32[768,512]{1,0:T(8,128)}, f32[768,512]{1,0:T(8,128)}, u32[]{:S(2)}, u32[]{:S(2)}) %collective-permute-start.10) | collective-permute-done | bytes 1572896 | tf_op jit(solution)/shard_map/ppermute | solution.py:174
  87.9 2.1 copy-done.1
  90.0 5.8 %shard_map.158 = (bf16[256,768]{1,0:T(8,128)(2,1)S(1)}, bf16[256,768]{1,0:T(8,128)(2,1)S(1)}, bf16[256,768]{1,0:T(8,128)(2,1)S(1)}, bf16[256,768]{1,0:T(8,128)(2...) custom-call(s32[4]{0:T(128)S(1)} %pad_add_fusion.place, ...), custom_call_target="tpu_custom_call" | custom-call | flops 1200000000 | bytes 6000000 | tf_op jit(solution)/shard_map/pallas_call | solution.py:42
  96.6 1.9 collective-permute-start.12
  99.6 7.7 %collective-permute-done.11.refs_1_ = bf16[256,768]{1,0:T(8,128)(2,1)S(1)} collective-permute-done((bf16[256,768]{1,0:T(8,128)(2,1)S(1)}, bf16[256,768]{1,0:T(8,128)(2,1)S(1)}, u32[]{:S(2)}, u32[]{:S(2)}) %collective-permute-start.11) | collective-permute-done | bytes 393248 | tf_op jit(solution)/shard_map/ppermute | solution.py:170
  107.4 8.5 %collective-permute-done.12.refs_2_ = bf16[256,768]{1,0:T(8,128)(2,1)S(1)} collective-permute-done((bf16[256,768]{1,0:T(8,128)(2,1)S(1)}, bf16[256,768]{1,0:T(8,128)(2,1)S(1)}, u32[]{:S(2)}, u32[]{:S(2)}) %collective-permute-start.12) | collective-permute-done | bytes 393248 | tf_op jit(solution)/shard_map/ppermute | solution.py:170
  116.1 13.9 %shard_map.159 = (bf16[256,768]{1,0:T(8,128)(2,1)S(1)}, bf16[256,768]{1,0:T(8,128)(2,1)}, bf16[256,768]{1,0:T(8,128)(2,1)}, bf16[256,768]{1,0:T(8,128)(2,1)}) custom-call(s32[4]{0:T(128)S(1)} %pad_add_fusion.place, bf16[256,768]{1,0:T(8,128)(2,1)S(1)} %get-tuple-element.107.refs_0_, bf16[256,768]{1,0:T(8,128)(2,1)S(1)} %collective-permute-done.11.refs_1_, ...), custom_call_target="tpu_custom_call" | custom-call | flops 17999998976 | bytes 5000000 | tf_op jit(solution)/shard_map/pallas_call | solution.py:42
  130.0 2.2 collective-permute-start.14
  132.2 2.5 collective-permute-start.15
  135.9 7.6 %shard_map.160 = (f32[768,512]{1,0:T(8,128)S(1)}, bf16[768,1024]{1,0:T(8,128)(2,1)}, f32[768,1024]{1,0:T(8,128)}) custom-call(s32[4]{0:T(128)S(1)} %pad_add_fusion.place, bf16[768,512]{1,0:T(8,128)(2,1)S(1)} %copy-done.23, bf16[16,256,256]{2,1,0:T(8,128)(2,1)} %bitcast.75, bf16[16,256,256]{2,1,0:T(8,128)(2,1)} %bitcast.76), custom_call_target="tpu_custom_call" | custom-call | flops 6000000000 | bytes 12000000 | tf_op jit(solution)/shard_map/pallas_call | solution.py:42
  144.6 9.0 %shard_map.162 = (f32[768,512]{1,0:T(8,128)S(1)}, bf16[16,256,256]{2,1,0:T(8,128)(2,1)S(1)}) custom-call(s32[4]{0:T(128)S(1)} %pad_add_fusion.place, bf16[768,512]{1,0:T(8,128)(2,1)S(1)} %bitcast.53, bf16[768,1024]{1,0:T(8,128)(2,1)} %get-tuple-element.120.active, f32[768,1024]{1,0:T(8,128)} %get-tuple-element.121.slope, bf16[768,512]{1,0:T(8,128)(2,1)S(1)} %copy-done.24, ...), custom_call_target="tpu_custom_call" | custom-call | flops 8000000000 | bytes 14000000 | tf_op jit(solution)/shard_map/pallas_call | solution.py:42
  153.7 4.7 %shard_map.163 = (f32[768,512]{1,0:T(8,128)}, bf16[3,256,768]{2,1,0:T(8,128)(2,1)S(1)}, f32[8,512]{1,0:T(8,128)S(1)}, bf16[256,768]{1,0:T(8,128)(2,1)S(1)}) custom-call(s32[4]{0:T(128)S(1)} %pad_add_fusion.place, bf16[256,768]{1,0:T(8,128)(2,1)S(1)} %get-tuple-element.111.refs_0_, bf16[256,768]{1,0:T(8,128)(2,1)S(1)} %collective-permute-done.14.refs_1_, ...), custom_call_target="tpu_custom_call" | custom-call | flops 1500000000 | bytes 6000000 | tf_op jit(solution)/shard_map/pallas_call | solution.py:42
  158.4 1.5 collective-permute-start.19
  159.9 1.3 collective-permute-done.19.refs_2_
  161.3 3.4 %shard_map.164 = bf16[16,400,256]{2,1,0:T(8,128)(2,1)} custom-call(s32[4]{0:T(128)S(1)} %pad_add_fusion.place, bf16[768,512]{1,0:T(8,128)(2,1)S(1)} %copy-done.21, bf16[3,256,768]{2,1,0:T(8,128)(2,1)S(1)} %get-tuple-element.125.mixed, f32[8,512]{1,0:T(8,128)S(1)} %get-tuple-element.126.sums, bf16[16,256,256]{2,1,0:T(8,128)(2,1)S(1)} %get-tuple-element.127.refs_0_, ...), custom_call_target="tpu_custom_call" | custom-call | flops 2000000000 | bytes 6000000 | tf_op jit(solution)/shard_map/pallas_call | solution.py:42
  165.3 3.1 %collective-permute-done.18.came = f32[768,512]{1,0:T(8,128)S(1)} collective-permute-done((f32[768,512]{1,0:T(8,128)}, f32[768,512]{1,0:T(8,128)S(1)}, u32[]{:S(2)}, u32[]{:S(2)}) %collective-permute-start.18) | collective-permute-done | bytes 1572896 | tf_op jit(solution)/shard_map/ppermute | solution.py:174
  169.5 1.4 copy-done.20
  170.9 1.7 shard_map.165.grad.refs_2_
  172.7 1.6 shard_map.166
  176.1 2.0 collective-permute-start.22
  178.1 9.3 %shard_map.167 = (f32[768,512]{1,0:T(8,128)S(1)}, bf16[16,288,256]{2,1,0:T(8,128)(2,1)S(1)}) custom-call(s32[4]{0:T(128)S(1)} %pad_add_fusion.place, bf16[768,512]{1,0:T(8,128)(2,1)S(1)} %shard_map.165.grad.refs_2_, bf16[768,1024]{1,0:T(8,128)(2,1)} %get-tuple-element.135.active, f32[768,1024]{1,0:T(8,128)} %get-tuple-element.136.slope, ...), custom_call_target="tpu_custom_call" | custom-call | flops 8000000000 | bytes 14000000 | tf_op jit(solution)/shard_map/pallas_call | solution.py:42
  187.4 1.5 copy-done.10
  190.0 6.2 %all-to-all-start.1 = ((bf16[16,288,256]{2,1,0:T(8,128)(2,1)}), bf16[16,288,256]{2,1,0:T(8,128)(2,1)}, u32[]{:S(2)}, u32[]{:S(2)}) async-start(bf16[16,288,256]{2,1,0:T(8,128)(2,1)} %copy-done.10), calls=%async_computation.1 | async-start | bytes 4718592 | tf_op jit(solution)/shard_map/all_to_all | solution.py:178
  196.3 10.7 %shard_map.168 = (bf16[192,768]{1,0:T(8,128)(2,1)S(1)}, bf16[192,768]{1,0:T(8,128)(2,1)S(1)}, bf16[192,768]{1,0:T(8,128)(2,1)S(1)}, bf16[192,768]{1,0:T(8,128)(2,1)S(1)}) custom-call(s32[4]{0:T(128)S(1)} %pad_add_fusion.place, bf16[64,768]{1,0:T(8,128)(2,1)S(1)} %get-tuple-element.139.refs_0_, bf16[64,768]{1,0:T(8,128)(2,1)S(1)} %collective-permute-done.20.refs_1_, ...), custom_call_target="tpu_custom_call" | custom-call | flops 16000000000 | bytes 5000000 | tf_op jit(solution)/shard_map/pallas_call | solution.py:42
  207.1 2.0 collective-permute-start.25
  210.2 3.6 %shard_map.161 = (f32[768,512]{1,0:T(8,128)}, bf16[256,768]{1,0:T(8,128)(2,1)}) custom-call(s32[4]{0:T(128)S(1)} %pad_add_fusion.place, bf16[256,768]{1,0:T(8,128)(2,1)S(1)} %copy-done.14, bf16[256,768]{1,0:T(8,128)(2,1)S(1)} %copy-done.16, bf16[256,768]{1,0:T(8,128)(2,1)} %collective-permute-done.15.refs_2_, ...), custom_call_target="tpu_custom_call" | custom-call | flops 800000000 | bytes 4000000 | tf_op jit(solution)/shard_map/pallas_call | solution.py:42
  213.8 2.4 collective-permute-start.17
  216.4 4.5 %collective-permute-done.25.refs_2_ = bf16[192,768]{1,0:T(8,128)(2,1)S(1)} collective-permute-done((bf16[192,768]{1,0:T(8,128)(2,1)S(1)}, bf16[192,768]{1,0:T(8,128)(2,1)S(1)}, u32[]{:S(2)}, u32[]{:S(2)}) %collective-permute-start.25) | collective-permute-done | bytes 294944 | tf_op jit(solution)/shard_map/ppermute | solution.py:170
  220.9 2.2 collective-permute-done.26.refs_3_
  223.1 3.6 %shard_map.169 = (f32[768,512]{1,0:T(8,128)}, bf16[3,256,768]{2,1,0:T(8,128)(2,1)S(1)}, f32[8,512]{1,0:T(8,128)S(1)}) custom-call(s32[4]{0:T(128)S(1)} %pad_add_fusion.place, bf16[192,768]{1,0:T(8,128)(2,1)S(1)} %get-tuple-element.146.refs_0_, bf16[192,768]{1,0:T(8,128)(2,1)S(1)} %collective-permute-done.24.refs_1_, ...), custom_call_target="tpu_custom_call" | custom-call | flops 1500000000 | bytes 6000000 | tf_op jit(solution)/shard_map/pallas_call | solution.py:42
  226.7 1.6 collective-permute-start.27
  228.2 2.3 shard_map.171
  230.7 2.0 reduce_sum.24.refs_4_
  232.7 6.6 %all-to-all-start.2 = ((bf16[16,112,256]{2,1,0:T(8,128)(2,1)}), bf16[16,112,256]{2,1,0:T(8,128)(2,1)}, u32[]{:S(2)}, u32[]{:S(2)}) async-start(bf16[16,112,256]{2,1,0:T(8,128)(2,1)} %shard_map.171), calls=%async_computation.2 | async-start | bytes 1835008 | tf_op jit(solution)/shard_map/all_to_all | solution.py:178
  239.9 3.1 %collective-permute-start.32 = (bf16[288,256]{1,0:T(8,128)(2,1)S(1)}, bf16[288,256]{1,0:T(8,128)(2,1)S(1)}, u32[]{:S(2)}, u32[]{:S(2)}) collective-permute-start(bf16[288,256]{1,0:T(8,128)(2,1)S(1)} %reduce_sum.24.refs_4_), channel_id=1, source_target_pairs={{0,32},{16,48},{32,0},{48,16},{1,33},{17,49},{33,1},{49,17},{2,34}... | collective-permute-start | bytes 442376 | tf_op jit(solution)/shard_map/ppermute | solution.py:170
  243.0 10.3 %all-to-all-done.2 = bf16[16,112,256]{2,1,0:T(8,128)(2,1)} async-done(((bf16[16,112,256]{2,1,0:T(8,128)(2,1)}), bf16[16,112,256]{2,1,0:T(8,128)(2,1)}, u32[]{:S(2)}, u32[]{:S(2)}) %all-to-all-start.2) | async-done | bytes 917536 | tf_op jit(solution)/shard_map/all_to_all | solution.py:178
  253.3 1.3 reduce_sum.25.refs_8_
  255.3 3.7 %collective-permute-start.35 = (bf16[112,256]{1,0:T(8,128)(2,1)S(1)}, bf16[112,256]{1,0:T(8,128)(2,1)S(1)}, u32[]{:S(2)}, u32[]{:S(2)}) collective-permute-start(bf16[112,256]{1,0:T(8,128)(2,1)S(1)} %reduce_sum.25.refs_8_), channel_id=1, source_target_pairs={{0,32},{16,48},{32,0},{48,16},{1,33},{17,49},{33,1},{49,17},{2,34}... | collective-permute-start | bytes 172040 | tf_op jit(solution)/shard_map/ppermute | solution.py:170
  259.6 2.7 reduce-scatter.4.cloned.1.call-done
  263.9 2.4 collective-permute-start.29
  267.0 3.2 %fusion = bf16[768,512]{1,0:T(8,128)(2,1)} fusion(bf16[768,512]{1,0:T(8,128)(2,1)S(1)} %copy-done.9, f32[768,512]{1,0:T(8,128)} %get-tuple-element.119, f32[768,512]{1,0:T(8,128)} %collective-permute-done.17, pred[]{:T(512)S(6)} %eq.5), kind=kLoop, calls=%fused_computation.1 | loop fusion | flops 1966080 | bytes 4718593 | tf_op jit(solution)/shard_map/jit(_where)/select_n | solution.py:891
  270.2 3.4 %shard_map.170 = bf16[768,512]{1,0:T(8,128)(2,1)S(1)} custom-call(s32[4]{0:T(128)S(1)} %pad_add_fusion.place, bf16[768,512]{1,0:T(8,128)(2,1)S(1)} %bitcast.59, bf16[768,512]{1,0:T(8,128)(2,1)S(1)} %shard_map.165.grad.refs_2_, f32[768,512]{1,0:T(8,128)S(1)} %copy-done.17, f32[768,512]{1,0:T(8,128)} %collective-permute-done.27.came), custom_call_target="tpu_custom_call" | custom-call | flops 100000000 | bytes 5000000 | tf_op jit(solution)/shard_map/pallas_call | solution.py:42
  275.5 2.2 collective-permute-start.37
  278.8 1.5 shard_map.173
  (139 shorter events, 25.2 us)
Async XLA Ops:
  7.2 63.4 %all-gather.5.cloned.1.call-start = ((), (), s32[]{:S(2)}) async-start(), calls=%async_computation.4 | async-start | bytes 4177920 | tf_op jit(solution)/shard_map/all_gather | solution.py:851
  9.8 2.6 collective-permute-start
  14.1 7.1 %copy-start.22 = (s32[3,1,256]{2,1,0:T(1,128)S(1)}, s32[3,1,256]{2,1,0:T(1,128)}, u32[]{:S(2)}) copy-start(s32[3,1,256]{2,1,0:T(1,128)} %param.10) | copy-start | bytes 9220
  14.1 21.5 %copy-start.6 = (bf16[3,1,256,512]{3,2,1,0:T(8,128)(2,1)S(1)}, bf16[3,1,256,512]{3,2,1,0:T(8,128)(2,1)}, u32[]{:S(2)}) copy-start(bf16[3,1,256,512]{3,2,1,0:T(8,128)(2,1)} %param.9) | copy-start | bytes 2359300
  14.1 21.2 %all-to-all-start = ((bf16[16,112,256]{2,1,0:T(8,128)(2,1)}), bf16[16,112,256]{2,1,0:T(8,128)(2,1)S(1)}, u32[]{:S(2)}, u32[]{:S(2)}) async-start(bf16[16,112,256]{2,1,0:T(8,128)(2,1)} %get-tuple-element.88), calls=%async_computation | async-start | bytes 1835008 | tf_op jit(solution)/shard_map/all_to_all | solution.py:178
  21.1 113.6 %all-gather.7.cloned.1.call-start = ((), (), s32[]{:S(2)}) async-start(), calls=%async_computation.5 | async-start | bytes 2228224 | tf_op jit(solution)/shard_map/all_gather | solution.py:852
  21.2 6.0 %collective-permute-start.1 = (s32[1,768]{1,0:T(1,128)S(1)}, s32[1,768]{1,0:T(1,128)S(1)}, u32[]{:S(2)}, u32[]{:S(2)}) collective-permute-start(s32[1,768]{1,0:T(1,128)S(1)} %bitcast.60), channel_id=1, source_target_pairs={{0,16},{16,32},{32,48},{48,0},{1,17},{17,33},{33,49},{49,1},{2,18}... | collective-permute-start | bytes 9224 | tf_op jit(solution)/shard_map/ppermute | solution.py:170
  22.9 4.4 %collective-permute-start.2 = (s32[1,768]{1,0:T(1,128)S(1)}, s32[1,768]{1,0:T(1,128)S(1)}, u32[]{:S(2)}, u32[]{:S(2)}) collective-permute-start(s32[1,768]{1,0:T(1,128)S(1)} %bitcast.61), channel_id=1, source_target_pairs={{0,32},{16,48},{32,0},{48,16},{1,33},{17,49},{33,1},{49,17},{2,34}... | collective-permute-start | bytes 9224 | tf_op jit(solution)/shard_map/ppermute | solution.py:170
  26.2 2.7 collective-permute-start.3
  40.1 8.8 %collective-permute-start.4 = (bf16[192,768]{1,0:T(8,128)(2,1)}, bf16[192,768]{1,0:T(8,128)(2,1)S(1)}, u32[]{:S(2)}, u32[]{:S(2)}) collective-permute-start(bf16[192,768]{1,0:T(8,128)(2,1)} %get-tuple-element.91), channel_id=1, source_target_pairs={{0,16},{16,32},{32,48},{48,0},{1,17},{17,33},{33,49},{49,1},{2,18}... | collective-permute-start | bytes 884744 | tf_op jit(solution)/shard_map/ppermute | solution.py:170
  42.1 12.1 %collective-permute-start.5 = (bf16[192,768]{1,0:T(8,128)(2,1)S(1)}, bf16[192,768]{1,0:T(8,128)(2,1)S(1)}, u32[]{:S(2)}, u32[]{:S(2)}) collective-permute-start(bf16[192,768]{1,0:T(8,128)(2,1)S(1)} %get-tuple-element.92), channel_id=1, source_target_pairs={{0,32},{16,48},{32,0},{48,16},{1,33},{17,49},{33,1},{49,17},{2,34}... | collective-permute-start | bytes 884744 | tf_op jit(solution)/shard_map/ppermute | solution.py:170
  45.8 8.4 %collective-permute-start.6 = (bf16[192,768]{1,0:T(8,128)(2,1)S(1)}, bf16[192,768]{1,0:T(8,128)(2,1)S(1)}, u32[]{:S(2)}, u32[]{:S(2)}) collective-permute-start(bf16[192,768]{1,0:T(8,128)(2,1)S(1)} %get-tuple-element.93), channel_id=1, source_target_pairs={{0,48},{16,0},{32,16},{48,32},{1,49},{17,1},{33,17},{49,33},{2,50}... | collective-permute-start | bytes 884744 | tf_op jit(solution)/shard_map/ppermute | solution.py:170
  46.2 216.1 %reduce-scatter.4.cloned.1.call-start = ((), (), s32[]{:S(2)}) async-start(), calls=%async_computation.6 | async-start | bytes 3481600
  62.3 17.3 %collective-permute-start.7 = (bf16[64,768]{1,0:T(8,128)(2,1)S(1)}, bf16[64,768]{1,0:T(8,128)(2,1)S(1)}, u32[]{:S(2)}, u32[]{:S(2)}) collective-permute-start(bf16[64,768]{1,0:T(8,128)(2,1)S(1)} %get-tuple-element.99), channel_id=1, source_target_pairs={{0,16},{16,32},{32,48},{48,0},{1,17},{17,33},{33,49},{49,1},{2,18}... | collective-permute-start | bytes 294920 | tf_op jit(solution)/shard_map/ppermute | solution.py:170
  66.2 13.4 %collective-permute-start.8 = (bf16[64,768]{1,0:T(8,128)(2,1)S(1)}, bf16[64,768]{1,0:T(8,128)(2,1)S(1)}, u32[]{:S(2)}, u32[]{:S(2)}) collective-permute-start(bf16[64,768]{1,0:T(8,128)(2,1)S(1)} %get-tuple-element.100), channel_id=1, source_target_pairs={{0,32},{16,48},{32,0},{48,16},{1,33},{17,49},{33,1},{49,17},{2,34}... | collective-permute-start | bytes 294920 | tf_op jit(solution)/shard_map/ppermute | solution.py:170
  66.2 13.4 %collective-permute-start.9 = (bf16[64,768]{1,0:T(8,128)(2,1)S(1)}, bf16[64,768]{1,0:T(8,128)(2,1)S(1)}, u32[]{:S(2)}, u32[]{:S(2)}) collective-permute-start(bf16[64,768]{1,0:T(8,128)(2,1)S(1)} %get-tuple-element.101), channel_id=1, source_target_pairs={{0,48},{16,0},{32,16},{48,32},{1,49},{17,1},{33,17},{49,33},{2,50}... | collective-permute-start | bytes 294920 | tf_op jit(solution)/shard_map/ppermute | solution.py:170
  71.8 7.9 %copy-start = (bf16[7680,256]{1,0:T(8,128)(2,1)S(1)}, bf16[7680,256]{1,0:T(8,128)(2,1)}, u32[]{:S(2)}) copy-start(bf16[7680,256]{1,0:T(8,128)(2,1)} %all-gather.5.cloned.1.call-done) | copy-start | bytes 11796484
  79.6 8.3 %copy-start.5 = (bf16[3,1,256,512]{3,2,1,0:T(8,128)(2,1)S(1)}, bf16[3,1,256,512]{3,2,1,0:T(8,128)(2,1)}, u32[]{:S(2)}) copy-start(bf16[3,1,256,512]{3,2,1,0:T(8,128)(2,1)} %param.11) | copy-start | bytes 2359300
  82.5 5.4 %collective-permute-start.10 = (f32[768,512]{1,0:T(8,128)}, f32[768,512]{1,0:T(8,128)}, u32[]{:S(2)}, u32[]{:S(2)}) collective-permute-start(f32[768,512]{1,0:T(8,128)} %get-tuple-element.105.refs_1_), channel_id=1, source_target_pairs={{0,64},{64,0},{1,65},{65,1},{2,66},{66,2},{3,67},{67,3},{4,68},{68... | collective-permute-start | bytes 4718600 | tf_op jit(solution)/shard_map/ppermute | solution.py:174
  95.8 11.6 %collective-permute-start.11 = (bf16[256,768]{1,0:T(8,128)(2,1)S(1)}, bf16[256,768]{1,0:T(8,128)(2,1)S(1)}, u32[]{:S(2)}, u32[]{:S(2)}) collective-permute-start(bf16[256,768]{1,0:T(8,128)(2,1)S(1)} %get-tuple-element.108), channel_id=1, source_target_pairs={{0,16},{16,32},{32,48},{48,0},{1,17},{17,33},{33,49},{49,1},{2,18}... | collective-permute-start | bytes 1179656 | tf_op jit(solution)/shard_map/ppermute | solution.py:170
  96.6 19.2 %collective-permute-start.12 = (bf16[256,768]{1,0:T(8,128)(2,1)S(1)}, bf16[256,768]{1,0:T(8,128)(2,1)S(1)}, u32[]{:S(2)}, u32[]{:S(2)}) collective-permute-start(bf16[256,768]{1,0:T(8,128)(2,1)S(1)} %get-tuple-element.109), channel_id=1, source_target_pairs={{0,32},{16,48},{32,0},{48,16},{1,33},{17,49},{33,1},{49,17},{2,34}... | collective-permute-start | bytes 1179656 | tf_op jit(solution)/shard_map/ppermute | solution.py:170
  98.5 17.6 %collective-permute-start.13 = (bf16[256,768]{1,0:T(8,128)(2,1)S(1)}, bf16[256,768]{1,0:T(8,128)(2,1)S(1)}, u32[]{:S(2)}, u32[]{:S(2)}) collective-permute-start(bf16[256,768]{1,0:T(8,128)(2,1)S(1)} %get-tuple-element.110), channel_id=1, source_target_pairs={{0,48},{16,0},{32,16},{48,32},{1,49},{17,1},{33,17},{49,33},{2,50}... | collective-permute-start | bytes 1179656 | tf_op jit(solution)/shard_map/ppermute | solution.py:170
  130.0 23.6 %copy-start.13 = (bf16[256,768]{1,0:T(8,128)(2,1)}, bf16[256,768]{1,0:T(8,128)(2,1)S(1)}, u32[]{:S(2)}) copy-start(bf16[256,768]{1,0:T(8,128)(2,1)S(1)} %get-tuple-element.111.refs_0_) | copy-start | bytes 1179652
  130.0 23.6 %collective-permute-start.14 = (bf16[256,768]{1,0:T(8,128)(2,1)}, bf16[256,768]{1,0:T(8,128)(2,1)S(1)}, u32[]{:S(2)}, u32[]{:S(2)}) collective-permute-start(bf16[256,768]{1,0:T(8,128)(2,1)} %get-tuple-element.112), channel_id=1, source_target_pairs={{0,16},{16,32},{32,48},{48,0},{1,17},{17,33},{33,49},{49,1},{2,18}... | collective-permute-start | bytes 1179656 | tf_op jit(solution)/shard_map/ppermute | solution.py:170
  132.2 21.4 %collective-permute-start.15 = (bf16[256,768]{1,0:T(8,128)(2,1)}, bf16[256,768]{1,0:T(8,128)(2,1)}, u32[]{:S(2)}, u32[]{:S(2)}) collective-permute-start(bf16[256,768]{1,0:T(8,128)(2,1)} %get-tuple-element.113), channel_id=1, source_target_pairs={{0,32},{16,48},{32,0},{48,16},{1,33},{17,49},{33,1},{49,17},{2,34}... | collective-permute-start | bytes 1179656 | tf_op jit(solution)/shard_map/ppermute | solution.py:170
  134.7 19.0 %collective-permute-start.16 = (bf16[256,768]{1,0:T(8,128)(2,1)}, bf16[256,768]{1,0:T(8,128)(2,1)}, u32[]{:S(2)}, u32[]{:S(2)}) collective-permute-start(bf16[256,768]{1,0:T(8,128)(2,1)} %get-tuple-element.114), channel_id=1, source_target_pairs={{0,48},{16,0},{32,16},{48,32},{1,49},{17,1},{33,17},{49,33},{2,50}... | collective-permute-start | bytes 1179656 | tf_op jit(solution)/shard_map/ppermute | solution.py:170
  135.9 8.8 %copy-start.24 = (bf16[768,512]{1,0:T(8,128)(2,1)S(1)}, bf16[768,512]{1,0:T(8,128)(2,1)}, u32[]{:S(2)}) copy-start(bf16[768,512]{1,0:T(8,128)(2,1)} %get-tuple-element.116.mlp_in) | copy-start | bytes 2359300
  144.6 9.1 %copy-start.2 = (bf16[7680,256]{1,0:T(8,128)(2,1)S(1)}, bf16[7680,256]{1,0:T(8,128)(2,1)}, u32[]{:S(2)}) copy-start(bf16[7680,256]{1,0:T(8,128)(2,1)} %all-gather.5.cloned.1.call-done) | copy-start | bytes 11796484
  144.6 9.1 %copy-start.7 = (bf16[768,512]{1,0:T(8,128)(2,1)S(1)}, bf16[768,512]{1,0:T(8,128)(2,1)}, u32[]{:S(2)}) copy-start(bf16[768,512]{1,0:T(8,128)(2,1)} %get-tuple-element.106.refs_9_.states) | copy-start | bytes 2359300
  153.7 4.8 %copy-start.15 = (bf16[256,768]{1,0:T(8,128)(2,1)}, bf16[256,768]{1,0:T(8,128)(2,1)S(1)}, u32[]{:S(2)}) copy-start(bf16[256,768]{1,0:T(8,128)(2,1)S(1)} %collective-permute-done.14.refs_1_) | copy-start | bytes 1179652
  153.7 7.5 %copy-start.21 = (bf16[768,512]{1,0:T(8,128)(2,1)S(1)}, bf16[768,512]{1,0:T(8,128)(2,1)}, u32[]{:S(2)}) copy-start(bf16[768,512]{1,0:T(8,128)(2,1)} %get-tuple-element.124.attn_in) | copy-start | bytes 2359300
  158.4 2.8 collective-permute-start.19
  164.7 3.7 %collective-permute-start.18 = (f32[768,512]{1,0:T(8,128)}, f32[768,512]{1,0:T(8,128)S(1)}, u32[]{:S(2)}, u32[]{:S(2)}) collective-permute-start(f32[768,512]{1,0:T(8,128)} %get-tuple-element.123.own), channel_id=1, source_target_pairs={{0,64},{64,0},{1,65},{65,1},{2,66},{66,2},{3,67},{67,3},{4,68},{68... | collective-permute-start | bytes 4718600 | tf_op jit(solution)/shard_map/ppermute | solution.py:174
  165.2 7.5 %copy-start.3 = (bf16[7680,256]{1,0:T(8,128)(2,1)S(1)}, bf16[7680,256]{1,0:T(8,128)(2,1)}, u32[]{:S(2)}) copy-start(bf16[7680,256]{1,0:T(8,128)(2,1)} %all-gather.5.cloned.1.call-done) | copy-start | bytes 11796484
  165.2 12.9 %collective-permute-start.23 = (bf16[256,768]{1,0:T(8,128)(2,1)}, bf16[256,768]{1,0:T(8,128)(2,1)S(1)}, u32[]{:S(2)}, u32[]{:S(2)}) collective-permute-start(bf16[256,768]{1,0:T(8,128)(2,1)} %get-tuple-element.137.refs_0_), channel_id=1, source_target_pairs={{0,64},{64,0},{1,65},{65,1},{2,66},{66,2},{3,67},{67,3},{4,68},{68... | collective-permute-start | bytes 1179656 | tf_op jit(solution)/shard_map/ppermute | solution.py:174
  172.7 5.4 %copy-start.32 = (bf16[768,512]{1,0:T(8,128)(2,1)S(1)}, bf16[768,512]{1,0:T(8,128)(2,1)}, u32[]{:S(2)}) copy-start(bf16[768,512]{1,0:T(8,128)(2,1)} %get-tuple-element.103.mlp_in) | copy-start | bytes 2359300
  174.3 21.9 %collective-permute-start.20 = (bf16[64,768]{1,0:T(8,128)(2,1)S(1)}, bf16[64,768]{1,0:T(8,128)(2,1)S(1)}, u32[]{:S(2)}, u32[]{:S(2)}) collective-permute-start(bf16[64,768]{1,0:T(8,128)(2,1)S(1)} %get-tuple-element.131), channel_id=1, source_target_pairs={{0,16},{16,32},{32,48},{48,0},{1,17},{17,33},{33,49},{49,1},{2,18}... | collective-permute-start | bytes 294920 | tf_op jit(solution)/shard_map/ppermute | solution.py:170
  175.6 20.7 %collective-permute-start.21 = (bf16[64,768]{1,0:T(8,128)(2,1)S(1)}, bf16[64,768]{1,0:T(8,128)(2,1)S(1)}, u32[]{:S(2)}, u32[]{:S(2)}) collective-permute-start(bf16[64,768]{1,0:T(8,128)(2,1)S(1)} %get-tuple-element.132), channel_id=1, source_target_pairs={{0,32},{16,48},{32,0},{48,16},{1,33},{17,49},{33,1},{49,17},{2,34}... | collective-permute-start | bytes 294920 | tf_op jit(solution)/shard_map/ppermute | solution.py:170
  176.1 20.1 %collective-permute-start.22 = (bf16[64,768]{1,0:T(8,128)(2,1)S(1)}, bf16[64,768]{1,0:T(8,128)(2,1)S(1)}, u32[]{:S(2)}, u32[]{:S(2)}) collective-permute-start(bf16[64,768]{1,0:T(8,128)(2,1)S(1)} %get-tuple-element.133), channel_id=1, source_target_pairs={{0,48},{16,0},{32,16},{48,32},{1,49},{17,1},{33,17},{49,33},{2,50}... | collective-permute-start | bytes 294920 | tf_op jit(solution)/shard_map/ppermute | solution.py:170
  190.0 40.7 %all-to-all-start.1 = ((bf16[16,288,256]{2,1,0:T(8,128)(2,1)}), bf16[16,288,256]{2,1,0:T(8,128)(2,1)}, u32[]{:S(2)}, u32[]{:S(2)}) async-start(bf16[16,288,256]{2,1,0:T(8,128)(2,1)} %copy-done.10), calls=%async_computation.1 | async-start | bytes 4718592 | tf_op jit(solution)/shard_map/all_to_all | solution.py:178
  196.3 14.0 %copy-start.4 = (bf16[7680,256]{1,0:T(8,128)(2,1)S(1)}, bf16[7680,256]{1,0:T(8,128)(2,1)}, u32[]{:S(2)}) copy-start(bf16[7680,256]{1,0:T(8,128)(2,1)} %all-gather.5.cloned.1.call-done) | copy-start | bytes 11796484
  196.3 14.0 %copy-start.12 = (f32[768,512]{1,0:T(8,128)S(1)}, f32[768,512]{1,0:T(8,128)}, u32[]{:S(2)}) copy-start(f32[768,512]{1,0:T(8,128)} %copy-done.11) | copy-start | bytes 4718596
  196.3 13.9 %copy-start.14 = (bf16[256,768]{1,0:T(8,128)(2,1)S(1)}, bf16[256,768]{1,0:T(8,128)(2,1)}, u32[]{:S(2)}) copy-start(bf16[256,768]{1,0:T(8,128)(2,1)} %copy-done.13) | copy-start | bytes 1179652
  196.3 13.9 %copy-start.16 = (bf16[256,768]{1,0:T(8,128)(2,1)S(1)}, bf16[256,768]{1,0:T(8,128)(2,1)}, u32[]{:S(2)}) copy-start(bf16[256,768]{1,0:T(8,128)(2,1)} %copy-done.15) | copy-start | bytes 1179652
  207.0 9.5 %collective-permute-start.24 = (bf16[192,768]{1,0:T(8,128)(2,1)S(1)}, bf16[192,768]{1,0:T(8,128)(2,1)S(1)}, u32[]{:S(2)}, u32[]{:S(2)}) collective-permute-start(bf16[192,768]{1,0:T(8,128)(2,1)S(1)} %get-tuple-element.147), channel_id=1, source_target_pairs={{0,16},{16,32},{32,48},{48,0},{1,17},{17,33},{33,49},{49,1},{2,18}... | collective-permute-start | bytes 884744 | tf_op jit(solution)/shard_map/ppermute | solution.py:170
  207.1 13.8 %collective-permute-start.25 = (bf16[192,768]{1,0:T(8,128)(2,1)S(1)}, bf16[192,768]{1,0:T(8,128)(2,1)S(1)}, u32[]{:S(2)}, u32[]{:S(2)}) collective-permute-start(bf16[192,768]{1,0:T(8,128)(2,1)S(1)} %get-tuple-element.148), channel_id=1, source_target_pairs={{0,32},{16,48},{32,0},{48,16},{1,33},{17,49},{33,1},{49,17},{2,34}... | collective-permute-start | bytes 884744 | tf_op jit(solution)/shard_map/ppermute | solution.py:170
  209.0 14.0 %collective-permute-start.26 = (bf16[192,768]{1,0:T(8,128)(2,1)S(1)}, bf16[192,768]{1,0:T(8,128)(2,1)S(1)}, u32[]{:S(2)}, u32[]{:S(2)}) collective-permute-start(bf16[192,768]{1,0:T(8,128)(2,1)S(1)} %get-tuple-element.149), channel_id=1, source_target_pairs={{0,48},{16,0},{32,16},{48,32},{1,49},{17,1},{33,17},{49,33},{2,50}... | collective-permute-start | bytes 884744 | tf_op jit(solution)/shard_map/ppermute | solution.py:170
  210.2 12.8 %copy-start.19 = (f32[768,512]{1,0:T(8,128)S(1)}, f32[768,512]{1,0:T(8,128)}, u32[]{:S(2)}) copy-start(f32[768,512]{1,0:T(8,128)} %copy-done.18) | copy-start | bytes 4718596
  213.8 40.8 %collective-permute-start.17 = (f32[768,512]{1,0:T(8,128)}, f32[768,512]{1,0:T(8,128)}, u32[]{:S(2)}, u32[]{:S(2)}) collective-permute-start(f32[768,512]{1,0:T(8,128)} %get-tuple-element.119), channel_id=1, source_target_pairs={{0,64},{64,0},{1,65},{65,1},{2,66},{66,2},{3,67},{67,3},{4,68},{68... | collective-permute-start | bytes 4718600 | tf_op jit(solution)/shard_map/ppermute | solution.py:174
  223.1 5.2 %copy-start.30 = (bf16[768,512]{1,0:T(8,128)(2,1)S(1)}, bf16[768,512]{1,0:T(8,128)(2,1)}, u32[]{:S(2)}) copy-start(bf16[768,512]{1,0:T(8,128)(2,1)} %get-tuple-element.152.attn_in) | copy-start | bytes 2359300
  226.7 28.6 %collective-permute-start.27 = (f32[768,512]{1,0:T(8,128)}, f32[768,512]{1,0:T(8,128)}, u32[]{:S(2)}, u32[]{:S(2)}) collective-permute-start(f32[768,512]{1,0:T(8,128)} %get-tuple-element.151.own), channel_id=1, source_target_pairs={{0,64},{64,0},{1,65},{65,1},{2,66},{66,2},{3,67},{67,3},{4,68},{68... | collective-permute-start | bytes 4718600 | tf_op jit(solution)/shard_map/ppermute | solution.py:174
  232.7 34.3 %copy-start.9 = (bf16[768,512]{1,0:T(8,128)(2,1)S(1)}, bf16[768,512]{1,0:T(8,128)(2,1)}, u32[]{:S(2)}) copy-start(bf16[768,512]{1,0:T(8,128)(2,1)} %get-tuple-element.106.refs_9_.states) | copy-start | bytes 2359300
  232.7 20.6 %all-to-all-start.2 = ((bf16[16,112,256]{2,1,0:T(8,128)(2,1)}), bf16[16,112,256]{2,1,0:T(8,128)(2,1)}, u32[]{:S(2)}, u32[]{:S(2)}) async-start(bf16[16,112,256]{2,1,0:T(8,128)(2,1)} %shard_map.171), calls=%async_computation.2 | async-start | bytes 1835008 | tf_op jit(solution)/shard_map/all_to_all | solution.py:178
  239.3 19.6 %collective-permute-start.31 = (bf16[288,256]{1,0:T(8,128)(2,1)S(1)}, bf16[288,256]{1,0:T(8,128)(2,1)S(1)}, u32[]{:S(2)}, u32[]{:S(2)}) collective-permute-start(bf16[288,256]{1,0:T(8,128)(2,1)S(1)} %reduce_sum.24.refs_4_), channel_id=1, source_target_pairs={{0,16},{16,32},{32,48},{48,0},{1,17},{17,33},{33,49},{49,1},{2,18}... | collective-permute-start | bytes 442376 | tf_op jit(solution)/shard_map/ppermute | solution.py:170
  239.9 19.0 %collective-permute-start.32 = (bf16[288,256]{1,0:T(8,128)(2,1)S(1)}, bf16[288,256]{1,0:T(8,128)(2,1)S(1)}, u32[]{:S(2)}, u32[]{:S(2)}) collective-permute-start(bf16[288,256]{1,0:T(8,128)(2,1)S(1)} %reduce_sum.24.refs_4_), channel_id=1, source_target_pairs={{0,32},{16,48},{32,0},{48,16},{1,33},{17,49},{33,1},{49,17},{2,34}... | collective-permute-start | bytes 442376 | tf_op jit(solution)/shard_map/ppermute | solution.py:170
  243.0 20.3 %collective-permute-start.33 = (bf16[288,256]{1,0:T(8,128)(2,1)S(1)}, bf16[288,256]{1,0:T(8,128)(2,1)S(1)}, u32[]{:S(2)}, u32[]{:S(2)}) collective-permute-start(bf16[288,256]{1,0:T(8,128)(2,1)S(1)} %reduce_sum.24.refs_4_), channel_id=1, source_target_pairs={{0,48},{16,0},{32,16},{48,32},{1,49},{17,1},{33,17},{49,33},{2,50}... | collective-permute-start | bytes 442376 | tf_op jit(solution)/shard_map/ppermute | solution.py:170
  254.6 11.7 %collective-permute-start.34 = (bf16[112,256]{1,0:T(8,128)(2,1)S(1)}, bf16[112,256]{1,0:T(8,128)(2,1)S(1)}, u32[]{:S(2)}, u32[]{:S(2)}) collective-permute-start(bf16[112,256]{1,0:T(8,128)(2,1)S(1)} %reduce_sum.25.refs_8_), channel_id=1, source_target_pairs={{0,16},{16,32},{32,48},{48,0},{1,17},{17,33},{33,49},{49,1},{2,18}... | collective-permute-start | bytes 172040 | tf_op jit(solution)/shard_map/ppermute | solution.py:170
  255.3 18.4 %collective-permute-start.35 = (bf16[112,256]{1,0:T(8,128)(2,1)S(1)}, bf16[112,256]{1,0:T(8,128)(2,1)S(1)}, u32[]{:S(2)}, u32[]{:S(2)}) collective-permute-start(bf16[112,256]{1,0:T(8,128)(2,1)S(1)} %reduce_sum.25.refs_8_), channel_id=1, source_target_pairs={{0,32},{16,48},{32,0},{48,16},{1,33},{17,49},{33,1},{49,17},{2,34}... | collective-permute-start | bytes 172040 | tf_op jit(solution)/shard_map/ppermute | solution.py:170
  258.9 14.8 %collective-permute-start.36 = (bf16[112,256]{1,0:T(8,128)(2,1)S(1)}, bf16[112,256]{1,0:T(8,128)(2,1)S(1)}, u32[]{:S(2)}, u32[]{:S(2)}) collective-permute-start(bf16[112,256]{1,0:T(8,128)(2,1)S(1)} %reduce_sum.25.refs_8_), channel_id=1, source_target_pairs={{0,48},{16,0},{32,16},{48,32},{1,49},{17,1},{33,17},{49,33},{2,50}... | collective-permute-start | bytes 172040 | tf_op jit(solution)/shard_map/ppermute | solution.py:170
  262.3 8.0 %copy-start.17 = (f32[768,512]{1,0:T(8,128)S(1)}, f32[768,512]{1,0:T(8,128)}, u32[]{:S(2)}) copy-start(f32[768,512]{1,0:T(8,128)} %get-tuple-element.151.own) | copy-start | bytes 4718596
  262.3 11.4 %collective-permute-start.28 = (bf16[400,256]{1,0:T(8,128)(2,1)}, bf16[400,256]{1,0:T(8,128)(2,1)S(1)}, u32[]{:S(2)}, u32[]{:S(2)}) collective-permute-start(bf16[400,256]{1,0:T(8,128)(2,1)} %bitcast.66), channel_id=1, source_target_pairs={{0,16},{16,32},{32,48},{48,0},{1,17},{17,33},{33,49},{49,1},{2,18}... | collective-permute-start | bytes 614408 | tf_op jit(solution)/shard_map/ppermute | solution.py:170
  263.9 9.8 %collective-permute-start.29 = (bf16[400,256]{1,0:T(8,128)(2,1)}, bf16[400,256]{1,0:T(8,128)(2,1)S(1)}, u32[]{:S(2)}, u32[]{:S(2)}) collective-permute-start(bf16[400,256]{1,0:T(8,128)(2,1)} %bitcast.67), channel_id=1, source_target_pairs={{0,32},{16,48},{32,0},{48,16},{1,33},{17,49},{33,1},{49,17},{2,34}... | collective-permute-start | bytes 614408 | tf_op jit(solution)/shard_map/ppermute | solution.py:170
  266.3 8.3 %collective-permute-start.30 = (bf16[400,256]{1,0:T(8,128)(2,1)}, bf16[400,256]{1,0:T(8,128)(2,1)S(1)}, u32[]{:S(2)}, u32[]{:S(2)}) collective-permute-start(bf16[400,256]{1,0:T(8,128)(2,1)} %bitcast.68), channel_id=1, source_target_pairs={{0,48},{16,0},{32,16},{48,32},{1,49},{17,1},{33,17},{49,33},{2,50}... | collective-permute-start | bytes 614408 | tf_op jit(solution)/shard_map/ppermute | solution.py:170
  275.5 3.3 %collective-permute-start.37 = (bf16[400,256]{1,0:T(8,128)(2,1)S(1)}, bf16[400,256]{1,0:T(8,128)(2,1)S(1)}, u32[]{:S(2)}, u32[]{:S(2)}) collective-permute-start(bf16[400,256]{1,0:T(8,128)(2,1)S(1)} %get-tuple-element.158), channel_id=1, source_target_pairs={{0,64},{64,0},{1,65},{65,1},{2,66},{66,2},{3,67},{67,3},{4,68},{68... | collective-permute-start | bytes 614408 | tf_op jit(solution)/shard_map/ppermute | solution.py:174
  (15 other events, 27.1 us)
Sparse Core Ops, SparseCore 0:
  14.2 56.3 all-gather.4
  73.3 43.6 all-gather.6
  164.8 97.3 reduce-scatter.3

commit v4 on v3

--- a/solution.py
+++ b/solution.py
@@ -744,8 +744,12 @@
     )[0]
 
 
+def add_up(got):
+    return jnp.sum(got.astype(F32), axis=0).astype(BF)
+
+
 def scatter_sum(pack):
-    return jnp.sum(to_owners(pack).astype(F32), axis=0).astype(BF)
+    return add_up(to_owners(pack))
 
 
 def choose_body(place, *refs):
@@ -903,7 +907,7 @@
             )
             came = after(came, pack)
             sent = attend_back(place, came, places, kept, heads_out, log_total)
-            sum_a = scatter_sum(pack)
+            got_a = to_owners(pack)
             came = regroup(sent)
         through, mixed, norm_sums, *heads_of = mixed_back(
             place, came, qkv_of[layer], norms[layer], turns, states, mlp_grad
@@ -912,10 +916,10 @@
             pack = weight_back(place, attn_in, mixed, norm_sums, (pack, heads_of[0], swap_core(heads_of[0]), grad))
             total = lax.psum_scatter(pack, "shard", scatter_dimension=0, tiled=False)
         else:
-            pack, sum_a = lax.optimization_barrier(
-                (weight_back(place, attn_in, mixed, norm_sums), sum_a)
+            pack, got_a = lax.optimization_barrier(
+                (weight_back(place, attn_in, mixed, norm_sums), got_a)
             )
-            pieces_a = regroup([sum_a] * 4)
+            pieces_a = regroup([add_up(got_a)] * 4)
             pieces_b = regroup([scatter_sum(pack)] * 4)
         swapped = swap_core(through)
         if layer == 1:

time: 289 us -> 288 us (level)
  transfers between devices with their start and end apart: 44 -> 44, of which waited for: 21 -> 20; matrix products, arithmetic and copies ran while one was open for 3% -> 3% of each run, Pallas kernels for 33% -> 33%
where the time goes in v4:
time: 288 us; the launch traced here: 287 us
  Pallas kernels  108 us (38%)
  starting transfers between devices  78.8 us (27%)
  waiting for transfers between devices  62.3 us (22%)
  local copies, waits for them, and re-layouts  14.8 us (5%)
  between operations  14.3 us (5%)
  other arithmetic  8.56 us (3%)
    pallas_call x22, Pallas kernels, call(): pl.pallas_call(body, out_shape=[(pltpu.HBM if out[4:] else struct)(out[0]...  108 us
    ppermute x30, starting transfers between devices, shift_z(): return lax.ppermute(value, 'seq', [(z, (z + step) % 4) for z in range(4)])  46.3 us
    ppermute x30, waiting for transfers between devices, shift_z(): return lax.ppermute(value, 'seq', [(z, (z + step) % 4) for z in range(4)])  33.1 us
    all_to_all x3, starting transfers between devices, to_owners(): return lax.all_to_all(pack, 'shard', 0, 0, tiled=True)  19.5 us
    all_to_all x3, waiting for transfers between devices, to_owners(): return lax.all_to_all(pack, 'shard', 0, 0, tiled=True)  15.1 us
    unnamed x70, local copies, waits for them, and re-layouts  13.8 us
    ppermute x8, starting transfers between devices, swap_core(): return lax.ppermute(value, 'section', [(0, 1), (1, 0)])  12.9 us
    ppermute x8, waiting for transfers between devices, swap_core(): return lax.ppermute(value, 'section', [(0, 1), (1, 0)])  8.99 us
  transfers between devices with their start and end apart: 44, of which 20 were waited for; matrix products, arithmetic and copies ran while one was open for 3% of the time, Pallas kernels for 33%

profile of v4, /device:TPU:1, one launch (start us, length us, event | category | flops | bytes accessed | tf_op | source)
XLA Modules:
  0.0 286.6 jit_solution(7433976870173054261)
XLA Ops:
  8.1 1.7 shard_map.152
  9.8 1.5 collective-permute-start
  12.4 1.7 shard_map.153
  14.1 7.0 %all-to-all-start = ((bf16[16,112,256]{2,1,0:T(8,128)(2,1)}), bf16[16,112,256]{2,1,0:T(8,128)(2,1)S(1)}, u32[]{:S(2)}, u32[]{:S(2)}) async-start(bf16[16,112,256]{2,1,0:T(8,128)(2,1)} %get-tuple-element.88), calls=%async_computation | async-start | bytes 1835008 | tf_op jit(solution)/shard_map/all_to_all | solution.py:178
  21.2 1.7 collective-permute-start.1
  22.9 3.3 %collective-permute-start.2 = (s32[1,768]{1,0:T(1,128)S(1)}, s32[1,768]{1,0:T(1,128)S(1)}, u32[]{:S(2)}, u32[]{:S(2)}) collective-permute-start(s32[1,768]{1,0:T(1,128)S(1)} %bitcast.61), channel_id=1, source_target_pairs={{0,32},{16,48},{32,0},{48,16},{1,33},{17,49},{33,1},{49,17},{2,34}... | collective-permute-start | bytes 9224 | tf_op jit(solution)/shard_map/ppermute | solution.py:170
  27.3 1.6 collective-permute-done.3.refs_7_
  28.9 6.4 %all-to-all-done.refs_1_.refs_2_.refs_3_.refs_4_.refs_5_.refs_6_ = bf16[16,112,256]{2,1,0:T(8,128)(2,1)S(1)} async-done(((bf16[16,112,256]{2,1,0:T(8,128)(2,1)}), bf16[16,112,256]{2,1,0:T(8,128)(2,1)S(1)}, u32[]{:S(2)}, u32[]{:S(2)}) %all-to-all-start) | async-done | bytes 917536 | tf_op jit(solution)/shard_map/all_to_all | solution.py:178
  35.6 3.8 %shard_map.154 = (bf16[192,768]{1,0:T(8,128)(2,1)S(1)}, bf16[192,768]{1,0:T(8,128)(2,1)}, bf16[192,768]{1,0:T(8,128)(2,1)S(1)}, bf16[192,768]{1,0:T(8,128)(2,1)S...) custom-call(s32[4]{0:T(128)S(1)} %pad_add_fusion.place, bf16[768,512]{1,0:T(8,128)(2,1)S(1)} %bitcast.56, ...), custom_call_target="tpu_custom_call" | custom-call | flops 1200000000 | bytes 6000000 | tf_op jit(solution)/shard_map/pallas_call | solution.py:42
  40.1 2.0 collective-permute-start.4
  42.1 3.7 %collective-permute-start.5 = (bf16[192,768]{1,0:T(8,128)(2,1)S(1)}, bf16[192,768]{1,0:T(8,128)(2,1)S(1)}, u32[]{:S(2)}, u32[]{:S(2)}) collective-permute-start(bf16[192,768]{1,0:T(8,128)(2,1)S(1)} %get-tuple-element.92), channel_id=1, source_target_pairs={{0,32},{16,48},{32,0},{48,16},{1,33},{17,49},{33,1},{49,17},{2,34}... | collective-permute-start | bytes 884744 | tf_op jit(solution)/shard_map/ppermute | solution.py:170
  46.2 2.7 collective-permute-done.4.refs_1_
  48.9 5.3 %collective-permute-done.5.refs_2_ = bf16[192,768]{1,0:T(8,128)(2,1)S(1)} collective-permute-done((bf16[192,768]{1,0:T(8,128)(2,1)S(1)}, bf16[192,768]{1,0:T(8,128)(2,1)S(1)}, u32[]{:S(2)}, u32[]{:S(2)}) %collective-permute-start.5) | collective-permute-done | bytes 294944 | tf_op jit(solution)/shard_map/ppermute | solution.py:170
  55.2 7.1 %shard_map.155 = (bf16[64,768]{1,0:T(8,128)(2,1)S(1)}, bf16[64,768]{1,0:T(8,128)(2,1)S(1)}, bf16[64,768]{1,0:T(8,128)(2,1)S(1)}, bf16[64,768]{1,0:T(8,128)(2,1)S...) custom-call(s32[4]{0:T(128)S(1)} %pad_add_fusion.place, ...), custom_call_target="tpu_custom_call" | custom-call | flops 8000000000 | bytes 4000000 | tf_op jit(solution)/shard_map/pallas_call | solution.py:42
  62.3 3.9 %collective-permute-start.7 = (bf16[64,768]{1,0:T(8,128)(2,1)S(1)}, bf16[64,768]{1,0:T(8,128)(2,1)S(1)}, u32[]{:S(2)}, u32[]{:S(2)}) collective-permute-start(bf16[64,768]{1,0:T(8,128)(2,1)S(1)} %get-tuple-element.99), channel_id=1, source_target_pairs={{0,16},{16,32},{32,48},{48,0},{1,17},{17,33},{33,49},{49,1},{2,18}... | collective-permute-start | bytes 294920 | tf_op jit(solution)/shard_map/ppermute | solution.py:170
  66.2 2.4 collective-permute-start.9
  68.6 2.0 all-gather.5.cloned.1.call-done
  71.8 7.8 %shard_map.156 = (f32[768,512]{1,0:T(8,128)S(1)}, bf16[768,1024]{1,0:T(8,128)(2,1)}, f32[768,1024]{1,0:T(8,128)}) custom-call(s32[4]{0:T(128)S(1)} %pad_add_fusion.place, bf16[768,512]{1,0:T(8,128)(2,1)S(1)} %copy-done.31, bf16[16,480,256]{2,1,0:T(8,128)(2,1)} %bitcast.38, bf16[16,480,256]{2,1,0:T(8,128)(2,1)} %bitcast.39), custom_call_target="tpu_custom_call" | custom-call | flops 6000000000 | bytes 12000000 | tf_op jit(solution)/shard_map/pallas_call | solution.py:42
  79.6 2.8 shard_map.157
  82.5 2.1 collective-permute-start.10
  84.6 3.3 %collective-permute-done.10.refs_2_ = f32[768,512]{1,0:T(8,128)} collective-permute-done((f32[768,512]{1,0:T(8,128)}, f32[768,512]{1,0:T(8,128)}, u32[]{:S(2)}, u32[]{:S(2)}) %collective-permute-start.10) | collective-permute-done | bytes 1572896 | tf_op jit(solution)/shard_map/ppermute | solution.py:174
  87.9 2.1 copy-done.1
  90.0 5.8 %shard_map.158 = (bf16[256,768]{1,0:T(8,128)(2,1)S(1)}, bf16[256,768]{1,0:T(8,128)(2,1)S(1)}, bf16[256,768]{1,0:T(8,128)(2,1)S(1)}, bf16[256,768]{1,0:T(8,128)(2...) custom-call(s32[4]{0:T(128)S(1)} %pad_add_fusion.place, ...), custom_call_target="tpu_custom_call" | custom-call | flops 1200000000 | bytes 6000000 | tf_op jit(solution)/shard_map/pallas_call | solution.py:42
  96.6 1.9 collective-permute-start.12
  99.6 7.7 %collective-permute-done.11.refs_1_ = bf16[256,768]{1,0:T(8,128)(2,1)S(1)} collective-permute-done((bf16[256,768]{1,0:T(8,128)(2,1)S(1)}, bf16[256,768]{1,0:T(8,128)(2,1)S(1)}, u32[]{:S(2)}, u32[]{:S(2)}) %collective-permute-start.11) | collective-permute-done | bytes 393248 | tf_op jit(solution)/shard_map/ppermute | solution.py:170
  107.4 8.5 %collective-permute-done.12.refs_2_ = bf16[256,768]{1,0:T(8,128)(2,1)S(1)} collective-permute-done((bf16[256,768]{1,0:T(8,128)(2,1)S(1)}, bf16[256,768]{1,0:T(8,128)(2,1)S(1)}, u32[]{:S(2)}, u32[]{:S(2)}) %collective-permute-start.12) | collective-permute-done | bytes 393248 | tf_op jit(solution)/shard_map/ppermute | solution.py:170
  116.1 13.9 %shard_map.159 = (bf16[256,768]{1,0:T(8,128)(2,1)S(1)}, bf16[256,768]{1,0:T(8,128)(2,1)}, bf16[256,768]{1,0:T(8,128)(2,1)}, bf16[256,768]{1,0:T(8,128)(2,1)}) custom-call(s32[4]{0:T(128)S(1)} %pad_add_fusion.place, bf16[256,768]{1,0:T(8,128)(2,1)S(1)} %get-tuple-element.107.refs_0_, bf16[256,768]{1,0:T(8,128)(2,1)S(1)} %collective-permute-done.11.refs_1_, ...), custom_call_target="tpu_custom_call" | custom-call | flops 17999998976 | bytes 5000000 | tf_op jit(solution)/shard_map/pallas_call | solution.py:42
  130.0 2.2 collective-permute-start.14
  132.2 2.5 collective-permute-start.15
  135.9 7.6 %shard_map.160 = (f32[768,512]{1,0:T(8,128)S(1)}, bf16[768,1024]{1,0:T(8,128)(2,1)}, f32[768,1024]{1,0:T(8,128)}) custom-call(s32[4]{0:T(128)S(1)} %pad_add_fusion.place, bf16[768,512]{1,0:T(8,128)(2,1)S(1)} %copy-done.23, bf16[16,256,256]{2,1,0:T(8,128)(2,1)} %bitcast.75, bf16[16,256,256]{2,1,0:T(8,128)(2,1)} %bitcast.76), custom_call_target="tpu_custom_call" | custom-call | flops 6000000000 | bytes 12000000 | tf_op jit(solution)/shard_map/pallas_call | solution.py:42
  144.6 9.0 %shard_map.162 = (f32[768,512]{1,0:T(8,128)S(1)}, bf16[16,256,256]{2,1,0:T(8,128)(2,1)S(1)}) custom-call(s32[4]{0:T(128)S(1)} %pad_add_fusion.place, bf16[768,512]{1,0:T(8,128)(2,1)S(1)} %bitcast.53, bf16[768,1024]{1,0:T(8,128)(2,1)} %get-tuple-element.120.active, f32[768,1024]{1,0:T(8,128)} %get-tuple-element.121.slope, bf16[768,512]{1,0:T(8,128)(2,1)S(1)} %copy-done.24, ...), custom_call_target="tpu_custom_call" | custom-call | flops 8000000000 | bytes 14000000 | tf_op jit(solution)/shard_map/pallas_call | solution.py:42
  153.7 4.7 %shard_map.163 = (f32[768,512]{1,0:T(8,128)}, bf16[3,256,768]{2,1,0:T(8,128)(2,1)S(1)}, f32[8,512]{1,0:T(8,128)S(1)}, bf16[256,768]{1,0:T(8,128)(2,1)S(1)}) custom-call(s32[4]{0:T(128)S(1)} %pad_add_fusion.place, bf16[256,768]{1,0:T(8,128)(2,1)S(1)} %get-tuple-element.111.refs_0_, bf16[256,768]{1,0:T(8,128)(2,1)S(1)} %collective-permute-done.14.refs_1_, ...), custom_call_target="tpu_custom_call" | custom-call | flops 1500000000 | bytes 6000000 | tf_op jit(solution)/shard_map/pallas_call | solution.py:42
  158.4 1.5 collective-permute-start.19
  159.9 1.3 collective-permute-done.19.refs_2_
  161.3 3.4 %shard_map.164 = bf16[16,400,256]{2,1,0:T(8,128)(2,1)} custom-call(s32[4]{0:T(128)S(1)} %pad_add_fusion.place, bf16[768,512]{1,0:T(8,128)(2,1)S(1)} %copy-done.21, bf16[3,256,768]{2,1,0:T(8,128)(2,1)S(1)} %get-tuple-element.125.mixed, f32[8,512]{1,0:T(8,128)S(1)} %get-tuple-element.126.sums, bf16[16,256,256]{2,1,0:T(8,128)(2,1)S(1)} %get-tuple-element.127.refs_0_, ...), custom_call_target="tpu_custom_call" | custom-call | flops 2000000000 | bytes 6000000 | tf_op jit(solution)/shard_map/pallas_call | solution.py:42
  165.3 3.1 %collective-permute-done.18.came = f32[768,512]{1,0:T(8,128)S(1)} collective-permute-done((f32[768,512]{1,0:T(8,128)}, f32[768,512]{1,0:T(8,128)S(1)}, u32[]{:S(2)}, u32[]{:S(2)}) %collective-permute-start.18) | collective-permute-done | bytes 1572896 | tf_op jit(solution)/shard_map/ppermute | solution.py:174
  169.5 1.4 copy-done.20
  170.9 1.7 shard_map.165.grad.refs_2_
  172.7 1.6 shard_map.166
  176.1 2.0 collective-permute-start.22
  178.1 9.3 %shard_map.167 = (f32[768,512]{1,0:T(8,128)S(1)}, bf16[16,288,256]{2,1,0:T(8,128)(2,1)S(1)}) custom-call(s32[4]{0:T(128)S(1)} %pad_add_fusion.place, bf16[768,512]{1,0:T(8,128)(2,1)S(1)} %shard_map.165.grad.refs_2_, bf16[768,1024]{1,0:T(8,128)(2,1)} %get-tuple-element.135.active, f32[768,1024]{1,0:T(8,128)} %get-tuple-element.136.slope, ...), custom_call_target="tpu_custom_call" | custom-call | flops 8000000000 | bytes 14000000 | tf_op jit(solution)/shard_map/pallas_call | solution.py:42
  187.4 1.5 copy-done.10
  190.0 6.2 %all-to-all-start.1 = ((bf16[16,288,256]{2,1,0:T(8,128)(2,1)}), bf16[16,288,256]{2,1,0:T(8,128)(2,1)}, u32[]{:S(2)}, u32[]{:S(2)}) async-start(bf16[16,288,256]{2,1,0:T(8,128)(2,1)} %copy-done.10), calls=%async_computation.1 | async-start | bytes 4718592 | tf_op jit(solution)/shard_map/all_to_all | solution.py:178
  196.3 10.7 %shard_map.168 = (bf16[192,768]{1,0:T(8,128)(2,1)S(1)}, bf16[192,768]{1,0:T(8,128)(2,1)S(1)}, bf16[192,768]{1,0:T(8,128)(2,1)S(1)}, bf16[192,768]{1,0:T(8,128)(2,1)S(1)}) custom-call(s32[4]{0:T(128)S(1)} %pad_add_fusion.place, bf16[64,768]{1,0:T(8,128)(2,1)S(1)} %get-tuple-element.139.refs_0_, bf16[64,768]{1,0:T(8,128)(2,1)S(1)} %collective-permute-done.20.refs_1_, ...), custom_call_target="tpu_custom_call" | custom-call | flops 16000000000 | bytes 5000000 | tf_op jit(solution)/shard_map/pallas_call | solution.py:42
  207.0 2.0 collective-permute-start.25
  210.2 3.6 %shard_map.161 = (f32[768,512]{1,0:T(8,128)}, bf16[256,768]{1,0:T(8,128)(2,1)}) custom-call(s32[4]{0:T(128)S(1)} %pad_add_fusion.place, bf16[256,768]{1,0:T(8,128)(2,1)S(1)} %copy-done.14, bf16[256,768]{1,0:T(8,128)(2,1)S(1)} %copy-done.16, bf16[256,768]{1,0:T(8,128)(2,1)} %collective-permute-done.15.refs_2_, ...), custom_call_target="tpu_custom_call" | custom-call | flops 800000000 | bytes 4000000 | tf_op jit(solution)/shard_map/pallas_call | solution.py:42
  213.8 2.4 collective-permute-start.17
  216.4 4.5 %collective-permute-done.25.refs_2_ = bf16[192,768]{1,0:T(8,128)(2,1)S(1)} collective-permute-done((bf16[192,768]{1,0:T(8,128)(2,1)S(1)}, bf16[192,768]{1,0:T(8,128)(2,1)S(1)}, u32[]{:S(2)}, u32[]{:S(2)}) %collective-permute-start.25) | collective-permute-done | bytes 294944 | tf_op jit(solution)/shard_map/ppermute | solution.py:170
  220.9 2.2 collective-permute-done.26.refs_3_
  223.1 3.6 %shard_map.169 = (f32[768,512]{1,0:T(8,128)}, bf16[3,256,768]{2,1,0:T(8,128)(2,1)S(1)}, f32[8,512]{1,0:T(8,128)S(1)}) custom-call(s32[4]{0:T(128)S(1)} %pad_add_fusion.place, bf16[192,768]{1,0:T(8,128)(2,1)S(1)} %get-tuple-element.146.refs_0_, bf16[192,768]{1,0:T(8,128)(2,1)S(1)} %collective-permute-done.24.refs_1_, ...), custom_call_target="tpu_custom_call" | custom-call | flops 1500000000 | bytes 6000000 | tf_op jit(solution)/shard_map/pallas_call | solution.py:42
  226.7 1.6 collective-permute-start.27
  228.2 2.3 shard_map.171
  230.9 6.3 %all-to-all-start.2 = ((bf16[16,112,256]{2,1,0:T(8,128)(2,1)}), bf16[16,112,256]{2,1,0:T(8,128)(2,1)}, u32[]{:S(2)}, u32[]{:S(2)}) async-start(bf16[16,112,256]{2,1,0:T(8,128)(2,1)} %shard_map.171), calls=%async_computation.2 | async-start | bytes 1835008 | tf_op jit(solution)/shard_map/all_to_all | solution.py:178
  237.2 2.1 reduce_sum.24.refs_4_
  239.8 3.0 %collective-permute-start.32 = (bf16[288,256]{1,0:T(8,128)(2,1)S(1)}, bf16[288,256]{1,0:T(8,128)(2,1)S(1)}, u32[]{:S(2)}, u32[]{:S(2)}) collective-permute-start(bf16[288,256]{1,0:T(8,128)(2,1)S(1)} %reduce_sum.24.refs_4_), channel_id=1, source_target_pairs={{0,32},{16,48},{32,0},{48,16},{1,33},{17,49},{33,1},{49,17},{2,34}... | collective-permute-start | bytes 442376 | tf_op jit(solution)/shard_map/ppermute | solution.py:170
  242.9 8.4 %all-to-all-done.2 = bf16[16,112,256]{2,1,0:T(8,128)(2,1)} async-done(((bf16[16,112,256]{2,1,0:T(8,128)(2,1)}), bf16[16,112,256]{2,1,0:T(8,128)(2,1)}, u32[]{:S(2)}, u32[]{:S(2)}) %all-to-all-start.2) | async-done | bytes 917536 | tf_op jit(solution)/shard_map/all_to_all | solution.py:178
  251.2 1.3 reduce_sum.25.refs_8_
  253.7 3.0 %collective-permute-start.35 = (bf16[112,256]{1,0:T(8,128)(2,1)S(1)}, bf16[112,256]{1,0:T(8,128)(2,1)S(1)}, u32[]{:S(2)}, u32[]{:S(2)}) collective-permute-start(bf16[112,256]{1,0:T(8,128)(2,1)S(1)} %reduce_sum.25.refs_8_), channel_id=1, source_target_pairs={{0,32},{16,48},{32,0},{48,16},{1,33},{17,49},{33,1},{49,17},{2,34}... | collective-permute-start | bytes 172040 | tf_op jit(solution)/shard_map/ppermute | solution.py:170
  257.4 3.0 %reduce-scatter.4.cloned.1.call-done = bf16[1,400,256]{2,1,0:T(8,128)(2,1)} async-done(((bf16[16,400,256]{2,1,0:T(8,128)(2,1)}), bf16[1,400,256]{2,1,0:T(8,128)(2,1)}) %reduce-scatter.4.cloned.1.call-update) | async-done | bytes 204816
  262.4 2.6 collective-permute-start.29
  266.0 3.2 %fusion = bf16[768,512]{1,0:T(8,128)(2,1)} fusion(bf16[768,512]{1,0:T(8,128)(2,1)S(1)} %copy-done.9, f32[768,512]{1,0:T(8,128)} %get-tuple-element.119, f32[768,512]{1,0:T(8,128)} %collective-permute-done.17, pred[]{:T(512)S(6)} %eq.5), kind=kLoop, calls=%fused_computation.1 | loop fusion | flops 1966080 | bytes 4718593 | tf_op jit(solution)/shard_map/jit(_where)/select_n | solution.py:895
  269.3 3.4 %shard_map.170 = bf16[768,512]{1,0:T(8,128)(2,1)S(1)} custom-call(s32[4]{0:T(128)S(1)} %pad_add_fusion.place, bf16[768,512]{1,0:T(8,128)(2,1)S(1)} %bitcast.59, bf16[768,512]{1,0:T(8,128)(2,1)S(1)} %shard_map.165.grad.refs_2_, f32[768,512]{1,0:T(8,128)S(1)} %copy-done.17, f32[768,512]{1,0:T(8,128)} %collective-permute-done.27.came), custom_call_target="tpu_custom_call" | custom-call | flops 100000000 | bytes 5000000 | tf_op jit(solution)/shard_map/pallas_call | solution.py:42
  273.6 3.3 %collective-permute-start.37 = (bf16[400,256]{1,0:T(8,128)(2,1)S(1)}, bf16[400,256]{1,0:T(8,128)(2,1)S(1)}, u32[]{:S(2)}, u32[]{:S(2)}) collective-permute-start(bf16[400,256]{1,0:T(8,128)(2,1)S(1)} %get-tuple-element.158), channel_id=1, source_target_pairs={{0,64},{64,0},{1,65},{65,1},{2,66},{66,2},{3,67},{67,3},{4,68},{68... | collective-permute-start | bytes 614408 | tf_op jit(solution)/shard_map/ppermute | solution.py:174
  277.9 1.5 shard_map.173
  (139 shorter events, 25.6 us)
Async XLA Ops:
  7.2 63.4 %all-gather.5.cloned.1.call-start = ((), (), s32[]{:S(2)}) async-start(), calls=%async_computation.4 | async-start | bytes 4177920 | tf_op jit(solution)/shard_map/all_gather | solution.py:855
  9.8 2.6 collective-permute-start
  14.1 7.1 %copy-start.22 = (s32[3,1,256]{2,1,0:T(1,128)S(1)}, s32[3,1,256]{2,1,0:T(1,128)}, u32[]{:S(2)}) copy-start(s32[3,1,256]{2,1,0:T(1,128)} %param.10) | copy-start | bytes 9220
  14.1 21.5 %copy-start.6 = (bf16[3,1,256,512]{3,2,1,0:T(8,128)(2,1)S(1)}, bf16[3,1,256,512]{3,2,1,0:T(8,128)(2,1)}, u32[]{:S(2)}) copy-start(bf16[3,1,256,512]{3,2,1,0:T(8,128)(2,1)} %param.9) | copy-start | bytes 2359300
  14.1 21.2 %all-to-all-start = ((bf16[16,112,256]{2,1,0:T(8,128)(2,1)}), bf16[16,112,256]{2,1,0:T(8,128)(2,1)S(1)}, u32[]{:S(2)}, u32[]{:S(2)}) async-start(bf16[16,112,256]{2,1,0:T(8,128)(2,1)} %get-tuple-element.88), calls=%async_computation | async-start | bytes 1835008 | tf_op jit(solution)/shard_map/all_to_all | solution.py:178
  21.1 113.6 %all-gather.7.cloned.1.call-start = ((), (), s32[]{:S(2)}) async-start(), calls=%async_computation.5 | async-start | bytes 2228224 | tf_op jit(solution)/shard_map/all_gather | solution.py:856
  21.2 6.0 %collective-permute-start.1 = (s32[1,768]{1,0:T(1,128)S(1)}, s32[1,768]{1,0:T(1,128)S(1)}, u32[]{:S(2)}, u32[]{:S(2)}) collective-permute-start(s32[1,768]{1,0:T(1,128)S(1)} %bitcast.60), channel_id=1, source_target_pairs={{0,16},{16,32},{32,48},{48,0},{1,17},{17,33},{33,49},{49,1},{2,18}... | collective-permute-start | bytes 9224 | tf_op jit(solution)/shard_map/ppermute | solution.py:170
  22.9 4.4 %collective-permute-start.2 = (s32[1,768]{1,0:T(1,128)S(1)}, s32[1,768]{1,0:T(1,128)S(1)}, u32[]{:S(2)}, u32[]{:S(2)}) collective-permute-start(s32[1,768]{1,0:T(1,128)S(1)} %bitcast.61), channel_id=1, source_target_pairs={{0,32},{16,48},{32,0},{48,16},{1,33},{17,49},{33,1},{49,17},{2,34}... | collective-permute-start | bytes 9224 | tf_op jit(solution)/shard_map/ppermute | solution.py:170
  26.2 2.7 collective-permute-start.3
  40.1 8.8 %collective-permute-start.4 = (bf16[192,768]{1,0:T(8,128)(2,1)}, bf16[192,768]{1,0:T(8,128)(2,1)S(1)}, u32[]{:S(2)}, u32[]{:S(2)}) collective-permute-start(bf16[192,768]{1,0:T(8,128)(2,1)} %get-tuple-element.91), channel_id=1, source_target_pairs={{0,16},{16,32},{32,48},{48,0},{1,17},{17,33},{33,49},{49,1},{2,18}... | collective-permute-start | bytes 884744 | tf_op jit(solution)/shard_map/ppermute | solution.py:170
  42.1 12.1 %collective-permute-start.5 = (bf16[192,768]{1,0:T(8,128)(2,1)S(1)}, bf16[192,768]{1,0:T(8,128)(2,1)S(1)}, u32[]{:S(2)}, u32[]{:S(2)}) collective-permute-start(bf16[192,768]{1,0:T(8,128)(2,1)S(1)} %get-tuple-element.92), channel_id=1, source_target_pairs={{0,32},{16,48},{32,0},{48,16},{1,33},{17,49},{33,1},{49,17},{2,34}... | collective-permute-start | bytes 884744 | tf_op jit(solution)/shard_map/ppermute | solution.py:170
  45.8 8.4 %collective-permute-start.6 = (bf16[192,768]{1,0:T(8,128)(2,1)S(1)}, bf16[192,768]{1,0:T(8,128)(2,1)S(1)}, u32[]{:S(2)}, u32[]{:S(2)}) collective-permute-start(bf16[192,768]{1,0:T(8,128)(2,1)S(1)} %get-tuple-element.93), channel_id=1, source_target_pairs={{0,48},{16,0},{32,16},{48,32},{1,49},{17,1},{33,17},{49,33},{2,50}... | collective-permute-start | bytes 884744 | tf_op jit(solution)/shard_map/ppermute | solution.py:170
  46.2 214.3 %reduce-scatter.4.cloned.1.call-start = ((), (), s32[]{:S(2)}) async-start(), calls=%async_computation.6 | async-start | bytes 3481600
  62.3 17.3 %collective-permute-start.7 = (bf16[64,768]{1,0:T(8,128)(2,1)S(1)}, bf16[64,768]{1,0:T(8,128)(2,1)S(1)}, u32[]{:S(2)}, u32[]{:S(2)}) collective-permute-start(bf16[64,768]{1,0:T(8,128)(2,1)S(1)} %get-tuple-element.99), channel_id=1, source_target_pairs={{0,16},{16,32},{32,48},{48,0},{1,17},{17,33},{33,49},{49,1},{2,18}... | collective-permute-start | bytes 294920 | tf_op jit(solution)/shard_map/ppermute | solution.py:170
  66.2 13.4 %collective-permute-start.8 = (bf16[64,768]{1,0:T(8,128)(2,1)S(1)}, bf16[64,768]{1,0:T(8,128)(2,1)S(1)}, u32[]{:S(2)}, u32[]{:S(2)}) collective-permute-start(bf16[64,768]{1,0:T(8,128)(2,1)S(1)} %get-tuple-element.100), channel_id=1, source_target_pairs={{0,32},{16,48},{32,0},{48,16},{1,33},{17,49},{33,1},{49,17},{2,34}... | collective-permute-start | bytes 294920 | tf_op jit(solution)/shard_map/ppermute | solution.py:170
  66.2 13.4 %collective-permute-start.9 = (bf16[64,768]{1,0:T(8,128)(2,1)S(1)}, bf16[64,768]{1,0:T(8,128)(2,1)S(1)}, u32[]{:S(2)}, u32[]{:S(2)}) collective-permute-start(bf16[64,768]{1,0:T(8,128)(2,1)S(1)} %get-tuple-element.101), channel_id=1, source_target_pairs={{0,48},{16,0},{32,16},{48,32},{1,49},{17,1},{33,17},{49,33},{2,50}... | collective-permute-start | bytes 294920 | tf_op jit(solution)/shard_map/ppermute | solution.py:170
  71.8 7.9 %copy-start = (bf16[7680,256]{1,0:T(8,128)(2,1)S(1)}, bf16[7680,256]{1,0:T(8,128)(2,1)}, u32[]{:S(2)}) copy-start(bf16[7680,256]{1,0:T(8,128)(2,1)} %all-gather.5.cloned.1.call-done) | copy-start | bytes 11796484
  79.6 8.3 %copy-start.5 = (bf16[3,1,256,512]{3,2,1,0:T(8,128)(2,1)S(1)}, bf16[3,1,256,512]{3,2,1,0:T(8,128)(2,1)}, u32[]{:S(2)}) copy-start(bf16[3,1,256,512]{3,2,1,0:T(8,128)(2,1)} %param.11) | copy-start | bytes 2359300
  82.5 5.4 %collective-permute-start.10 = (f32[768,512]{1,0:T(8,128)}, f32[768,512]{1,0:T(8,128)}, u32[]{:S(2)}, u32[]{:S(2)}) collective-permute-start(f32[768,512]{1,0:T(8,128)} %get-tuple-element.105.refs_1_), channel_id=1, source_target_pairs={{0,64},{64,0},{1,65},{65,1},{2,66},{66,2},{3,67},{67,3},{4,68},{68... | collective-permute-start | bytes 4718600 | tf_op jit(solution)/shard_map/ppermute | solution.py:174
  95.8 11.6 %collective-permute-start.11 = (bf16[256,768]{1,0:T(8,128)(2,1)S(1)}, bf16[256,768]{1,0:T(8,128)(2,1)S(1)}, u32[]{:S(2)}, u32[]{:S(2)}) collective-permute-start(bf16[256,768]{1,0:T(8,128)(2,1)S(1)} %get-tuple-element.108), channel_id=1, source_target_pairs={{0,16},{16,32},{32,48},{48,0},{1,17},{17,33},{33,49},{49,1},{2,18}... | collective-permute-start | bytes 1179656 | tf_op jit(solution)/shard_map/ppermute | solution.py:170
  96.6 19.2 %collective-permute-start.12 = (bf16[256,768]{1,0:T(8,128)(2,1)S(1)}, bf16[256,768]{1,0:T(8,128)(2,1)S(1)}, u32[]{:S(2)}, u32[]{:S(2)}) collective-permute-start(bf16[256,768]{1,0:T(8,128)(2,1)S(1)} %get-tuple-element.109), channel_id=1, source_target_pairs={{0,32},{16,48},{32,0},{48,16},{1,33},{17,49},{33,1},{49,17},{2,34}... | collective-permute-start | bytes 1179656 | tf_op jit(solution)/shard_map/ppermute | solution.py:170
  98.5 17.6 %collective-permute-start.13 = (bf16[256,768]{1,0:T(8,128)(2,1)S(1)}, bf16[256,768]{1,0:T(8,128)(2,1)S(1)}, u32[]{:S(2)}, u32[]{:S(2)}) collective-permute-start(bf16[256,768]{1,0:T(8,128)(2,1)S(1)} %get-tuple-element.110), channel_id=1, source_target_pairs={{0,48},{16,0},{32,16},{48,32},{1,49},{17,1},{33,17},{49,33},{2,50}... | collective-permute-start | bytes 1179656 | tf_op jit(solution)/shard_map/ppermute | solution.py:170
  130.0 23.6 %copy-start.13 = (bf16[256,768]{1,0:T(8,128)(2,1)}, bf16[256,768]{1,0:T(8,128)(2,1)S(1)}, u32[]{:S(2)}) copy-start(bf16[256,768]{1,0:T(8,128)(2,1)S(1)} %get-tuple-element.111.refs_0_) | copy-start | bytes 1179652
  130.0 23.6 %collective-permute-start.14 = (bf16[256,768]{1,0:T(8,128)(2,1)}, bf16[256,768]{1,0:T(8,128)(2,1)S(1)}, u32[]{:S(2)}, u32[]{:S(2)}) collective-permute-start(bf16[256,768]{1,0:T(8,128)(2,1)} %get-tuple-element.112), channel_id=1, source_target_pairs={{0,16},{16,32},{32,48},{48,0},{1,17},{17,33},{33,49},{49,1},{2,18}... | collective-permute-start | bytes 1179656 | tf_op jit(solution)/shard_map/ppermute | solution.py:170
  132.2 21.4 %collective-permute-start.15 = (bf16[256,768]{1,0:T(8,128)(2,1)}, bf16[256,768]{1,0:T(8,128)(2,1)}, u32[]{:S(2)}, u32[]{:S(2)}) collective-permute-start(bf16[256,768]{1,0:T(8,128)(2,1)} %get-tuple-element.113), channel_id=1, source_target_pairs={{0,32},{16,48},{32,0},{48,16},{1,33},{17,49},{33,1},{49,17},{2,34}... | collective-permute-start | bytes 1179656 | tf_op jit(solution)/shard_map/ppermute | solution.py:170
  134.7 19.0 %collective-permute-start.16 = (bf16[256,768]{1,0:T(8,128)(2,1)}, bf16[256,768]{1,0:T(8,128)(2,1)}, u32[]{:S(2)}, u32[]{:S(2)}) collective-permute-start(bf16[256,768]{1,0:T(8,128)(2,1)} %get-tuple-element.114), channel_id=1, source_target_pairs={{0,48},{16,0},{32,16},{48,32},{1,49},{17,1},{33,17},{49,33},{2,50}... | collective-permute-start | bytes 1179656 | tf_op jit(solution)/shard_map/ppermute | solution.py:170
  135.9 8.8 %copy-start.24 = (bf16[768,512]{1,0:T(8,128)(2,1)S(1)}, bf16[768,512]{1,0:T(8,128)(2,1)}, u32[]{:S(2)}) copy-start(bf16[768,512]{1,0:T(8,128)(2,1)} %get-tuple-element.116.mlp_in) | copy-start | bytes 2359300
  144.6 9.1 %copy-start.2 = (bf16[7680,256]{1,0:T(8,128)(2,1)S(1)}, bf16[7680,256]{1,0:T(8,128)(2,1)}, u32[]{:S(2)}) copy-start(bf16[7680,256]{1,0:T(8,128)(2,1)} %all-gather.5.cloned.1.call-done) | copy-start | bytes 11796484
  144.6 9.1 %copy-start.7 = (bf16[768,512]{1,0:T(8,128)(2,1)S(1)}, bf16[768,512]{1,0:T(8,128)(2,1)}, u32[]{:S(2)}) copy-start(bf16[768,512]{1,0:T(8,128)(2,1)} %get-tuple-element.106.refs_9_.states) | copy-start | bytes 2359300
  153.7 4.8 %copy-start.15 = (bf16[256,768]{1,0:T(8,128)(2,1)}, bf16[256,768]{1,0:T(8,128)(2,1)S(1)}, u32[]{:S(2)}) copy-start(bf16[256,768]{1,0:T(8,128)(2,1)S(1)} %collective-permute-done.14.refs_1_) | copy-start | bytes 1179652
  153.7 7.5 %copy-start.21 = (bf16[768,512]{1,0:T(8,128)(2,1)S(1)}, bf16[768,512]{1,0:T(8,128)(2,1)}, u32[]{:S(2)}) copy-start(bf16[768,512]{1,0:T(8,128)(2,1)} %get-tuple-element.124.attn_in) | copy-start | bytes 2359300
  158.4 2.8 collective-permute-start.19
  164.7 3.7 %collective-permute-start.18 = (f32[768,512]{1,0:T(8,128)}, f32[768,512]{1,0:T(8,128)S(1)}, u32[]{:S(2)}, u32[]{:S(2)}) collective-permute-start(f32[768,512]{1,0:T(8,128)} %get-tuple-element.123.own), channel_id=1, source_target_pairs={{0,64},{64,0},{1,65},{65,1},{2,66},{66,2},{3,67},{67,3},{4,68},{68... | collective-permute-start | bytes 4718600 | tf_op jit(solution)/shard_map/ppermute | solution.py:174
  165.2 7.5 %copy-start.3 = (bf16[7680,256]{1,0:T(8,128)(2,1)S(1)}, bf16[7680,256]{1,0:T(8,128)(2,1)}, u32[]{:S(2)}) copy-start(bf16[7680,256]{1,0:T(8,128)(2,1)} %all-gather.5.cloned.1.call-done) | copy-start | bytes 11796484
  165.2 12.9 %collective-permute-start.23 = (bf16[256,768]{1,0:T(8,128)(2,1)}, bf16[256,768]{1,0:T(8,128)(2,1)S(1)}, u32[]{:S(2)}, u32[]{:S(2)}) collective-permute-start(bf16[256,768]{1,0:T(8,128)(2,1)} %get-tuple-element.137.refs_0_), channel_id=1, source_target_pairs={{0,64},{64,0},{1,65},{65,1},{2,66},{66,2},{3,67},{67,3},{4,68},{68... | collective-permute-start | bytes 1179656 | tf_op jit(solution)/shard_map/ppermute | solution.py:174
  172.7 5.4 %copy-start.32 = (bf16[768,512]{1,0:T(8,128)(2,1)S(1)}, bf16[768,512]{1,0:T(8,128)(2,1)}, u32[]{:S(2)}) copy-start(bf16[768,512]{1,0:T(8,128)(2,1)} %get-tuple-element.103.mlp_in) | copy-start | bytes 2359300
  174.3 21.9 %collective-permute-start.20 = (bf16[64,768]{1,0:T(8,128)(2,1)S(1)}, bf16[64,768]{1,0:T(8,128)(2,1)S(1)}, u32[]{:S(2)}, u32[]{:S(2)}) collective-permute-start(bf16[64,768]{1,0:T(8,128)(2,1)S(1)} %get-tuple-element.131), channel_id=1, source_target_pairs={{0,16},{16,32},{32,48},{48,0},{1,17},{17,33},{33,49},{49,1},{2,18}... | collective-permute-start | bytes 294920 | tf_op jit(solution)/shard_map/ppermute | solution.py:170
  175.6 20.6 %collective-permute-start.21 = (bf16[64,768]{1,0:T(8,128)(2,1)S(1)}, bf16[64,768]{1,0:T(8,128)(2,1)S(1)}, u32[]{:S(2)}, u32[]{:S(2)}) collective-permute-start(bf16[64,768]{1,0:T(8,128)(2,1)S(1)} %get-tuple-element.132), channel_id=1, source_target_pairs={{0,32},{16,48},{32,0},{48,16},{1,33},{17,49},{33,1},{49,17},{2,34}... | collective-permute-start | bytes 294920 | tf_op jit(solution)/shard_map/ppermute | solution.py:170
  176.1 20.1 %collective-permute-start.22 = (bf16[64,768]{1,0:T(8,128)(2,1)S(1)}, bf16[64,768]{1,0:T(8,128)(2,1)S(1)}, u32[]{:S(2)}, u32[]{:S(2)}) collective-permute-start(bf16[64,768]{1,0:T(8,128)(2,1)S(1)} %get-tuple-element.133), channel_id=1, source_target_pairs={{0,48},{16,0},{32,16},{48,32},{1,49},{17,1},{33,17},{49,33},{2,50}... | collective-permute-start | bytes 294920 | tf_op jit(solution)/shard_map/ppermute | solution.py:170
  190.0 40.8 %all-to-all-start.1 = ((bf16[16,288,256]{2,1,0:T(8,128)(2,1)}), bf16[16,288,256]{2,1,0:T(8,128)(2,1)}, u32[]{:S(2)}, u32[]{:S(2)}) async-start(bf16[16,288,256]{2,1,0:T(8,128)(2,1)} %copy-done.10), calls=%async_computation.1 | async-start | bytes 4718592 | tf_op jit(solution)/shard_map/all_to_all | solution.py:178
  196.3 14.0 %copy-start.4 = (bf16[7680,256]{1,0:T(8,128)(2,1)S(1)}, bf16[7680,256]{1,0:T(8,128)(2,1)}, u32[]{:S(2)}) copy-start(bf16[7680,256]{1,0:T(8,128)(2,1)} %all-gather.5.cloned.1.call-done) | copy-start | bytes 11796484
  196.3 14.0 %copy-start.12 = (f32[768,512]{1,0:T(8,128)S(1)}, f32[768,512]{1,0:T(8,128)}, u32[]{:S(2)}) copy-start(f32[768,512]{1,0:T(8,128)} %copy-done.11) | copy-start | bytes 4718596
  196.3 13.9 %copy-start.14 = (bf16[256,768]{1,0:T(8,128)(2,1)S(1)}, bf16[256,768]{1,0:T(8,128)(2,1)}, u32[]{:S(2)}) copy-start(bf16[256,768]{1,0:T(8,128)(2,1)} %copy-done.13) | copy-start | bytes 1179652
  196.3 13.9 %copy-start.16 = (bf16[256,768]{1,0:T(8,128)(2,1)S(1)}, bf16[256,768]{1,0:T(8,128)(2,1)}, u32[]{:S(2)}) copy-start(bf16[256,768]{1,0:T(8,128)(2,1)} %copy-done.15) | copy-start | bytes 1179652
  207.0 9.4 %collective-permute-start.24 = (bf16[192,768]{1,0:T(8,128)(2,1)S(1)}, bf16[192,768]{1,0:T(8,128)(2,1)S(1)}, u32[]{:S(2)}, u32[]{:S(2)}) collective-permute-start(bf16[192,768]{1,0:T(8,128)(2,1)S(1)} %get-tuple-element.147), channel_id=1, source_target_pairs={{0,16},{16,32},{32,48},{48,0},{1,17},{17,33},{33,49},{49,1},{2,18}... | collective-permute-start | bytes 884744 | tf_op jit(solution)/shard_map/ppermute | solution.py:170
  207.0 13.8 %collective-permute-start.25 = (bf16[192,768]{1,0:T(8,128)(2,1)S(1)}, bf16[192,768]{1,0:T(8,128)(2,1)S(1)}, u32[]{:S(2)}, u32[]{:S(2)}) collective-permute-start(bf16[192,768]{1,0:T(8,128)(2,1)S(1)} %get-tuple-element.148), channel_id=1, source_target_pairs={{0,32},{16,48},{32,0},{48,16},{1,33},{17,49},{33,1},{49,17},{2,34}... | collective-permute-start | bytes 884744 | tf_op jit(solution)/shard_map/ppermute | solution.py:170
  209.0 14.0 %collective-permute-start.26 = (bf16[192,768]{1,0:T(8,128)(2,1)S(1)}, bf16[192,768]{1,0:T(8,128)(2,1)S(1)}, u32[]{:S(2)}, u32[]{:S(2)}) collective-permute-start(bf16[192,768]{1,0:T(8,128)(2,1)S(1)} %get-tuple-element.149), channel_id=1, source_target_pairs={{0,48},{16,0},{32,16},{48,32},{1,49},{17,1},{33,17},{49,33},{2,50}... | collective-permute-start | bytes 884744 | tf_op jit(solution)/shard_map/ppermute | solution.py:170
  210.2 12.8 %copy-start.19 = (f32[768,512]{1,0:T(8,128)S(1)}, f32[768,512]{1,0:T(8,128)}, u32[]{:S(2)}) copy-start(f32[768,512]{1,0:T(8,128)} %copy-done.18) | copy-start | bytes 4718596
  213.8 38.7 %collective-permute-start.17 = (f32[768,512]{1,0:T(8,128)}, f32[768,512]{1,0:T(8,128)}, u32[]{:S(2)}, u32[]{:S(2)}) collective-permute-start(f32[768,512]{1,0:T(8,128)} %get-tuple-element.119), channel_id=1, source_target_pairs={{0,64},{64,0},{1,65},{65,1},{2,66},{66,2},{3,67},{67,3},{4,68},{68... | collective-permute-start | bytes 4718600 | tf_op jit(solution)/shard_map/ppermute | solution.py:174
  223.1 5.2 %copy-start.30 = (bf16[768,512]{1,0:T(8,128)(2,1)S(1)}, bf16[768,512]{1,0:T(8,128)(2,1)}, u32[]{:S(2)}) copy-start(bf16[768,512]{1,0:T(8,128)(2,1)} %get-tuple-element.152.attn_in) | copy-start | bytes 2359300
  226.7 27.0 %collective-permute-start.27 = (f32[768,512]{1,0:T(8,128)}, f32[768,512]{1,0:T(8,128)}, u32[]{:S(2)}, u32[]{:S(2)}) collective-permute-start(f32[768,512]{1,0:T(8,128)} %get-tuple-element.151.own), channel_id=1, source_target_pairs={{0,64},{64,0},{1,65},{65,1},{2,66},{66,2},{3,67},{67,3},{4,68},{68... | collective-permute-start | bytes 4718600 | tf_op jit(solution)/shard_map/ppermute | solution.py:174
  230.9 20.4 %all-to-all-start.2 = ((bf16[16,112,256]{2,1,0:T(8,128)(2,1)}), bf16[16,112,256]{2,1,0:T(8,128)(2,1)}, u32[]{:S(2)}, u32[]{:S(2)}) async-start(bf16[16,112,256]{2,1,0:T(8,128)(2,1)} %shard_map.171), calls=%async_computation.2 | async-start | bytes 1835008 | tf_op jit(solution)/shard_map/all_to_all | solution.py:178
  237.2 28.9 %copy-start.9 = (bf16[768,512]{1,0:T(8,128)(2,1)S(1)}, bf16[768,512]{1,0:T(8,128)(2,1)}, u32[]{:S(2)}) copy-start(bf16[768,512]{1,0:T(8,128)(2,1)} %get-tuple-element.106.refs_9_.states) | copy-start | bytes 2359300
  239.3 17.5 %collective-permute-start.31 = (bf16[288,256]{1,0:T(8,128)(2,1)S(1)}, bf16[288,256]{1,0:T(8,128)(2,1)S(1)}, u32[]{:S(2)}, u32[]{:S(2)}) collective-permute-start(bf16[288,256]{1,0:T(8,128)(2,1)S(1)} %reduce_sum.24.refs_4_), channel_id=1, source_target_pairs={{0,16},{16,32},{32,48},{48,0},{1,17},{17,33},{33,49},{49,1},{2,18}... | collective-permute-start | bytes 442376 | tf_op jit(solution)/shard_map/ppermute | solution.py:170
  239.8 16.9 %collective-permute-start.32 = (bf16[288,256]{1,0:T(8,128)(2,1)S(1)}, bf16[288,256]{1,0:T(8,128)(2,1)S(1)}, u32[]{:S(2)}, u32[]{:S(2)}) collective-permute-start(bf16[288,256]{1,0:T(8,128)(2,1)S(1)} %reduce_sum.24.refs_4_), channel_id=1, source_target_pairs={{0,32},{16,48},{32,0},{48,16},{1,33},{17,49},{33,1},{49,17},{2,34}... | collective-permute-start | bytes 442376 | tf_op jit(solution)/shard_map/ppermute | solution.py:170
  242.9 18.9 %collective-permute-start.33 = (bf16[288,256]{1,0:T(8,128)(2,1)S(1)}, bf16[288,256]{1,0:T(8,128)(2,1)S(1)}, u32[]{:S(2)}, u32[]{:S(2)}) collective-permute-start(bf16[288,256]{1,0:T(8,128)(2,1)S(1)} %reduce_sum.24.refs_4_), channel_id=1, source_target_pairs={{0,48},{16,0},{32,16},{48,32},{1,49},{17,1},{33,17},{49,33},{2,50}... | collective-permute-start | bytes 442376 | tf_op jit(solution)/shard_map/ppermute | solution.py:170
  252.5 12.5 %collective-permute-start.34 = (bf16[112,256]{1,0:T(8,128)(2,1)S(1)}, bf16[112,256]{1,0:T(8,128)(2,1)S(1)}, u32[]{:S(2)}, u32[]{:S(2)}) collective-permute-start(bf16[112,256]{1,0:T(8,128)(2,1)S(1)} %reduce_sum.25.refs_8_), channel_id=1, source_target_pairs={{0,16},{16,32},{32,48},{48,0},{1,17},{17,33},{33,49},{49,1},{2,18}... | collective-permute-start | bytes 172040 | tf_op jit(solution)/shard_map/ppermute | solution.py:170
  253.7 19.0 %collective-permute-start.35 = (bf16[112,256]{1,0:T(8,128)(2,1)S(1)}, bf16[112,256]{1,0:T(8,128)(2,1)S(1)}, u32[]{:S(2)}, u32[]{:S(2)}) collective-permute-start(bf16[112,256]{1,0:T(8,128)(2,1)S(1)} %reduce_sum.25.refs_8_), channel_id=1, source_target_pairs={{0,32},{16,48},{32,0},{48,16},{1,33},{17,49},{33,1},{49,17},{2,34}... | collective-permute-start | bytes 172040 | tf_op jit(solution)/shard_map/ppermute | solution.py:170
  256.7 16.0 %collective-permute-start.36 = (bf16[112,256]{1,0:T(8,128)(2,1)S(1)}, bf16[112,256]{1,0:T(8,128)(2,1)S(1)}, u32[]{:S(2)}, u32[]{:S(2)}) collective-permute-start(bf16[112,256]{1,0:T(8,128)(2,1)S(1)} %reduce_sum.25.refs_8_), channel_id=1, source_target_pairs={{0,48},{16,0},{32,16},{48,32},{1,49},{17,1},{33,17},{49,33},{2,50}... | collective-permute-start | bytes 172040 | tf_op jit(solution)/shard_map/ppermute | solution.py:170
  260.4 8.8 %copy-start.17 = (f32[768,512]{1,0:T(8,128)S(1)}, f32[768,512]{1,0:T(8,128)}, u32[]{:S(2)}) copy-start(f32[768,512]{1,0:T(8,128)} %get-tuple-element.151.own) | copy-start | bytes 4718596
  260.4 12.3 %collective-permute-start.28 = (bf16[400,256]{1,0:T(8,128)(2,1)}, bf16[400,256]{1,0:T(8,128)(2,1)S(1)}, u32[]{:S(2)}, u32[]{:S(2)}) collective-permute-start(bf16[400,256]{1,0:T(8,128)(2,1)} %bitcast.66), channel_id=1, source_target_pairs={{0,16},{16,32},{32,48},{48,0},{1,17},{17,33},{33,49},{49,1},{2,18}... | collective-permute-start | bytes 614408 | tf_op jit(solution)/shard_map/ppermute | solution.py:170
  262.4 10.3 %collective-permute-start.29 = (bf16[400,256]{1,0:T(8,128)(2,1)}, bf16[400,256]{1,0:T(8,128)(2,1)S(1)}, u32[]{:S(2)}, u32[]{:S(2)}) collective-permute-start(bf16[400,256]{1,0:T(8,128)(2,1)} %bitcast.67), channel_id=1, source_target_pairs={{0,32},{16,48},{32,0},{48,16},{1,33},{17,49},{33,1},{49,17},{2,34}... | collective-permute-start | bytes 614408 | tf_op jit(solution)/shard_map/ppermute | solution.py:170
  265.0 7.7 %collective-permute-start.30 = (bf16[400,256]{1,0:T(8,128)(2,1)}, bf16[400,256]{1,0:T(8,128)(2,1)S(1)}, u32[]{:S(2)}, u32[]{:S(2)}) collective-permute-start(bf16[400,256]{1,0:T(8,128)(2,1)} %bitcast.68), channel_id=1, source_target_pairs={{0,48},{16,0},{32,16},{48,32},{1,49},{17,1},{33,17},{49,33},{2,50}... | collective-permute-start | bytes 614408 | tf_op jit(solution)/shard_map/ppermute | solution.py:170
  273.6 4.4 %collective-permute-start.37 = (bf16[400,256]{1,0:T(8,128)(2,1)S(1)}, bf16[400,256]{1,0:T(8,128)(2,1)S(1)}, u32[]{:S(2)}, u32[]{:S(2)}) collective-permute-start(bf16[400,256]{1,0:T(8,128)(2,1)S(1)} %get-tuple-element.158), channel_id=1, source_target_pairs={{0,64},{64,0},{1,65},{65,1},{2,66},{66,2},{3,67},{67,3},{4,68},{68... | collective-permute-start | bytes 614408 | tf_op jit(solution)/shard_map/ppermute | solution.py:174
  (15 other events, 24.2 us)
Sparse Core Ops, SparseCore 0:
  14.2 56.3 all-gather.4
  73.3 43.6 all-gather.6
  164.8 95.5 reduce-scatter.3
